TPU v7x, 32 devices: a whole 2x2x4 slice. The times are simulated.
32 devices in a mesh: grp: 4 (over y, x), tile: 8 (over z, core).
Axes of the slice: x: 2, y: 2, z: 4, core: 2. Of those that a mesh axis runs over, the one named last changes fastest.
Arguments:
- latent: bfloat16 [8, 16, 16, 512], P(None, 'grp', 'tile'), may hold values from -36 to 36
- coarse_filters: bfloat16 [3, 3, 3, 512, 512], P(None, None, None, None, 'grp'), may hold values from -0.0546875 to 0.0546875
- mid_filters: bfloat16 [3, 3, 3, 256, 256], P(None, None, None, None, 'tile'), may hold values from -0.078125 to 0.078125
- fine_filters: bfloat16 [3, 3, 3, 128, 128], replicated, may hold values from -0.109375 to 0.109375
- coarse_proj: bfloat16 [512, 256], replicated, may hold values from -0.25 to 0.25
- mid_proj: bfloat16 [256, 128], replicated, may hold values from -0.375 to 0.375
Outputs:
- frames_out: bfloat16 [8, 64, 64, 128], P(None, 'grp', 'tile')
All inputs are finite; a program needn't handle non-finite values.
Results may differ from a plain program's by a relative error of at most 0.018.
Values may be sent and summed in bfloat16 or wider, within the bound.
No kernel may reach another device: no remote copies, remote signals or barrier semaphores. Data moves between devices by JAX's collectives and lax.ppermute only.
A program may use at most 128 MiB of HBM per device.

v0:
```python
import jax
import jax.numpy as jnp
from jax import lax
from jax.sharding import PartitionSpec as P


def with_halo(shard, sides, width):
    for axis, dim in sides:
        size, length = (lax.axis_size(axis), shard.shape[dim])
        up = [(i, (i + 1) % size) for i in range(size - 1)]
        down = [(j, i) for i, j in up]
        last = lax.slice_in_dim(shard, length - width, length, axis=dim)
        initial = lax.slice_in_dim(shard, 0, width, axis=dim)
        before = lax.ppermute(last, axis, up)
        after = lax.ppermute(initial, axis, down)
        shard = jnp.concatenate([before, shard, after], axis=dim)
    return shard


def activate(values):
    widened = values.astype(jnp.float32)
    scaled = widened * lax.rsqrt(jnp.mean(widened * widened, axis=-1, keepdims=True) + 1e-06)
    return jax.nn.silu(scaled).astype(jnp.bfloat16)


def double_size(values):
    return jnp.repeat(jnp.repeat(values, 2, axis=1), 2, axis=2)


def time_padded(values):
    return jnp.pad(values, ((2, 0), (0, 0), (0, 0), (0, 0)))


def stencil_columns(extended):
    padded = time_padded(extended)
    height = extended.shape[1] - 2
    breadth = extended.shape[2] - 2
    return jnp.concatenate(
        [
            padded[:, row_step : row_step + height, col_step : col_step + breadth, :]
            for row_step in range(3)
            for col_step in range(3)
        ],
        axis=-1,
    )


def apply_columns(columns, filters):
    frames = columns.shape[0] - 2
    folded = filters.reshape(3, 9 * filters.shape[3], filters.shape[4])
    total = jnp.dot(columns[0:frames], folded[0], preferred_element_type=jnp.float32)
    for frame_step in (1, 2):
        total = total + jnp.dot(
            columns[frame_step : frame_step + frames],
            folded[frame_step],
            preferred_element_type=jnp.float32,
        )
    return total


def coarse_conv(extended, filters):
    padded = time_padded(extended)
    frames = extended.shape[0]
    height = extended.shape[1] - 2
    breadth = extended.shape[2] - 2
    inputs = filters.shape[3]
    outputs = filters.shape[4]
    total = jnp.zeros((frames, height, breadth, outputs), jnp.float32)
    for frame_step in range(3):
        spread = jnp.transpose(filters[frame_step], (2, 0, 1, 3)).reshape(inputs, 9 * outputs)
        products = jnp.dot(
            padded[frame_step : frame_step + frames], spread, preferred_element_type=jnp.float32
        )
        for row_step in range(3):
            for col_step in range(3):
                lane = 3 * row_step + col_step
                total = (
                    total
                    + products[
                        :,
                        row_step : row_step + height,
                        col_step : col_step + breadth,
                        lane * outputs : (lane + 1) * outputs,
                    ]
                )
    return total


def middle_conv(extended, mid_filters):
    columns = stencil_columns(extended)
    return apply_columns(columns, lax.all_gather(mid_filters, "tile", axis=4, tiled=True))


def body(latent, coarse_filters, mid_filters, fine_filters, coarse_proj, mid_proj):
    first_act = activate(latent)
    whole = lax.all_gather(first_act, "grp", axis=1, tiled=True)
    widened = with_halo(whole, (("tile", 2),), 1)
    padded = jnp.pad(widened, ((0, 0), (1, 1), (0, 0), (0, 0)))
    filtered = coarse_conv(padded, coarse_filters).astype(jnp.bfloat16)
    returned = lax.all_to_all(filtered, "grp", split_axis=1, concat_axis=3, tiled=True)
    level_zero = (latent.astype(jnp.float32) + returned.astype(jnp.float32)).astype(jnp.bfloat16)
    reduced = jnp.dot(level_zero, coarse_proj, preferred_element_type=jnp.float32).astype(
        jnp.bfloat16
    )
    mid_act = double_size(activate(reduced))
    mid_ext = with_halo(mid_act, (("grp", 1), ("tile", 2)), 1)
    mid_terms = middle_conv(mid_ext, mid_filters)
    mid_out = (double_size(reduced).astype(jnp.float32) + mid_terms).astype(jnp.bfloat16)
    fine_low = jnp.dot(mid_out, mid_proj, preferred_element_type=jnp.float32).astype(jnp.bfloat16)
    fine_in = double_size(fine_low)
    fine_act = double_size(activate(fine_low))
    fine_ext = with_halo(fine_act, (("grp", 1), ("tile", 2)), 1)
    fine_terms = apply_columns(stencil_columns(fine_ext), fine_filters)
    return (fine_in.astype(jnp.float32) + fine_terms).astype(jnp.bfloat16)


def solution(mesh):
    in_specs = (
        P(None, "grp", "tile", None),
        P(None, None, None, None, "grp"),
        P(None, None, None, None, "tile"),
        P(),
        P(),
        P(),
    )
    out_specs = P(None, "grp", "tile", None)
    return jax.shard_map(body, mesh=mesh, in_specs=in_specs, out_specs=out_specs, check_vma=False)
```

profile of v0, /device:TPU:1, one launch (start us, length us, event | category | flops | bytes accessed | tf_op | source)
XLA Modules:
  0.0 115.4 jit_solution(12043338412759679403)
XLA Ops:
  9.2 7.8 %all_gather.6 = bf16[8,16,2,512]{3,0,2,1:T(8,128)(2,1)S(1)} all-gather(bf16[8,4,2,512]{3,0,2,1:T(8,128)(2,1)S(1)} %fusion.32), channel_id=1, replica_groups=mesh['grp'=4,'tile'=8] {'grp'}, dimensions={1}, use_global_device_ids=true | all-gather | bytes 327680 | tf_op jit(solution)/shard_map/all_gather | solution.py:96
  17.2 5.8 %collective-permute-start = (bf16[8,16,1,512]{3,1,2,0:T(8,128)(2,1)S(1)}, bf16[8,16,1,512]{3,1,2,0:T(8,128)(2,1)S(1)}, u32[]{:S(2)}, u32[]{:S(2)}) collective-permute-start(bf16[8,16,1,512]{3,1,2,0:T(8,128)(2,1)S(1)} %get-tuple-element.18), channel_id=1, source_target_pairs={{0,1},{1,2},{2,3},{3,4},{4,5},{5,6},{6,7},{8,9},{9,10},{10,11},{11... | collective-permute-start | bytes 393224 | tf_op jit(solution)/shard_map/ppermute | solution.py:14
  23.0 1.9 %collective-permute-start.1 = (bf16[8,16,1,512]{3,1,2,0:T(8,128)(2,1)S(1)}, bf16[8,16,1,512]{3,1,2,0:T(8,128)(2,1)S(1)}, u32[]{:S(2)}, u32[]{:S(2)}) collective-permute-start(bf16[8,16,1,512]{3,1,2,0:T(8,128)(2,1)S(1)} %get-tuple-element.19), channel_id=1, source_target_pairs={{1,0},{2,1},{3,2},{4,3},{5,4},{6,5},{7,6},{9,8},{10,9},{11,10},{12... | collective-permute-start | bytes 393224 | tf_op jit(solution)/shard_map/ppermute | solution.py:15
  24.9 3.4 %fusion.47 = (bf16[1,3,3,512,128]{4,3,2,1,0:T(8,128)(2,1)S(1)}, bf16[1,3,3,512,128]{4,3,2,1,0:T(8,128)(2,1)}, bf16[1,3,3,512,128]{4,3,2,1,0:T(8,128)(2,1)S(1)}) fusion(bf16[3,3,3,512,128]{4,3,2,1,0:T(8,128)(2,1)} %param.7), kind=kLoop, calls=%fused_computation.113 | loop fusion | bytes 7077888 | tf_op jit(solution)/shard_map/slice | solution.py:70
  28.3 2.4 %copy.68 = bf16[1,3,3,512,128]{3,4,2,1,0:T(8,128)(2,1)} copy(bf16[1,3,3,512,128]{4,3,2,1,0:T(8,128)(2,1)} %get-tuple-element.9) | data formatting | bytes 2359296
  32.8 2.5 %collective-permute-done.1 = bf16[8,16,1,512]{3,1,2,0:T(8,128)(2,1)S(1)} collective-permute-done((bf16[8,16,1,512]{3,1,2,0:T(8,128)(2,1)S(1)}, bf16[8,16,1,512]{3,1,2,0:T(8,128)(2,1)S(1)}, u32[]{:S(2)}, u32[]{:S(2)}) %collective-permute-start.1) | collective-permute-done | bytes 131104 | tf_op jit(solution)/shard_map/ppermute | solution.py:15
  39.7 7.0 %all_to_all.4 = bf16[8,16,2,128]{3,2,0,1:T(2,128)(2,1)S(1)} all-to-all(bf16[8,16,2,128]{3,2,0,1:T(2,128)(2,1)S(1)} %copy.43), channel_id=1, replica_groups=mesh['grp'=4,'tile'=8] {'grp'}, dimensions={1} | all-to-all | bytes 131072 | tf_op jit(solution)/shard_map/all_to_all | solution.py:100
  47.4 2.4 %collective-permute-start.2 = (bf16[8,1,4,256]{3,2,1,0:T(4,128)(2,1)S(1)}, bf16[8,1,4,256]{3,2,1,0:T(4,128)(2,1)S(1)}, u32[]{:S(2)}, u32[]{:S(2)}) collective-permute-start(bf16[8,1,4,256]{3,2,1,0:T(4,128)(2,1)S(1)} %get-tuple-element.23), channel_id=1, source_target_pairs={{0,8},{8,16},{16,24},{1,9},{9,17},{17,25},{2,10},{10,18},{18,26},{... | collective-permute-start | bytes 49160 | tf_op jit(solution)/shard_map/ppermute | solution.py:14
  51.2 3.1 %collective-permute-done.3 = bf16[8,1,4,256]{3,2,1,0:T(4,128)(2,1)S(1)} collective-permute-done((bf16[8,1,4,256]{3,2,1,0:T(4,128)(2,1)S(1)}, bf16[8,1,4,256]{3,2,1,0:T(4,128)(2,1)S(1)}, u32[]{:S(2)}, u32[]{:S(2)}) %collective-permute-start.3) | collective-permute-done | bytes 16416 | tf_op jit(solution)/shard_map/ppermute | solution.py:15
  54.4 3.2 %collective-permute-start.4 = (bf16[8,10,1,256]{3,2,1,0:T(2,128)(2,1)S(1)}, bf16[8,10,1,256]{3,2,1,0:T(2,128)(2,1)S(1)}, u32[]{:S(2)}, u32[]{:S(2)}) collective-permute-start(bf16[8,10,1,256]{3,2,1,0:T(2,128)(2,1)S(1)} %get-tuple-element.20), channel_id=1, source_target_pairs={{0,1},{1,2},{2,3},{3,4},{4,5},{5,6},{6,7},{8,9},{9,10},{10,11},{11... | collective-permute-start | bytes 122888 | tf_op jit(solution)/shard_map/ppermute | solution.py:14
  57.6 1.9 %collective-permute-start.5 = (bf16[8,10,1,256]{3,2,1,0:T(2,128)(2,1)S(1)}, bf16[8,10,1,256]{3,2,1,0:T(2,128)(2,1)S(1)}, u32[]{:S(2)}, u32[]{:S(2)}) collective-permute-start(bf16[8,10,1,256]{3,2,1,0:T(2,128)(2,1)S(1)} %get-tuple-element.21), channel_id=1, source_target_pairs={{1,0},{2,1},{3,2},{4,3},{5,4},{6,5},{7,6},{9,8},{10,9},{11,10},{12... | collective-permute-start | bytes 122888 | tf_op jit(solution)/shard_map/ppermute | solution.py:15
  60.0 3.4 %collective-permute-done.5 = bf16[8,10,1,256]{3,2,1,0:T(2,128)(2,1)S(1)} collective-permute-done((bf16[8,10,1,256]{3,2,1,0:T(2,128)(2,1)S(1)}, bf16[8,10,1,256]{3,2,1,0:T(2,128)(2,1)S(1)}, u32[]{:S(2)}, u32[]{:S(2)}) %collective-permute-start.5) | collective-permute-done | bytes 40992 | tf_op jit(solution)/shard_map/ppermute | solution.py:15
  70.8 3.3 %fusion.46 = (bf16[1,3,3,256,256]{3,4,2,1,0:T(8,128)(2,1)S(1)}, bf16[1,3,3,256,256]{3,4,2,1,0:T(8,128)(2,1)S(1)}, bf16[1,3,3,256,256]{3,4,2,1,0:T(8,128)(2,1)}) fusion(bf16[3,3,3,256,256]{3,4,2,1,0:T(8,128)(2,1)} %all-gather.2.cloned.1.call-done), kind=kLoop, calls=%fused_computation.112 | loop fusion | bytes 7077888 | tf_op jit(solution)/shard_map/slice | solution.py:55
  74.1 2.4 %copy.70 = bf16[1,3,3,256,256]{4,3,2,1,0:T(8,128)(2,1)} copy(bf16[1,3,3,256,256]{3,4,2,1,0:T(8,128)(2,1)} %get-tuple-element.7) | data formatting | bytes 2359296
  76.5 1.5 %copy.71 = bf16[1,3,3,256,256]{4,3,2,1,0:T(8,128)(2,1)} copy(bf16[1,3,3,256,256]{3,4,2,1,0:T(8,128)(2,1)S(1)} %get-tuple-element.6) | data formatting | bytes 2359296
  78.8 2.4 %fusion.53 = f32[8,8,4,256]{3,2,1,0:T(4,128)S(1)} fusion(bf16[10,8,4,2304]{3,2,1,0:T(4,128)(2,1)} %slice_dynamic-update-slice_fusion.9, bf16[2304,256,1,1]{1,0,3,2:T(8,128)(2,1)} %bitcast.105), kind=kOutput, calls=%fused_computation.120 | convolution fusion | flops 301989888 | bytes 2916352 | tf_op jit(solution)/shard_map/dot_general | solution.py:51
  81.2 2.0 %convolution_add_fusion.3 = f32[8,8,4,256]{3,2,1,0:T(4,128)S(1)} fusion(f32[8,8,4,256]{3,2,1,0:T(4,128)S(1)} %fusion.53, bf16[10,8,4,2304]{3,2,1,0:T(4,128)(2,1)} %slice_dynamic-update-slice_fusion.9, bf16[2304,256,1,1]{1,0,3,2:T(8,128)(2,1)S(1)} %bitcast.106), kind=kOutput, calls=%fused_computation.15 | convolution fusion | flops 302055424 | bytes 3178496 | tf_op jit(solution)/shard_map/dot_general | solution.py:53
  83.2 2.0 %fusion.9 = bf16[8,8,4,256]{3,2,1,0:T(4,128)(2,1)S(1)} fusion(f32[8,8,4,256]{3,2,1,0:T(4,128)S(1)} %convert_element_type.86, f32[8,8,4,256]{3,2,1,0:T(4,128)S(1)} %convolution_add_fusion.3, bf16[10,8,4,2304]{3,2,1,0:T(4,128)(2,1)} %slice_dynamic-update-slice_fusion.9, bf16[2304,256,1,1]{1,0,3,2:T(8,128)(2,1)S(1)} %bitcast.104), kind=kOutput, calls=%fused_computation.16 | convolution fusion | flops 302186496 | bytes 3309568 | tf_op jit(solution)/shard_map/dot_general | solution.py:53
  86.0 4.0 %collective-permute-start.6 = (bf16[8,1,8,128]{3,2,1,0:T(8,128)(2,1)S(1)}, bf16[8,1,8,128]{3,2,1,0:T(8,128)(2,1)S(1)}, u32[]{:S(2)}, u32[]{:S(2)}) collective-permute-start(bf16[8,1,8,128]{3,2,1,0:T(8,128)(2,1)S(1)} %get-tuple-element.16), channel_id=1, source_target_pairs={{0,8},{8,16},{16,24},{1,9},{9,17},{17,25},{2,10},{10,18},{18,26},{... | collective-permute-start | bytes 49160 | tf_op jit(solution)/shard_map/ppermute | solution.py:14
  91.3 3.2 %collective-permute-done.7 = bf16[8,1,8,128]{3,2,1,0:T(8,128)(2,1)S(1)} collective-permute-done((bf16[8,1,8,128]{3,2,1,0:T(8,128)(2,1)S(1)}, bf16[8,1,8,128]{3,2,1,0:T(8,128)(2,1)S(1)}, u32[]{:S(2)}, u32[]{:S(2)}) %collective-permute-start.7) | collective-permute-done | bytes 16416 | tf_op jit(solution)/shard_map/ppermute | solution.py:15
  94.6 3.3 %collective-permute-start.8 = (bf16[8,18,1,128]{3,2,1,0:T(2,128)(2,1)S(1)}, bf16[8,18,1,128]{3,2,1,0:T(2,128)(2,1)S(1)}, u32[]{:S(2)}, u32[]{:S(2)}) collective-permute-start(bf16[8,18,1,128]{3,2,1,0:T(2,128)(2,1)S(1)} %get-tuple-element.14), channel_id=1, source_target_pairs={{0,1},{1,2},{2,3},{3,4},{4,5},{5,6},{6,7},{8,9},{9,10},{10,11},{11... | collective-permute-start | bytes 110600 | tf_op jit(solution)/shard_map/ppermute | solution.py:14
  97.9 2.1 %collective-permute-start.9 = (bf16[8,18,1,128]{3,2,1,0:T(2,128)(2,1)S(1)}, bf16[8,18,1,128]{3,2,1,0:T(2,128)(2,1)S(1)}, u32[]{:S(2)}, u32[]{:S(2)}) collective-permute-start(bf16[8,18,1,128]{3,2,1,0:T(2,128)(2,1)S(1)} %get-tuple-element.15), channel_id=1, source_target_pairs={{1,0},{2,1},{3,2},{4,3},{5,4},{6,5},{7,6},{9,8},{10,9},{11,10},{12... | collective-permute-start | bytes 110600 | tf_op jit(solution)/shard_map/ppermute | solution.py:15
  100.1 3.4 %collective-permute-done.9 = bf16[8,18,1,128]{3,2,1,0:T(2,128)(2,1)S(1)} collective-permute-done((bf16[8,18,1,128]{3,2,1,0:T(2,128)(2,1)S(1)}, bf16[8,18,1,128]{3,2,1,0:T(2,128)(2,1)S(1)}, u32[]{:S(2)}, u32[]{:S(2)}) %collective-permute-start.9) | collective-permute-done | bytes 36896 | tf_op jit(solution)/shard_map/ppermute | solution.py:15
  107.0 1.5 %fusion.7 = bf16[8,16,8,128]{3,2,1,0:T(8,128)(2,1)} fusion(f32[8,16,8,128]{3,2,1,0:T(8,128)S(1)} %bitcast.99, f32[8,16,8,128]{3,2,1,0:T(8,128)S(1)} %convolution_add_fusion.1, bf16[10,16,8,1152]{3,2,1,0:T(8,128)(2,1)S(1)} %slice_dynamic-update-slice_fusion, bf16[1152,128,1,1]{1,0,3,2:T(8,128)(2,1)S(1)} %bitcast.100), kind=kOutput, calls=%fused_computation.12 | convolution fusion | flops 302383104 | bytes 4554752 | tf_op jit(solution)/shard_map/dot_general | solution.py:53
  (88 shorter events, 25.5 us)
Async XLA Ops:
  6.5 40.2 %copy-start = (bf16[512,256]{1,0:T(8,128)(2,1)S(1)}, bf16[512,256]{1,0:T(8,128)(2,1)}, u32[]{:S(2)}) copy-start(bf16[512,256]{1,0:T(8,128)(2,1)} %param.10) | copy-start | bytes 786436
  6.5 64.3 %all-gather.2.cloned.1.call-start = ((), (), s32[]{:S(2)}) async-start(), calls=%async_computation.1 | async-start | bytes 3981312 | tf_op jit(solution)/shard_map/all_gather | solution.py:91
  17.2 15.6 %collective-permute-start = (bf16[8,16,1,512]{3,1,2,0:T(8,128)(2,1)S(1)}, bf16[8,16,1,512]{3,1,2,0:T(8,128)(2,1)S(1)}, u32[]{:S(2)}, u32[]{:S(2)}) collective-permute-start(bf16[8,16,1,512]{3,1,2,0:T(8,128)(2,1)S(1)} %get-tuple-element.18), channel_id=1, source_target_pairs={{0,1},{1,2},{2,3},{3,4},{4,5},{5,6},{6,7},{8,9},{9,10},{10,11},{11... | collective-permute-start | bytes 393224 | tf_op jit(solution)/shard_map/ppermute | solution.py:14
  23.0 12.4 %collective-permute-start.1 = (bf16[8,16,1,512]{3,1,2,0:T(8,128)(2,1)S(1)}, bf16[8,16,1,512]{3,1,2,0:T(8,128)(2,1)S(1)}, u32[]{:S(2)}, u32[]{:S(2)}) collective-permute-start(bf16[8,16,1,512]{3,1,2,0:T(8,128)(2,1)S(1)} %get-tuple-element.19), channel_id=1, source_target_pairs={{1,0},{2,1},{3,2},{4,3},{5,4},{6,5},{7,6},{9,8},{10,9},{11,10},{12... | collective-permute-start | bytes 393224 | tf_op jit(solution)/shard_map/ppermute | solution.py:15
  35.3 1.3 %copy-start.2 = (bf16[1,3,3,512,128]{3,4,2,1,0:T(8,128)(2,1)S(1)}, bf16[1,3,3,512,128]{3,4,2,1,0:T(8,128)(2,1)}, u32[]{:S(2)}) copy-start(bf16[1,3,3,512,128]{3,4,2,1,0:T(8,128)(2,1)} %copy.68) | copy-start | bytes 3538948
  36.7 1.3 %copy-start.1 = (bf16[1,3,3,512,128]{3,4,2,1,0:T(8,128)(2,1)S(1)}, bf16[1,3,3,512,128]{3,4,2,1,0:T(8,128)(2,1)}, u32[]{:S(2)}) copy-start(bf16[1,3,3,512,128]{3,4,2,1,0:T(8,128)(2,1)} %copy.67) | copy-start | bytes 3538948
  39.3 7.5 %copy-start.5 = (bf16[8,4,2,512]{3,2,1,0:T(2,128)(2,1)S(1)}, bf16[8,4,2,512]{3,2,1,0:T(2,128)(2,1)}, u32[]{:S(2)}) copy-start(bf16[8,4,2,512]{3,2,1,0:T(2,128)(2,1)} %param.6) | copy-start | bytes 196612
  47.4 3.7 %collective-permute-start.2 = (bf16[8,1,4,256]{3,2,1,0:T(4,128)(2,1)S(1)}, bf16[8,1,4,256]{3,2,1,0:T(4,128)(2,1)S(1)}, u32[]{:S(2)}, u32[]{:S(2)}) collective-permute-start(bf16[8,1,4,256]{3,2,1,0:T(4,128)(2,1)S(1)} %get-tuple-element.23), channel_id=1, source_target_pairs={{0,8},{8,16},{16,24},{1,9},{9,17},{17,25},{2,10},{10,18},{18,26},{... | collective-permute-start | bytes 49160 | tf_op jit(solution)/shard_map/ppermute | solution.py:14
  49.8 4.5 %collective-permute-start.3 = (bf16[8,1,4,256]{3,2,1,0:T(4,128)(2,1)S(1)}, bf16[8,1,4,256]{3,2,1,0:T(4,128)(2,1)S(1)}, u32[]{:S(2)}, u32[]{:S(2)}) collective-permute-start(bf16[8,1,4,256]{3,2,1,0:T(4,128)(2,1)S(1)} %get-tuple-element.22), channel_id=1, source_target_pairs={{8,0},{16,8},{24,16},{9,1},{17,9},{25,17},{10,2},{18,10},{26,18},{... | collective-permute-start | bytes 49160 | tf_op jit(solution)/shard_map/ppermute | solution.py:15
  54.4 5.6 %collective-permute-start.4 = (bf16[8,10,1,256]{3,2,1,0:T(2,128)(2,1)S(1)}, bf16[8,10,1,256]{3,2,1,0:T(2,128)(2,1)S(1)}, u32[]{:S(2)}, u32[]{:S(2)}) collective-permute-start(bf16[8,10,1,256]{3,2,1,0:T(2,128)(2,1)S(1)} %get-tuple-element.20), channel_id=1, source_target_pairs={{0,1},{1,2},{2,3},{3,4},{4,5},{5,6},{6,7},{8,9},{9,10},{10,11},{11... | collective-permute-start | bytes 122888 | tf_op jit(solution)/shard_map/ppermute | solution.py:14
  57.6 5.8 %collective-permute-start.5 = (bf16[8,10,1,256]{3,2,1,0:T(2,128)(2,1)S(1)}, bf16[8,10,1,256]{3,2,1,0:T(2,128)(2,1)S(1)}, u32[]{:S(2)}, u32[]{:S(2)}) collective-permute-start(bf16[8,10,1,256]{3,2,1,0:T(2,128)(2,1)S(1)} %get-tuple-element.21), channel_id=1, source_target_pairs={{1,0},{2,1},{3,2},{4,3},{5,4},{6,5},{7,6},{9,8},{10,9},{11,10},{12... | collective-permute-start | bytes 122888 | tf_op jit(solution)/shard_map/ppermute | solution.py:15
  78.8 2.4 %copy-start.3 = (bf16[1,3,3,256,256]{4,3,2,1,0:T(8,128)(2,1)S(1)}, bf16[1,3,3,256,256]{4,3,2,1,0:T(8,128)(2,1)}, u32[]{:S(2)}) copy-start(bf16[1,3,3,256,256]{4,3,2,1,0:T(8,128)(2,1)} %copy.71) | copy-start | bytes 3538948
  83.2 2.0 %copy-start.6 = (bf16[256,128]{1,0:T(8,128)(2,1)S(1)}, bf16[256,128]{1,0:T(8,128)(2,1)}, u32[]{:S(2)}) copy-start(bf16[256,128]{1,0:T(8,128)(2,1)} %param.11) | copy-start | bytes 196612
  85.2 14.7 %copy-start.4 = (bf16[3,3,3,128,128]{4,3,2,1,0:T(8,128)(2,1)S(1)}, bf16[3,3,3,128,128]{4,3,2,1,0:T(8,128)(2,1)}, u32[]{:S(2)}) copy-start(bf16[3,3,3,128,128]{4,3,2,1,0:T(8,128)(2,1)} %param.9) | copy-start | bytes 2654212
  86.0 5.3 %collective-permute-start.6 = (bf16[8,1,8,128]{3,2,1,0:T(8,128)(2,1)S(1)}, bf16[8,1,8,128]{3,2,1,0:T(8,128)(2,1)S(1)}, u32[]{:S(2)}, u32[]{:S(2)}) collective-permute-start(bf16[8,1,8,128]{3,2,1,0:T(8,128)(2,1)S(1)} %get-tuple-element.16), channel_id=1, source_target_pairs={{0,8},{8,16},{16,24},{1,9},{9,17},{17,25},{2,10},{10,18},{18,26},{... | collective-permute-start | bytes 49160 | tf_op jit(solution)/shard_map/ppermute | solution.py:14
  90.0 4.5 %collective-permute-start.7 = (bf16[8,1,8,128]{3,2,1,0:T(8,128)(2,1)S(1)}, bf16[8,1,8,128]{3,2,1,0:T(8,128)(2,1)S(1)}, u32[]{:S(2)}, u32[]{:S(2)}) collective-permute-start(bf16[8,1,8,128]{3,2,1,0:T(8,128)(2,1)S(1)} %get-tuple-element.17), channel_id=1, source_target_pairs={{8,0},{16,8},{24,16},{9,1},{17,9},{25,17},{10,2},{18,10},{26,18},{... | collective-permute-start | bytes 49160 | tf_op jit(solution)/shard_map/ppermute | solution.py:15
  94.6 5.5 %collective-permute-start.8 = (bf16[8,18,1,128]{3,2,1,0:T(2,128)(2,1)S(1)}, bf16[8,18,1,128]{3,2,1,0:T(2,128)(2,1)S(1)}, u32[]{:S(2)}, u32[]{:S(2)}) collective-permute-start(bf16[8,18,1,128]{3,2,1,0:T(2,128)(2,1)S(1)} %get-tuple-element.14), channel_id=1, source_target_pairs={{0,1},{1,2},{2,3},{3,4},{4,5},{5,6},{6,7},{8,9},{9,10},{10,11},{11... | collective-permute-start | bytes 110600 | tf_op jit(solution)/shard_map/ppermute | solution.py:14
  97.9 5.7 %collective-permute-start.9 = (bf16[8,18,1,128]{3,2,1,0:T(2,128)(2,1)S(1)}, bf16[8,18,1,128]{3,2,1,0:T(2,128)(2,1)S(1)}, u32[]{:S(2)}, u32[]{:S(2)}) collective-permute-start(bf16[8,18,1,128]{3,2,1,0:T(2,128)(2,1)S(1)} %get-tuple-element.15), channel_id=1, source_target_pairs={{1,0},{2,1},{3,2},{4,3},{5,4},{6,5},{7,6},{9,8},{10,9},{11,10},{12... | collective-permute-start | bytes 110600 | tf_op jit(solution)/shard_map/ppermute | solution.py:15
Sparse Core Ops, SparseCore 0:
  9.0 45.3 all-gather.1
where the time goes:
time: 116 us; the launch traced here: 115 us
  starting transfers between devices  27.1 us (23%)
  local copies, waits for them, and re-layouts  25.9 us (22%)
  waiting for transfers between devices  16.3 us (14%)
  blocking collectives  14.8 us (13%)
  between operations  14 us (12%)
  matrix products  13.9 us (12%)
  other arithmetic  3.28 us (3%)
    ppermute x5, starting transfers between devices, with_halo(): before = lax.ppermute(last, axis, up)  18.6 us
    unnamed x38, local copies, waits for them, and re-layouts  16.6 us
    ppermute x5, waiting for transfers between devices, with_halo(): after = lax.ppermute(initial, axis, down)  15.6 us
    ppermute x5, starting transfers between devices, with_halo(): after = lax.ppermute(initial, axis, down)  8.53 us
    all_gather x1, blocking collectives, body(): whole = lax.all_gather(first_act, 'grp', axis=1, tiled=True)  7.81 us
    all_to_all x1, blocking collectives, body(): lax.all_to_all(filtered, 'grp', split_axis=1, concat_axis=3, tiled=True)  7.02 us
    dot_general x4, matrix products, apply_columns(): jnp.dot(columns[frame_step:frame_step + frames], folded[frame_step], pref...  6.27 us
    dot_general x3, matrix products, coarse_conv(): jnp.dot(padded[frame_step:frame_step + frames], spread, preferred_element...  3.92 us
  transfers between devices with their start and end apart: 11, of which 5 were waited for; matrix products, arithmetic and copies ran while one was open for 20% of the time, Pallas kernels for 0%

commit v1 on v0

v1 whole, which is shorter than its diff:
```python
import functools

import jax
import jax.numpy as jnp
from jax import lax
from jax.experimental import pallas as pl
from jax.experimental.pallas import tpu as pltpu
from jax.sharding import PartitionSpec as P

VMEM = pl.BlockSpec(memory_space=pltpu.VMEM)
F32 = jnp.float32
BF16 = jnp.bfloat16


def call(kernel, outs, scratch, flops, nbytes, *args):
    return pl.pallas_call(
        kernel,
        out_shape=outs,
        in_specs=[VMEM] * len(args),
        out_specs=jax.tree.map(lambda _: VMEM, outs),
        scratch_shapes=scratch,
        compiler_params=pltpu.CompilerParams(vmem_limit_bytes=40 << 20),
        cost_estimate=pl.CostEstimate(flops=flops, bytes_accessed=nbytes, transcendentals=0),
    )(*args)


def dot(left, right):
    return jnp.dot(left, right, preferred_element_type=F32)


def activate(values):
    scaled = values * lax.rsqrt(jnp.mean(values * values, axis=-1, keepdims=True) + 1e-06)
    return scaled / (1.0 + jnp.exp(-scaled))


def delayed(values, steps):
    if steps == 0:
        return values
    axis = values.ndim - 2
    frame = lax.broadcasted_iota(jnp.int32, values.shape, axis)
    return jnp.where(frame >= steps, pltpu.roll(values, steps, axis), 0.0)


def coarse_kernel(groups, *refs):
    pieces, (filters, proj, part, straight, shifted) = refs[:groups], refs[groups:]
    rows, cols, frames, depth = pieces[0].shape
    width = filters.shape[4]
    height = groups * rows
    me = lax.axis_index("grp")
    edge = jnp.zeros((1, cols * frames, depth), BF16)
    for step in range(3):
        shifted[step, 0:1] = edge
        shifted[step, height + 1 : height + 2] = edge
    for k in range(groups):
        at = (me ^ k) * rows
        raw = pieces[k][...]
        flat = raw.reshape(rows * cols * frames, depth)
        direct = dot(flat, proj[...]).reshape(rows, cols, frames, proj.shape[1])
        for col in range(cols):
            straight[col, pl.ds(at, rows)] = direct[:, col]
        act = activate(raw.astype(F32))
        for step in range(3):
            moved = delayed(act, 2 - step).reshape(rows, cols * frames, depth)
            shifted[step, pl.ds(at + 1, rows)] = moved.astype(BF16)
    joined = width % 128 == 0
    totals = [None] * (1 if joined else 3)
    for step in range(3):
        for row in range(3):
            left = shifted[step, row : row + height].reshape(height * cols * frames, depth)
            taps = [filters[step, row, col] for col in range(3)]
            if joined:
                taps = [jnp.concatenate(taps, axis=1)]
            for n, tap in enumerate(taps):
                term = dot(left, tap)
                totals[n] = term if totals[n] is None else totals[n] + term
    if joined:
        totals = [totals[0][:, n * width : (n + 1) * width] for n in range(3)]
    totals = [total.reshape(height, cols, frames, width) for total in totals]
    for out in range(cols + 2):
        value = sum(
            totals[tap][:, out - 2 + tap] for tap in range(3) if 0 <= out - 2 + tap < cols
        )
        part[out] = value.reshape(height * frames, width).astype(BF16)


def project_kernel(groups, *refs):
    parts, (proj, straight, own, even_out, odd_out) = refs[:groups], refs[groups:]
    extent, cells, width = parts[0].shape
    outputs = proj.shape[2]
    total = None
    for k in range(groups):
        term = dot(parts[k][...].reshape(extent * cells, width), proj[k])
        total = term if total is None else total + term
    total = total.reshape(extent, cells, outputs)
    cols = extent - 2
    middle = total[1 : cols + 1] + straight[...].reshape(cols, cells, outputs)
    own[0] = total[0]
    own[1 : cols + 1] = middle
    own[cols + 1] = total[cols + 1]
    left = jnp.stack([total[0], middle[0]])
    right = jnp.stack([middle[cols - 1], total[cols + 1]])
    odd = lax.axis_index("tile") % 2 == 1
    even_out[...] = jnp.where(odd, left, right).astype(BF16)
    odd_out[...] = jnp.where(odd, right, left).astype(BF16)


def middle_kernel(groups, rows, frames, own, even_in, odd_in, filters, *refs):
    outs, (block, acts, acts_odd, kept, sums) = refs[:groups], refs[groups:]
    extent, cells, depth = own.shape
    cols = extent - 2
    height = cells // frames
    me = lax.axis_index("grp")
    tile = lax.axis_index("tile")
    odd = tile % 2 == 1
    even_got = even_in[...].astype(F32)
    odd_got = odd_in[...].astype(F32)
    from_left = jnp.where(odd, even_got, odd_got)
    from_right = jnp.where(odd, odd_got, even_got)
    values = []
    for col in range(extent):
        value = own[col]
        if col < 2:
            value = value + from_left[col]
        if col >= cols:
            value = value + from_right[col - cols]
        if col == 0:
            value = jnp.where(tile == 0, 0.0, value)
        if col == extent - 1:
            value = jnp.where(tile == lax.axis_size("tile") - 1, 0.0, value)
        values.append(value.astype(BF16).astype(F32).reshape(height, frames, depth))
    nothing = jnp.zeros((1, frames, depth), F32)
    for col in range(extent):
        kept[col, 0:1] = nothing
        kept[col, 1 : height + 1] = values[col]
        kept[col, height + 1 : height + 2] = nothing
        act = activate(values[col])
        for step in range(3):
            moved = delayed(act, 2 - step)
            framed = jnp.concatenate([nothing, moved, nothing], axis=0)
            acts[step, col] = framed.reshape(cells + 2 * frames, depth).astype(BF16)
            acts_odd[step, col] = moved.reshape(cells, depth).astype(BF16)
    block[...] = (
        kept[:, pl.ds(me * rows, rows + 2)]
        .reshape(extent, (rows + 2) * frames, depth)
        .astype(BF16)
    )
    pairs = extent - 1
    total = None
    for step in range(3):
        for row in range(3):
            for side in range(2):
                if row == 1:
                    left = acts_odd[step, side : side + pairs]
                else:
                    first = row * frames
                    left = acts[step, side : side + pairs, first : first + cells]
                term = dot(left.reshape(pairs * cells, depth), filters[step, row, side])
                total = term if total is None else total + term
    lanes = total.shape[1]
    total = total.reshape(pairs, height, frames, lanes)
    empty = jnp.zeros((pairs, 1, frames, lanes), F32)
    sums[:, 0:1] = empty
    sums[:, 1 : height + 1] = total
    sums[:, height + 1 : height + 2] = empty
    for k in range(groups):
        chunk = sums[:, pl.ds((me ^ k) * rows, rows + 2)]
        outs[k][...] = chunk.reshape(pairs, (rows + 2) * frames, lanes).astype(BF16)


def fine_kernel(groups, frames, *refs):
    chunks = refs[:groups]
    block, spread, proj, filters, out, acts, acts_odd, lows = refs[groups:]
    pairs, cells, lanes = chunks[0].shape
    extent = block.shape[0]
    rows = cells // frames - 2
    width = proj.shape[1]
    tall, broad = 2 * rows, 2 * (extent - 2)
    me, last_me = lax.axis_index("grp"), lax.axis_size("grp") - 1
    tile, last_tile = lax.axis_index("tile"), lax.axis_size("tile") - 1
    total = None
    for k in range(groups):
        term = dot(chunks[k][...].reshape(pairs * cells, lanes), spread[k])
        total = term if total is None else total + term
    total = total.reshape(pairs, rows + 2, frames, 4 * width)
    base = dot(block[...].reshape(extent * cells, block.shape[2]), proj[...])
    base = base.reshape(extent, rows + 2, frames, width)
    nothing = jnp.zeros((1, frames, width), F32)
    for col in range(broad + 2):
        pair, side = divmod(col, 2)
        upper, lower = [
            total[pair, :, :, (2 * p + side) * width : (2 * p + side + 1) * width]
            + base[pair + side]
            for p in range(2)
        ]
        woven = jnp.stack([lower[: rows + 1], upper[1:]], axis=1)
        value = woven.reshape(tall + 2, frames, width).astype(BF16).astype(F32)
        if col == 0:
            value = jnp.where(tile == 0, 0.0, value)
        if col == broad + 1:
            value = jnp.where(tile == last_tile, 0.0, value)
        top = jnp.where(me == 0, 0.0, value[0:1])
        bottom = jnp.where(me == last_me, 0.0, value[tall + 1 : tall + 2])
        value = jnp.concatenate([top, value[1 : tall + 1], bottom], axis=0)
        lows[col] = value[1 : tall + 1]
        act = activate(value)
        for step in range(3):
            moved = delayed(act, 2 - step)
            acts[step, col] = moved.reshape((tall + 2) * frames, width).astype(BF16)
            acts_odd[step, col] = (
                moved[1 : tall + 1].reshape(tall * frames, width).astype(BF16)
            )
    span = broad + 1
    strip = tall * frames
    for p in range(2):
        sums = None
        for step in range(3):
            for near in range(2):
                row = p + near
                if row == 1:
                    pick = [acts_odd[step, side : side + span] for side in range(2)]
                else:
                    first = row * frames
                    pick = [
                        acts[step, side : side + span, first : first + strip]
                        for side in range(2)
                    ]
                left = jnp.concatenate([v.reshape(span * strip, width) for v in pick], axis=1)
                term = dot(left, filters[step, p, near])
                sums = term if sums is None else sums + term
        sums = sums.reshape(span, tall, frames, 2 * width)
        fields = []
        for col in range(2 * broad):
            pair, side = divmod(col + 1, 2)
            low = lows[pair + side]
            fields.append(sums[pair, :, :, side * width : (side + 1) * width] + low)
        field = jnp.stack(fields, axis=1)
        for row in range(tall):
            out[:, 2 * row + p] = jnp.swapaxes(field[row], 0, 1).astype(BF16)


def fold_middle_kernel(pieces, out):
    parts, n, depth = pieces.shape[0], pieces.shape[4], pieces.shape[5]

    def per_step(step, carry):
        taps = [
            [
                pieces[:, step, row, col].astype(F32).reshape(parts * n, depth)
                for col in range(3)
            ]
            for row in range(3)
        ]
        nothing = jnp.zeros((parts * n, depth), F32)
        for side in range(2):
            narrow = [
                [taps[r][0] + taps[r][1] if side == 0 else taps[r][2],
                 taps[r][0] if side == 0 else taps[r][1] + taps[r][2]]
                for r in range(3)
            ]
            for row in range(3):
                blocks = []
                for p in range(2):
                    for q in range(2):
                        if row == 1:
                            value = narrow[1][q] + narrow[2 if p == 0 else 0][q]
                        elif row == 0:
                            value = narrow[0][q] if p == 0 else nothing
                        else:
                            value = nothing if p == 0 else narrow[2][q]
                        blocks.append(value)
                out[step, row, side] = jnp.concatenate(blocks, axis=0).T.astype(BF16)
        return carry

    lax.fori_loop(0, 3, per_step, 0)


def fold_fine_kernel(filters, out):
    def per_step(step, carry):
        taps = [[filters[step, r, c].astype(F32) for c in range(3)] for r in range(3)]
        for p in range(2):
            for near in range(2):
                if p == 0:
                    line = taps[0] if near == 0 else [x + y for x, y in zip(taps[1], taps[2])]
                else:
                    line = [x + y for x, y in zip(taps[0], taps[1])] if near == 0 else taps[2]
                first = jnp.concatenate([line[0] + line[1], line[0]], axis=1)
                second = jnp.concatenate([line[2], line[1] + line[2]], axis=1)
                out[step, p, near] = jnp.concatenate([first, second], axis=0).astype(BF16)
        return carry

    lax.fori_loop(0, 3, per_step, 0)


def reorder(values, index):
    size, rest = values.shape[0], values.shape[1:]
    bit = 1
    while bit < size:
        pairs = values.reshape(size // (2 * bit), 2, bit, *rest)
        pairs = jnp.where((index & bit) != 0, pairs[:, ::-1], pairs)
        values = pairs.reshape(size, *rest)
        bit *= 2
    return values


def exchange(values, axis, k):
    size = lax.axis_size(axis)
    return lax.ppermute(values, axis, [(i, i ^ k) for i in range(size)])


def body(latent, coarse_filters, mid_filters, fine_filters, coarse_proj, mid_proj):
    groups, tiles = lax.axis_size("grp"), lax.axis_size("tile")
    me, tile = lax.axis_index("grp"), lax.axis_index("tile")
    frames, rows, cols, depth0 = latent.shape
    depth1, depth2 = mid_proj.shape
    width0 = coarse_filters.shape[4]
    height = groups * rows
    cells = height * frames
    own_mid = mid_filters.shape[4]

    first = jnp.transpose(latent, (1, 2, 0, 3))
    pieces = [first] + [exchange(first, "grp", k) for k in range(1, groups)]

    mid_rows = jnp.transpose(mid_filters, (0, 1, 2, 4, 3))
    if own_mid % groups == 0 and (own_mid // groups) % 8 == 0:
        share = own_mid // groups
        mine = lax.dynamic_slice_in_dim(mid_rows, me * share, share, axis=3)[None]
        bit = 2
        while bit < tiles:
            mine = jnp.concatenate([mine, exchange(mine, "tile", bit)])
            bit *= 2
        mine = jnp.concatenate([mine, exchange(mine, "tile", 1)])
        table = mid_proj.reshape(tiles // 2, 2, groups, share, depth2).transpose(1, 0, 2, 3, 4)
        table = reorder(table, tile & 1)
        table = jnp.swapaxes(reorder(jnp.swapaxes(table, 0, 1), tile >> 1), 0, 1)
        table = table.transpose(2, 0, 1, 3, 4).reshape(groups, tiles * share, depth2)
    else:
        share = depth1 // groups
        every = lax.all_gather(mid_rows, "tile", axis=3, tiled=True)
        mine = lax.dynamic_slice_in_dim(every, me * share, share, axis=3)[None]
        table = mid_proj.reshape(groups, share, depth2)
    lanes = 4 * mine.shape[0] * mine.shape[4]
    table = reorder(table, me)
    spread = (
        jnp.eye(4, dtype=BF16)[None, :, None, :, None] * table[:, None, :, None, :]
    ).reshape(groups, lanes, 4 * depth2)
    proj = reorder(coarse_proj.reshape(groups, width0, depth1), me)

    fine_folded = call(
        fold_fine_kernel,
        jax.ShapeDtypeStruct((3, 2, 2, 2 * depth2, 2 * depth2), BF16),
        [],
        10**6,
        4 * 10**6,
        fine_filters,
    )
    mid_folded = call(
        fold_middle_kernel,
        jax.ShapeDtypeStruct((3, 3, 2, depth1, lanes), BF16),
        [],
        10**6,
        4 * 10**6,
        mine,
    )

    part, straight = call(
        functools.partial(coarse_kernel, groups),
        (
            jax.ShapeDtypeStruct((cols + 2, cells, width0), BF16),
            jax.ShapeDtypeStruct((cols, height, frames, depth1), F32),
        ),
        [pltpu.VMEM((3, height + 2, cols * frames, depth0), BF16)],
        2 * 27 * cells * cols * depth0 * width0,
        5 * 10**6,
        *pieces,
        coarse_filters,
        coarse_proj,
    )
    parts = [part] + [exchange(part, "grp", k) for k in range(1, groups)]
    own, even_out, odd_out = call(
        functools.partial(project_kernel, groups),
        (
            jax.ShapeDtypeStruct((cols + 2, cells, depth1), F32),
            jax.ShapeDtypeStruct((2, cells, depth1), BF16),
            jax.ShapeDtypeStruct((2, cells, depth1), BF16),
        ),
        [],
        2 * cells * (cols + 2) * depth0 * depth1,
        2 * 10**6,
        *parts,
        proj,
        straight,
    )
    odd_pairs = [(i, i + 1) for i in range(1, tiles - 1, 2)]
    even_in = exchange(even_out, "tile", 1)
    odd_in = lax.ppermute(odd_out, "tile", odd_pairs + [(j, i) for i, j in odd_pairs])
    local = (rows + 2) * frames
    *chunks, block = call(
        functools.partial(middle_kernel, groups, rows, frames),
        tuple(jax.ShapeDtypeStruct((cols + 1, local, lanes), BF16) for _ in range(groups))
        + (jax.ShapeDtypeStruct((cols + 2, local, depth1), BF16),),
        [
            pltpu.VMEM((3, cols + 2, cells + 2 * frames, depth1), BF16),
            pltpu.VMEM((3, cols + 2, cells, depth1), BF16),
            pltpu.VMEM((cols + 2, height + 2, frames, depth1), F32),
            pltpu.VMEM((cols + 1, height + 2, frames, lanes), F32),
        ],
        2 * 18 * (cols + 1) * cells * depth1 * lanes,
        5 * 10**6,
        own,
        even_in,
        odd_in,
        mid_folded,
    )
    chunks = [chunks[0]] + [exchange(chunks[k], "grp", k) for k in range(1, groups)]
    tall, broad = 2 * rows, 2 * cols
    return call(
        functools.partial(fine_kernel, groups, frames),
        jax.ShapeDtypeStruct((frames, 2 * tall, 2 * broad, depth2), BF16),
        [
            pltpu.VMEM((3, broad + 2, (tall + 2) * frames, depth2), BF16),
            pltpu.VMEM((3, broad + 2, tall * frames, depth2), BF16),
            pltpu.VMEM((broad + 2, tall, frames, depth2), F32),
        ],
        2 * 24 * (broad + 1) * tall * frames * depth2 * 2 * depth2,
        3 * 10**6,
        *chunks,
        block,
        spread,
        mid_proj,
        fine_folded,
    )


def solution(mesh):
    in_specs = (
        P(None, "grp", "tile", None),
        P(None, None, None, None, "grp"),
        P(None, None, None, None, "tile"),
        P(),
        P(),
        P(),
    )
    out_specs = P(None, "grp", "tile", None)
    return jax.shard_map(body, mesh=mesh, in_specs=in_specs, out_specs=out_specs, check_vma=False)
```

time: 116 us -> 52.2 us (0.45)
  local copies, waits for them, and re-layouts: 25.9 us -> 4.01 us
  blocking collectives: 14.8 us -> 0 us
  matrix products: 13.9 us -> 0 us
  between operations: 14 us -> 0.23 us
  starting transfers between devices: 27.1 us -> 18 us
  Pallas kernels: 0 us -> 6.38 us
  waiting for transfers between devices: 16.3 us -> 22 us
  other arithmetic: 3.28 us -> 1.37 us
    dot_general x11 -> x0, matrix products: 13.9 us -> none  [the longest x4 6.27 us: apply_columns(): jnp.dot(columns[frame_step:frame_step + frames], folded[frame_step], pref...]
    unnamed x38 -> x12, local copies, waits for them, and re-layouts: 16.6 us -> 2.97 us
    ppermute x10 -> x14, starting transfers between devices: 27.1 us -> 18 us  [the longest x13 15.8 us: exchange(): return lax.ppermute(values, axis, [(i, i ^ k) for i in range(size)])]
    all_gather x1 -> x0, blocking collectives: 7.81 us -> none  [body(): whole = lax.all_gather(first_act, 'grp', axis=1, tiled=True)]
    all_to_all x1 -> x0, blocking collectives: 7.02 us -> none  [body(): lax.all_to_all(filtered, 'grp', split_axis=1, concat_axis=3, tiled=True)]
    slice x7 -> x0, local copies, waits for them, and re-layouts: 6.93 us -> none  [the longest x1 3.39 us: coarse_conv(): filters[frame_step]]
    pallas_call x0 -> x6, Pallas kernels: none -> 6.38 us  [call(): pl.pallas_call(kernel, out_shape=outs, in_specs=[VMEM] * len(args), out_s...]
    ppermute x10 -> x14, waiting for transfers between devices: 15.6 us -> 22 us  [the longest x13 18.4 us: exchange(): return lax.ppermute(values, axis, [(i, i ^ k) for i in range(size)])]
  transfers between devices with their start and end apart: 11 -> 14, of which waited for: 5 -> 9; matrix products, arithmetic and copies ran while one was open for 20% -> 5% of each run, Pallas kernels for 0% -> 6%
where the time goes in v1:
time: 52.2 us; the launch traced here: 52 us
  waiting for transfers between devices  22 us (42%)
  starting transfers between devices  18 us (34%)
  Pallas kernels  6.38 us (12%)
  local copies, waits for them, and re-layouts  4.01 us (8%)
  other arithmetic  1.37 us (3%)
    ppermute x13, waiting for transfers between devices, exchange(): return lax.ppermute(values, axis, [(i, i ^ k) for i in range(size)])  18.4 us
    ppermute x13, starting transfers between devices, exchange(): return lax.ppermute(values, axis, [(i, i ^ k) for i in range(size)])  15.8 us
    pallas_call x6, Pallas kernels, call(): pl.pallas_call(kernel, out_shape=outs, in_specs=[VMEM] * len(args), out_s...  6.38 us
    ppermute x1, waiting for transfers between devices, body(): lax.ppermute(odd_out, 'tile', odd_pairs + [(j, i) for i, j in odd_pairs])  3.57 us
    unnamed x12, local copies, waits for them, and re-layouts  2.97 us
    ppermute x1, starting transfers between devices, body(): lax.ppermute(odd_out, 'tile', odd_pairs + [(j, i) for i, j in odd_pairs])  2.2 us
  transfers between devices with their start and end apart: 14, of which 9 were waited for; matrix products, arithmetic and copies ran while one was open for 5% of the time, Pallas kernels for 6%

profile of v1, /device:TPU:1, one launch (start us, length us, event | category | flops | bytes accessed | tf_op | source)
XLA Modules:
  0.0 52.0 jit_solution(5520337884009967727)
XLA Ops:
  0.0 0.9 %copy.13 = bf16[8,4,2,512]{3,0,2,1:T(8,128)(2,1)S(1)} copy(bf16[8,4,2,512]{3,2,1,0:T(2,128)(2,1)} %param.6) | data formatting | bytes 131072 | tf_op args[0]
  0.9 2.1 %collective-permute-start = (bf16[4,2,8,512]{3,2,1,0:T(8,128)(2,1)S(1)}, bf16[4,2,8,512]{3,2,1,0:T(8,128)(2,1)S(1)}, u32[]{:S(2)}, u32[]{:S(2)}) collective-permute-start(bf16[4,2,8,512]{3,2,1,0:T(8,128)(2,1)S(1)} %bitcast.33), channel_id=1, source_target_pairs={{0,8},{8,0},{16,24},{24,16},{1,9},{9,1},{17,25},{25,17},{2,10},{10... | collective-permute-start | bytes 196616 | tf_op jit(solution)/shard_map/ppermute | solution.py:306
  3.0 1.2 %collective-permute-start.1 = (bf16[4,2,8,512]{3,2,1,0:T(8,128)(2,1)S(1)}, bf16[4,2,8,512]{3,2,1,0:T(8,128)(2,1)S(1)}, u32[]{:S(2)}, u32[]{:S(2)}) collective-permute-start(bf16[4,2,8,512]{3,2,1,0:T(8,128)(2,1)S(1)} %bitcast.34), channel_id=1, source_target_pairs={{0,16},{8,24},{16,0},{24,8},{1,17},{9,25},{17,1},{25,9},{2,18},{10... | collective-permute-start | bytes 196616 | tf_op jit(solution)/shard_map/ppermute | solution.py:306
  4.3 1.5 %collective-permute-start.8 = (bf16[1,3,3,3,8,256]{5,4,3,2,1,0:T(8,128)(2,1)S(1)}, bf16[1,3,3,3,8,256]{5,4,3,2,1,0:T(8,128)(2,1)S(1)}, u32[]{:S(2)}, u32[]{:S(2)}) collective-permute-start(bf16[1,3,3,3,8,256]{5,4,3,2,1,0:T(8,128)(2,1)S(1)} %dynamic-slice_bitcast_fusion), channel_id=1, source_target_pairs={{0,2},{1,3},{2,0},{3,1},{4,6},{5,7},{6,4},{7,5},{8,10},{9,11},{10,... | collective-permute-start | bytes 331784 | tf_op jit(solution)/shard_map/ppermute | solution.py:306
  5.9 0.9 %reverse_select_fusion.6 = bf16[2,4,4,8,128]{4,3,2,0,1:T(8,128)(2,1)S(1)} fusion(bf16[2,4,4,8,128]{4,3,2,0,1:T(8,128)(2,1)} %bitcast.37, pred[]{:T(512)S(6)} %ne.21), kind=kLoop, calls=%fused_computation.13 | loop fusion | flops 32768 | bytes 131073 | tf_op jit(solution)/shard_map/jit(_where)/select_n | solution.py:298
  8.0 2.5 %collective-permute-start.9 = (bf16[2,3,3,3,8,256]{5,4,3,2,1,0:T(8,128)(2,1)S(1)}, bf16[2,3,3,3,8,256]{5,4,3,2,1,0:T(8,128)(2,1)S(1)}, u32[]{:S(2)}, u32[]{:S(2)}) collective-permute-start(bf16[2,3,3,3,8,256]{5,4,3,2,1,0:T(8,128)(2,1)S(1)} %pad_maximum_fusion.2), channel_id=1, source_target_pairs={{0,4},{1,5},{2,6},{3,7},{4,0},{5,1},{6,2},{7,3},{8,12},{9,13},{10,... | collective-permute-start | bytes 663560 | tf_op jit(solution)/shard_map/ppermute | solution.py:306
  10.6 9.4 %collective-permute-done.9 = bf16[2,3,3,3,8,256]{5,4,3,2,1,0:T(8,128)(2,1)S(1)} collective-permute-done((bf16[2,3,3,3,8,256]{5,4,3,2,1,0:T(8,128)(2,1)S(1)}, bf16[2,3,3,3,8,256]{5,4,3,2,1,0:T(8,128)(2,1)S(1)}, u32[]{:S(2)}, u32[]{:S(2)}) %collective-permute-start.9) | collective-permute-done | bytes 221216 | tf_op jit(solution)/shard_map/ppermute | solution.py:306
  20.1 1.7 %collective-permute-start.10 = (bf16[4,3,3,3,8,256]{5,4,3,2,1,0:T(8,128)(2,1)S(1)}, bf16[4,3,3,3,8,256]{5,4,3,2,1,0:T(8,128)(2,1)S(1)}, u32[]{:S(2)}, u32[]{:S(2)}) collective-permute-start(bf16[4,3,3,3,8,256]{5,4,3,2,1,0:T(8,128)(2,1)S(1)} %pad_maximum_fusion.1), channel_id=1, source_target_pairs={{0,1},{1,0},{2,3},{3,2},{4,5},{5,4},{6,7},{7,6},{8,9},{9,8},{10,11... | collective-permute-start | bytes 1327112 | tf_op jit(solution)/shard_map/ppermute | solution.py:306
  22.0 2.0 %copy-done.1 = bf16[3,3,3,512,128]{4,3,2,1,0:T(8,128)(2,1)S(1)} copy-done((bf16[3,3,3,512,128]{4,3,2,1,0:T(8,128)(2,1)S(1)}, bf16[3,3,3,512,128]{4,3,2,1,0:T(8,128)(2,1)}, u32[]{:S(2)}) %copy-start.1) | copy-done | bytes 3538968
  24.0 1.8 %shard_map.64 = (bf16[4,128,128]{2,1,0:T(8,128)(2,1)S(1)}, f32[2,16,8,256]{3,2,1,0:T(8,128)S(1)}) custom-call(bf16[4,2,8,512]{3,2,1,0:T(8,128)(2,1)S(1)} %bitcast.36, bf16[4,2,8,512]{3,2,1,0:T(8,128)(2,1)S(1)} %collective-permute-done.refs_1_, bf16[4,2,8,512]{3,2,1,0:T(8,128)(2,1)S(1)} %collective-permute-done.1.refs_2_, ...), custom_call_target="tpu_custom_call" | custom-call | flops 905969664 | bytes 5000000 | tf_op jit(solution)/shard_map/pallas_call | solution.py:16
  25.8 1.3 %collective-permute-start.3 = (bf16[4,128,128]{2,1,0:T(8,128)(2,1)S(1)}, bf16[4,128,128]{2,1,0:T(8,128)(2,1)S(1)}, u32[]{:S(2)}, u32[]{:S(2)}) collective-permute-start(bf16[4,128,128]{2,1,0:T(8,128)(2,1)S(1)} %get-tuple-element.15.refs_0_), channel_id=1, source_target_pairs={{0,8},{8,0},{16,24},{24,16},{1,9},{9,1},{17,25},{25,17},{2,10},{10... | collective-permute-start | bytes 393224 | tf_op jit(solution)/shard_map/ppermute | solution.py:306
  27.1 1.3 %collective-permute-start.4 = (bf16[4,128,128]{2,1,0:T(8,128)(2,1)S(1)}, bf16[4,128,128]{2,1,0:T(8,128)(2,1)S(1)}, u32[]{:S(2)}, u32[]{:S(2)}) collective-permute-start(bf16[4,128,128]{2,1,0:T(8,128)(2,1)S(1)} %get-tuple-element.15.refs_0_), channel_id=1, source_target_pairs={{0,16},{8,24},{16,0},{24,8},{1,17},{9,25},{17,1},{25,9},{2,18},{10... | collective-permute-start | bytes 393224 | tf_op jit(solution)/shard_map/ppermute | solution.py:306
  28.6 2.4 %collective-permute-done.3.refs_1_ = bf16[4,128,128]{2,1,0:T(8,128)(2,1)S(1)} collective-permute-done((bf16[4,128,128]{2,1,0:T(8,128)(2,1)S(1)}, bf16[4,128,128]{2,1,0:T(8,128)(2,1)S(1)}, u32[]{:S(2)}, u32[]{:S(2)}) %collective-permute-start.3) | collective-permute-done | bytes 131104 | tf_op jit(solution)/shard_map/ppermute | solution.py:306
  31.0 2.7 %collective-permute-done.4.refs_2_ = bf16[4,128,128]{2,1,0:T(8,128)(2,1)S(1)} collective-permute-done((bf16[4,128,128]{2,1,0:T(8,128)(2,1)S(1)}, bf16[4,128,128]{2,1,0:T(8,128)(2,1)S(1)}, u32[]{:S(2)}, u32[]{:S(2)}) %collective-permute-start.4) | collective-permute-done | bytes 131104 | tf_op jit(solution)/shard_map/ppermute | solution.py:306
  33.7 1.0 %collective-permute-done.5.refs_3_ = bf16[4,128,128]{2,1,0:T(8,128)(2,1)S(1)} collective-permute-done((bf16[4,128,128]{2,1,0:T(8,128)(2,1)S(1)}, bf16[4,128,128]{2,1,0:T(8,128)(2,1)S(1)}, u32[]{:S(2)}, u32[]{:S(2)}) %collective-permute-start.5) | collective-permute-done | bytes 131104 | tf_op jit(solution)/shard_map/ppermute | solution.py:306
  35.1 1.2 %collective-permute-start.6 = (bf16[2,128,256]{2,1,0:T(8,128)(2,1)S(1)}, bf16[2,128,256]{2,1,0:T(8,128)(2,1)S(1)}, u32[]{:S(2)}, u32[]{:S(2)}) collective-permute-start(bf16[2,128,256]{2,1,0:T(8,128)(2,1)S(1)} %get-tuple-element.18), channel_id=1, source_target_pairs={{0,1},{1,0},{2,3},{3,2},{4,5},{5,4},{6,7},{7,6},{8,9},{9,8},{10,11... | collective-permute-start | bytes 393224 | tf_op jit(solution)/shard_map/ppermute | solution.py:306
  36.3 2.2 %collective-permute-start.7 = (bf16[2,128,256]{2,1,0:T(8,128)(2,1)S(1)}, bf16[2,128,256]{2,1,0:T(8,128)(2,1)S(1)}, u32[]{:S(2)}, u32[]{:S(2)}) collective-permute-start(bf16[2,128,256]{2,1,0:T(8,128)(2,1)S(1)} %get-tuple-element.19), channel_id=1, source_target_pairs={{1,2},{3,4},{5,6},{2,1},{4,3},{6,5},{9,10},{11,12},{13,14},{10,9},... | collective-permute-start | bytes 393224 | tf_op jit(solution)/shard_map/ppermute | solution.py:394
  39.3 3.6 %collective-permute-done.7.odd_in = bf16[2,128,256]{2,1,0:T(8,128)(2,1)S(1)} collective-permute-done((bf16[2,128,256]{2,1,0:T(8,128)(2,1)S(1)}, bf16[2,128,256]{2,1,0:T(8,128)(2,1)S(1)}, u32[]{:S(2)}, u32[]{:S(2)}) %collective-permute-start.7) | collective-permute-done | bytes 131104 | tf_op jit(solution)/shard_map/ppermute | solution.py:394
  42.9 1.3 %shard_map.67 = (bf16[3,48,256]{2,1,0:T(8,128)(2,1)S(1)}, bf16[3,48,256]{2,1,0:T(8,128)(2,1)S(1)}, bf16[3,48,256]{2,1,0:T(8,128)(2,1)S(1)}, bf16[3,48,256]{2,1,0:T(8,128)(2,1)S(1)}, bf16[4,48,256]{2,1,0:T(8,128)(2,1)S(1)}) custom-call(f32[4,128,256]{2,1,0:T(8,128)S(1)} %get-tuple-element.17.own, bf16[2,128,256]{2,1,0:T(8,128)(2,1)S(1)} %collective-permute-done.6.even_in, ...), custom_call_target="tpu_custom_call" | custom-call | flops 905969664 | bytes 5000000 | tf_op jit(solution)/shard_map/pallas_call | solution.py:16
  44.2 1.1 %collective-permute-start.11 = (bf16[3,48,256]{2,1,0:T(8,128)(2,1)S(1)}, bf16[3,48,256]{2,1,0:T(8,128)(2,1)S(1)}, u32[]{:S(2)}, u32[]{:S(2)}) collective-permute-start(bf16[3,48,256]{2,1,0:T(8,128)(2,1)S(1)} %get-tuple-element.21), channel_id=1, source_target_pairs={{0,8},{8,0},{16,24},{24,16},{1,9},{9,1},{17,25},{25,17},{2,10},{10... | collective-permute-start | bytes 221192 | tf_op jit(solution)/shard_map/ppermute | solution.py:306
  45.9 1.0 %collective-permute-start.13 = (bf16[3,48,256]{2,1,0:T(8,128)(2,1)S(1)}, bf16[3,48,256]{2,1,0:T(8,128)(2,1)S(1)}, u32[]{:S(2)}, u32[]{:S(2)}) collective-permute-start(bf16[3,48,256]{2,1,0:T(8,128)(2,1)S(1)} %get-tuple-element.23), channel_id=1, source_target_pairs={{0,24},{8,16},{16,8},{24,0},{1,25},{9,17},{17,9},{25,1},{2,26},{10... | collective-permute-start | bytes 221192 | tf_op jit(solution)/shard_map/ppermute | solution.py:306
  47.5 1.1 %collective-permute-done.12.refs_2_ = bf16[3,48,256]{2,1,0:T(8,128)(2,1)S(1)} collective-permute-done((bf16[3,48,256]{2,1,0:T(8,128)(2,1)S(1)}, bf16[3,48,256]{2,1,0:T(8,128)(2,1)S(1)}, u32[]{:S(2)}, u32[]{:S(2)}) %collective-permute-start.12) | collective-permute-done | bytes 73760 | tf_op jit(solution)/shard_map/ppermute | solution.py:306
  48.6 1.5 %collective-permute-done.13.refs_3_ = bf16[3,48,256]{2,1,0:T(8,128)(2,1)S(1)} collective-permute-done((bf16[3,48,256]{2,1,0:T(8,128)(2,1)S(1)}, bf16[3,48,256]{2,1,0:T(8,128)(2,1)S(1)}, u32[]{:S(2)}, u32[]{:S(2)}) %collective-permute-start.13) | collective-permute-done | bytes 73760 | tf_op jit(solution)/shard_map/ppermute | solution.py:306
  50.0 1.9 %shard_map.69 = bf16[8,16,8,128]{3,2,1,0:T(8,128)(2,1)} custom-call(bf16[3,48,256]{2,1,0:T(8,128)(2,1)S(1)} %get-tuple-element.20.refs_0_, bf16[3,48,256]{2,1,0:T(8,128)(2,1)S(1)} %collective-permute-done.11.refs_1_, bf16[3,48,256]{2,1,0:T(8,128)(2,1)S(1)} %collective-permute-done.12.refs_2_, bf16[3,48,256]{2,1,0:T(8,128)(2,1)S(1)} %collective-permute-done.13.refs_3_, ...), custom_call_target="tpu_custom_call" | custom-call | flops 503316480 | bytes 3000000 | tf_op jit(solution)/shard_map/pallas_call | solution.py:16
  (39 shorter events, 3.9 us)
Async XLA Ops:
  0.0 4.3 %copy-start = (bf16[3,3,3,256,32]{3,4,2,1,0:T(8,128)(2,1)S(1)}, bf16[3,3,3,256,32]{3,4,2,1,0:T(8,128)(2,1)}, u32[]{:S(2)}) copy-start(bf16[3,3,3,256,32]{3,4,2,1,0:T(8,128)(2,1)} %param.8) | copy-start | bytes 1327108
  0.9 9.6 %copy-start.2 = (bf16[512,256]{1,0:T(8,128)(2,1)S(1)}, bf16[512,256]{1,0:T(8,128)(2,1)}, u32[]{:S(2)}) copy-start(bf16[512,256]{1,0:T(8,128)(2,1)} %refs_5_.1) | copy-start | bytes 786436
  0.9 21.1 %collective-permute-start = (bf16[4,2,8,512]{3,2,1,0:T(8,128)(2,1)S(1)}, bf16[4,2,8,512]{3,2,1,0:T(8,128)(2,1)S(1)}, u32[]{:S(2)}, u32[]{:S(2)}) collective-permute-start(bf16[4,2,8,512]{3,2,1,0:T(8,128)(2,1)S(1)} %bitcast.33), channel_id=1, source_target_pairs={{0,8},{8,0},{16,24},{24,16},{1,9},{9,1},{17,25},{25,17},{2,10},{10... | collective-permute-start | bytes 196616 | tf_op jit(solution)/shard_map/ppermute | solution.py:306
  3.0 19.0 %collective-permute-start.1 = (bf16[4,2,8,512]{3,2,1,0:T(8,128)(2,1)S(1)}, bf16[4,2,8,512]{3,2,1,0:T(8,128)(2,1)S(1)}, u32[]{:S(2)}, u32[]{:S(2)}) collective-permute-start(bf16[4,2,8,512]{3,2,1,0:T(8,128)(2,1)S(1)} %bitcast.34), channel_id=1, source_target_pairs={{0,16},{8,24},{16,0},{24,8},{1,17},{9,25},{17,1},{25,9},{2,18},{10... | collective-permute-start | bytes 196616 | tf_op jit(solution)/shard_map/ppermute | solution.py:306
  4.3 17.7 %collective-permute-start.2 = (bf16[4,2,8,512]{3,2,1,0:T(8,128)(2,1)S(1)}, bf16[4,2,8,512]{3,2,1,0:T(8,128)(2,1)S(1)}, u32[]{:S(2)}, u32[]{:S(2)}) collective-permute-start(bf16[4,2,8,512]{3,2,1,0:T(8,128)(2,1)S(1)} %bitcast.35), channel_id=1, source_target_pairs={{0,24},{8,16},{16,8},{24,0},{1,25},{9,17},{17,9},{25,1},{2,26},{10... | collective-permute-start | bytes 196616 | tf_op jit(solution)/shard_map/ppermute | solution.py:306
  4.3 3.7 %collective-permute-start.8 = (bf16[1,3,3,3,8,256]{5,4,3,2,1,0:T(8,128)(2,1)S(1)}, bf16[1,3,3,3,8,256]{5,4,3,2,1,0:T(8,128)(2,1)S(1)}, u32[]{:S(2)}, u32[]{:S(2)}) collective-permute-start(bf16[1,3,3,3,8,256]{5,4,3,2,1,0:T(8,128)(2,1)S(1)} %dynamic-slice_bitcast_fusion), channel_id=1, source_target_pairs={{0,2},{1,3},{2,0},{3,1},{4,6},{5,7},{6,4},{7,5},{8,10},{9,11},{10,... | collective-permute-start | bytes 331784 | tf_op jit(solution)/shard_map/ppermute | solution.py:306
  8.0 12.0 %collective-permute-start.9 = (bf16[2,3,3,3,8,256]{5,4,3,2,1,0:T(8,128)(2,1)S(1)}, bf16[2,3,3,3,8,256]{5,4,3,2,1,0:T(8,128)(2,1)S(1)}, u32[]{:S(2)}, u32[]{:S(2)}) collective-permute-start(bf16[2,3,3,3,8,256]{5,4,3,2,1,0:T(8,128)(2,1)S(1)} %pad_maximum_fusion.2), channel_id=1, source_target_pairs={{0,4},{1,5},{2,6},{3,7},{4,0},{5,1},{6,2},{7,3},{8,12},{9,13},{10,... | collective-permute-start | bytes 663560 | tf_op jit(solution)/shard_map/ppermute | solution.py:306
  20.1 18.4 %collective-permute-start.10 = (bf16[4,3,3,3,8,256]{5,4,3,2,1,0:T(8,128)(2,1)S(1)}, bf16[4,3,3,3,8,256]{5,4,3,2,1,0:T(8,128)(2,1)S(1)}, u32[]{:S(2)}, u32[]{:S(2)}) collective-permute-start(bf16[4,3,3,3,8,256]{5,4,3,2,1,0:T(8,128)(2,1)S(1)} %pad_maximum_fusion.1), channel_id=1, source_target_pairs={{0,1},{1,0},{2,3},{3,2},{4,5},{5,4},{6,7},{7,6},{8,9},{9,8},{10,11... | collective-permute-start | bytes 1327112 | tf_op jit(solution)/shard_map/ppermute | solution.py:306
  22.0 2.0 %copy-start.1 = (bf16[3,3,3,512,128]{4,3,2,1,0:T(8,128)(2,1)S(1)}, bf16[3,3,3,512,128]{4,3,2,1,0:T(8,128)(2,1)}, u32[]{:S(2)}) copy-start(bf16[3,3,3,512,128]{4,3,2,1,0:T(8,128)(2,1)} %refs_4_.1) | copy-start | bytes 10616836
  25.8 5.2 %collective-permute-start.3 = (bf16[4,128,128]{2,1,0:T(8,128)(2,1)S(1)}, bf16[4,128,128]{2,1,0:T(8,128)(2,1)S(1)}, u32[]{:S(2)}, u32[]{:S(2)}) collective-permute-start(bf16[4,128,128]{2,1,0:T(8,128)(2,1)S(1)} %get-tuple-element.15.refs_0_), channel_id=1, source_target_pairs={{0,8},{8,0},{16,24},{24,16},{1,9},{9,1},{17,25},{25,17},{2,10},{10... | collective-permute-start | bytes 393224 | tf_op jit(solution)/shard_map/ppermute | solution.py:306
  27.1 6.6 %collective-permute-start.4 = (bf16[4,128,128]{2,1,0:T(8,128)(2,1)S(1)}, bf16[4,128,128]{2,1,0:T(8,128)(2,1)S(1)}, u32[]{:S(2)}, u32[]{:S(2)}) collective-permute-start(bf16[4,128,128]{2,1,0:T(8,128)(2,1)S(1)} %get-tuple-element.15.refs_0_), channel_id=1, source_target_pairs={{0,16},{8,24},{16,0},{24,8},{1,17},{9,25},{17,1},{25,9},{2,18},{10... | collective-permute-start | bytes 393224 | tf_op jit(solution)/shard_map/ppermute | solution.py:306
  28.5 6.2 %collective-permute-start.5 = (bf16[4,128,128]{2,1,0:T(8,128)(2,1)S(1)}, bf16[4,128,128]{2,1,0:T(8,128)(2,1)S(1)}, u32[]{:S(2)}, u32[]{:S(2)}) collective-permute-start(bf16[4,128,128]{2,1,0:T(8,128)(2,1)S(1)} %get-tuple-element.15.refs_0_), channel_id=1, source_target_pairs={{0,24},{8,16},{16,8},{24,0},{1,25},{9,17},{17,9},{25,1},{2,26},{10... | collective-permute-start | bytes 393224 | tf_op jit(solution)/shard_map/ppermute | solution.py:306
  35.1 4.2 %collective-permute-start.6 = (bf16[2,128,256]{2,1,0:T(8,128)(2,1)S(1)}, bf16[2,128,256]{2,1,0:T(8,128)(2,1)S(1)}, u32[]{:S(2)}, u32[]{:S(2)}) collective-permute-start(bf16[2,128,256]{2,1,0:T(8,128)(2,1)S(1)} %get-tuple-element.18), channel_id=1, source_target_pairs={{0,1},{1,0},{2,3},{3,2},{4,5},{5,4},{6,7},{7,6},{8,9},{9,8},{10,11... | collective-permute-start | bytes 393224 | tf_op jit(solution)/shard_map/ppermute | solution.py:306
  36.3 6.6 %collective-permute-start.7 = (bf16[2,128,256]{2,1,0:T(8,128)(2,1)S(1)}, bf16[2,128,256]{2,1,0:T(8,128)(2,1)S(1)}, u32[]{:S(2)}, u32[]{:S(2)}) collective-permute-start(bf16[2,128,256]{2,1,0:T(8,128)(2,1)S(1)} %get-tuple-element.19), channel_id=1, source_target_pairs={{1,2},{3,4},{5,6},{2,1},{4,3},{6,5},{9,10},{11,12},{13,14},{10,9},... | collective-permute-start | bytes 393224 | tf_op jit(solution)/shard_map/ppermute | solution.py:394
  42.9 4.1 %copy-start.3 = (bf16[3,3,3,128,128]{4,3,2,1,0:T(8,128)(2,1)S(1)}, bf16[3,3,3,128,128]{4,3,2,1,0:T(8,128)(2,1)}, u32[]{:S(2)}) copy-start(bf16[3,3,3,128,128]{4,3,2,1,0:T(8,128)(2,1)} %filters.1) | copy-start | bytes 2654212
  44.2 3.3 %collective-permute-start.11 = (bf16[3,48,256]{2,1,0:T(8,128)(2,1)S(1)}, bf16[3,48,256]{2,1,0:T(8,128)(2,1)S(1)}, u32[]{:S(2)}, u32[]{:S(2)}) collective-permute-start(bf16[3,48,256]{2,1,0:T(8,128)(2,1)S(1)} %get-tuple-element.21), channel_id=1, source_target_pairs={{0,8},{8,0},{16,24},{24,16},{1,9},{9,1},{17,25},{25,17},{2,10},{10... | collective-permute-start | bytes 221192 | tf_op jit(solution)/shard_map/ppermute | solution.py:306
  45.4 3.2 %collective-permute-start.12 = (bf16[3,48,256]{2,1,0:T(8,128)(2,1)S(1)}, bf16[3,48,256]{2,1,0:T(8,128)(2,1)S(1)}, u32[]{:S(2)}, u32[]{:S(2)}) collective-permute-start(bf16[3,48,256]{2,1,0:T(8,128)(2,1)S(1)} %get-tuple-element.22), channel_id=1, source_target_pairs={{0,16},{8,24},{16,0},{24,8},{1,17},{9,25},{17,1},{25,9},{2,18},{10... | collective-permute-start | bytes 221192 | tf_op jit(solution)/shard_map/ppermute | solution.py:306
  45.9 4.1 %collective-permute-start.13 = (bf16[3,48,256]{2,1,0:T(8,128)(2,1)S(1)}, bf16[3,48,256]{2,1,0:T(8,128)(2,1)S(1)}, u32[]{:S(2)}, u32[]{:S(2)}) collective-permute-start(bf16[3,48,256]{2,1,0:T(8,128)(2,1)S(1)} %get-tuple-element.23), channel_id=1, source_target_pairs={{0,24},{8,16},{16,8},{24,0},{1,25},{9,17},{17,9},{25,1},{2,26},{10... | collective-permute-start | bytes 221192 | tf_op jit(solution)/shard_map/ppermute | solution.py:306
  47.0 3.1 %copy-start.4 = (bf16[256,128]{1,0:T(8,128)(2,1)S(1)}, bf16[256,128]{1,0:T(8,128)(2,1)}, u32[]{:S(2)}) copy-start(bf16[256,128]{1,0:T(8,128)(2,1)} %refs_6_.1) | copy-start | bytes 196612

commit v2 on v1

--- a/solution.py
+++ b/solution.py
@@ -8,15 +8,20 @@
 from jax.sharding import PartitionSpec as P
 
 VMEM = pl.BlockSpec(memory_space=pltpu.VMEM)
+FAR = pl.BlockSpec(memory_space=pltpu.HBM)
 F32 = jnp.float32
 BF16 = jnp.bfloat16
 
 
-def call(kernel, outs, scratch, flops, nbytes, *args):
+def call(kernel, outs, scratch, flops, nbytes, *args, stay=()):
+    args = [
+        pltpu.with_memory_space_constraint(arg, pltpu.HBM) if n in stay else arg
+        for n, arg in enumerate(args)
+    ]
     return pl.pallas_call(
         kernel,
         out_shape=outs,
-        in_specs=[VMEM] * len(args),
+        in_specs=[FAR if n in stay else VMEM for n in range(len(args))],
         out_specs=jax.tree.map(lambda _: VMEM, outs),
         scratch_shapes=scratch,
         compiler_params=pltpu.CompilerParams(vmem_limit_bytes=40 << 20),
@@ -42,7 +47,7 @@
 
 
 def coarse_kernel(groups, *refs):
-    pieces, (filters, proj, part, straight, shifted) = refs[:groups], refs[groups:]
+    pieces, (filters, part, shifted) = refs[:groups], refs[groups:]
     rows, cols, frames, depth = pieces[0].shape
     width = filters.shape[4]
     height = groups * rows
@@ -54,10 +59,6 @@
     for k in range(groups):
         at = (me ^ k) * rows
         raw = pieces[k][...]
-        flat = raw.reshape(rows * cols * frames, depth)
-        direct = dot(flat, proj[...]).reshape(rows, cols, frames, proj.shape[1])
-        for col in range(cols):
-            straight[col, pl.ds(at, rows)] = direct[:, col]
         act = activate(raw.astype(F32))
         for step in range(3):
             moved = delayed(act, 2 - step).reshape(rows, cols * frames, depth)
@@ -83,13 +84,26 @@
         part[out] = value.reshape(height * frames, width).astype(BF16)
 
 
+def straight_kernel(groups, *refs):
+    pieces, (proj, straight) = refs[:groups], refs[groups:]
+    rows, cols, frames, depth = pieces[0].shape
+    me = lax.axis_index("grp")
+    for k in range(groups):
+        flat = pieces[k][...].reshape(rows * cols * frames, depth)
+        direct = dot(flat, proj[...]).reshape(rows, cols, frames, proj.shape[1])
+        for col in range(cols):
+            straight[col, pl.ds((me ^ k) * rows, rows)] = direct[:, col]
+
+
 def project_kernel(groups, *refs):
     parts, (proj, straight, own, even_out, odd_out) = refs[:groups], refs[groups:]
     extent, cells, width = parts[0].shape
-    outputs = proj.shape[2]
+    outputs = proj.shape[1]
+    me = lax.axis_index("grp")
     total = None
     for k in range(groups):
-        term = dot(parts[k][...].reshape(extent * cells, width), proj[k])
+        weights = proj[pl.ds(pl.multiple_of((me ^ k) * width, width), width)]
+        term = dot(parts[k][...].reshape(extent * cells, width), weights)
         total = term if total is None else total + term
     total = total.reshape(extent, cells, outputs)
     cols = extent - 2
@@ -273,7 +287,19 @@
     lax.fori_loop(0, 3, per_step, 0)
 
 
-def fold_fine_kernel(filters, out):
+def pick_kernel(groups, stored, out, filters, arrived):
+    copy = pltpu.make_async_copy(stored, filters, arrived)
+    copy.start()
+    me = lax.axis_index("grp")
+    share = out.shape[3]
+    copy.wait()
+    value = filters[:, :, :, 0:share].astype(F32)
+    for k in range(1, groups):
+        value = jnp.where(me == k, filters[:, :, :, k * share : (k + 1) * share].astype(F32), value)
+    out[...] = value.astype(BF16)
+
+
+def prepare_kernel(groups, parts, filters, proj, folded, spread, plain):
     def per_step(step, carry):
         taps = [[filters[step, r, c].astype(F32) for c in range(3)] for r in range(3)]
         for p in range(2):
@@ -284,21 +310,30 @@
                     line = [x + y for x, y in zip(taps[0], taps[1])] if near == 0 else taps[2]
                 first = jnp.concatenate([line[0] + line[1], line[0]], axis=1)
                 second = jnp.concatenate([line[2], line[1] + line[2]], axis=1)
-                out[step, p, near] = jnp.concatenate([first, second], axis=0).astype(BF16)
+                folded[step, p, near] = jnp.concatenate([first, second], axis=0).astype(BF16)
         return carry
 
     lax.fori_loop(0, 3, per_step, 0)
-
-
-def reorder(values, index):
-    size, rest = values.shape[0], values.shape[1:]
-    bit = 1
-    while bit < size:
-        pairs = values.reshape(size // (2 * bit), 2, bit, *rest)
-        pairs = jnp.where((index & bit) != 0, pairs[:, ::-1], pairs)
-        values = pairs.reshape(size, *rest)
-        bit *= 2
-    return values
+    depth, width = proj.shape
+    plain[...] = proj[...].astype(F32)
+    me, tile = lax.axis_index("grp"), lax.axis_index("tile")
+    share = depth // (groups * parts)
+    spread[...] = jnp.zeros(spread.shape, BF16)
+    for k in range(groups):
+        lines = []
+        for s in range(parts):
+            if parts == 1:
+                first = (me ^ k) * share
+            else:
+                source = tile ^ (s // (parts // 2)) ^ (2 * (s % (parts // 2)))
+                first = (source * groups + (me ^ k)) * share
+            lines.append(plain[pl.ds(pl.multiple_of(first, 8), share)])
+        block = jnp.concatenate(lines, axis=0).astype(BF16)
+        height = parts * share
+        for phase in range(4):
+            spread[
+                k, phase * height : (phase + 1) * height, phase * width : (phase + 1) * width
+            ] = block
 
 
 def exchange(values, axis, k):
@@ -316,62 +351,46 @@
     cells = height * frames
     own_mid = mid_filters.shape[4]
 
-    first = jnp.transpose(latent, (1, 2, 0, 3))
-    pieces = [first] + [exchange(first, "grp", k) for k in range(1, groups)]
+    divided = own_mid % groups == 0 and (own_mid // groups) % 8 == 0
+    share, shares = (own_mid // groups, tiles) if divided else (depth1 // groups, 1)
+    lanes = 4 * shares * share
+    arrived = [exchange(latent, "grp", k) for k in range(1, groups)]
+    arrived = lax.optimization_barrier(arrived)
+    pieces = [jnp.transpose(piece, (1, 2, 0, 3)) for piece in [latent] + arrived]
 
     mid_rows = jnp.transpose(mid_filters, (0, 1, 2, 4, 3))
-    if own_mid % groups == 0 and (own_mid // groups) % 8 == 0:
-        share = own_mid // groups
-        mine = lax.dynamic_slice_in_dim(mid_rows, me * share, share, axis=3)[None]
-        bit = 2
-        while bit < tiles:
-            mine = jnp.concatenate([mine, exchange(mine, "tile", bit)])
-            bit *= 2
-        mine = jnp.concatenate([mine, exchange(mine, "tile", 1)])
-        table = mid_proj.reshape(tiles // 2, 2, groups, share, depth2).transpose(1, 0, 2, 3, 4)
-        table = reorder(table, tile & 1)
-        table = jnp.swapaxes(reorder(jnp.swapaxes(table, 0, 1), tile >> 1), 0, 1)
-        table = table.transpose(2, 0, 1, 3, 4).reshape(groups, tiles * share, depth2)
+    if divided:
+        mine = call(
+            functools.partial(pick_kernel, groups),
+            jax.ShapeDtypeStruct((3, 3, 3, share, depth1), BF16),
+            [pltpu.VMEM(mid_rows.shape, BF16), pltpu.SemaphoreType.DMA],
+            6 * 10**9,
+            10**6,
+            mid_rows,
+            stay=(0,),
+        )
+        mine = [mine] + [exchange(mine, "tile", k) for k in range(2, tiles, 2)]
+        mine = jnp.stack(mine)
     else:
-        share = depth1 // groups
         every = lax.all_gather(mid_rows, "tile", axis=3, tiled=True)
         mine = lax.dynamic_slice_in_dim(every, me * share, share, axis=3)[None]
-        table = mid_proj.reshape(groups, share, depth2)
-    lanes = 4 * mine.shape[0] * mine.shape[4]
-    table = reorder(table, me)
-    spread = (
-        jnp.eye(4, dtype=BF16)[None, :, None, :, None] * table[:, None, :, None, :]
-    ).reshape(groups, lanes, 4 * depth2)
-    proj = reorder(coarse_proj.reshape(groups, width0, depth1), me)
-
-    fine_folded = call(
-        fold_fine_kernel,
-        jax.ShapeDtypeStruct((3, 2, 2, 2 * depth2, 2 * depth2), BF16),
-        [],
-        10**6,
-        4 * 10**6,
-        fine_filters,
-    )
-    mid_folded = call(
-        fold_middle_kernel,
-        jax.ShapeDtypeStruct((3, 3, 2, depth1, lanes), BF16),
-        [],
-        10**6,
-        4 * 10**6,
-        mine,
-    )
-
-    part, straight = call(
+
+    part = call(
         functools.partial(coarse_kernel, groups),
-        (
-            jax.ShapeDtypeStruct((cols + 2, cells, width0), BF16),
-            jax.ShapeDtypeStruct((cols, height, frames, depth1), F32),
-        ),
+        jax.ShapeDtypeStruct((cols + 2, cells, width0), BF16),
         [pltpu.VMEM((3, height + 2, cols * frames, depth0), BF16)],
         2 * 27 * cells * cols * depth0 * width0,
         5 * 10**6,
         *pieces,
         coarse_filters,
+    )
+    straight = call(
+        functools.partial(straight_kernel, groups),
+        jax.ShapeDtypeStruct((cols, height, frames, depth1), F32),
+        [],
+        2 * cells * cols * depth0 * depth1,
+        10**6,
+        *pieces,
         coarse_proj,
     )
     parts = [part] + [exchange(part, "grp", k) for k in range(1, groups)]
@@ -386,8 +405,19 @@
         2 * cells * (cols + 2) * depth0 * depth1,
         2 * 10**6,
         *parts,
-        proj,
+        coarse_proj,
         straight,
+    )
+    if divided:
+        later, _ = lax.optimization_barrier((mine, own))
+        mine = jnp.concatenate([mine, exchange(later, "tile", 1)])
+    mid_folded = call(
+        fold_middle_kernel,
+        jax.ShapeDtypeStruct((3, 3, 2, depth1, lanes), BF16),
+        [],
+        10**6,
+        4 * 10**6,
+        mine,
     )
     odd_pairs = [(i, i + 1) for i in range(1, tiles - 1, 2)]
     even_in = exchange(even_out, "tile", 1)
@@ -411,6 +441,18 @@
         mid_folded,
     )
     chunks = [chunks[0]] + [exchange(chunks[k], "grp", k) for k in range(1, groups)]
+    fine_folded, spread = call(
+        functools.partial(prepare_kernel, groups, shares),
+        (
+            jax.ShapeDtypeStruct((3, 2, 2, 2 * depth2, 2 * depth2), BF16),
+            jax.ShapeDtypeStruct((groups, lanes, 4 * depth2), BF16),
+        ),
+        [pltpu.VMEM((depth1, depth2), F32)],
+        10**6,
+        4 * 10**6,
+        fine_filters,
+        mid_proj,
+    )
     tall, broad = 2 * rows, 2 * cols
     return call(
         functools.partial(fine_kernel, groups, frames),

time: 52.2 us -> 39.4 us (0.75)
  the two profiles are of different devices: /device:TPU:1 before, /device:TPU:8 now
where the time goes in v2:
time: 39.4 us; the launch traced here: 39.2 us
  starting transfers between devices  18.6 us (47%)
  waiting for transfers between devices  11.4 us (29%)
  Pallas kernels  7.97 us (20%)
  local copies, waits for them, and re-layouts  0.95 us (2%)
    ppermute x14, starting transfers between devices, exchange(): return lax.ppermute(values, axis, [(i, i ^ k) for i in range(size)])  16.4 us
    ppermute x14, waiting for transfers between devices, exchange(): return lax.ppermute(values, axis, [(i, i ^ k) for i in range(size)])  8.12 us
    pallas_call x8, Pallas kernels, call(): pl.pallas_call(kernel, out_shape=outs, in_specs=[FAR if n in stay else VM...  7.97 us
    ppermute x1, waiting for transfers between devices, body(): lax.ppermute(odd_out, 'tile', odd_pairs + [(j, i) for i, j in odd_pairs])  3.33 us
    ppermute x1, starting transfers between devices, body(): lax.ppermute(odd_out, 'tile', odd_pairs + [(j, i) for i, j in odd_pairs])  2.16 us
    unnamed x13, local copies, waits for them, and re-layouts  0.92 us
  transfers between devices with their start and end apart: 15, of which 8 were waited for; matrix products, arithmetic and copies ran while one was open for 0% of the time, Pallas kernels for 11%

profile of v2, /device:TPU:8, one launch (start us, length us, event | category | flops | bytes accessed | tf_op | source)
XLA Modules:
  0.0 39.2 jit_solution(11392183011652384722)
XLA Ops:
  0.0 0.9 %copy.13 = bf16[8,4,2,512]{3,0,2,1:T(8,128)(2,1)S(1)} copy(bf16[8,4,2,512]{3,2,1,0:T(2,128)(2,1)} %param.6) | data formatting | bytes 131072 | tf_op args[0]
  0.9 1.6 %collective-permute-start = (bf16[8,4,2,512]{3,0,2,1:T(8,128)(2,1)S(1)}, bf16[8,4,2,512]{3,0,2,1:T(8,128)(2,1)S(1)}, u32[]{:S(2)}, u32[]{:S(2)}) collective-permute-start(bf16[8,4,2,512]{3,0,2,1:T(8,128)(2,1)S(1)} %copy.13), channel_id=1, source_target_pairs={{0,8},{8,0},{16,24},{24,16},{1,9},{9,1},{17,25},{25,17},{2,10},{10... | collective-permute-start | bytes 196616 | tf_op jit(solution)/shard_map/ppermute | solution.py:341
  2.4 1.5 %collective-permute-start.2 = (bf16[8,4,2,512]{3,0,2,1:T(8,128)(2,1)S(1)}, bf16[8,4,2,512]{3,0,2,1:T(8,128)(2,1)S(1)}, u32[]{:S(2)}, u32[]{:S(2)}) collective-permute-start(bf16[8,4,2,512]{3,0,2,1:T(8,128)(2,1)S(1)} %copy.13), channel_id=1, source_target_pairs={{0,24},{8,16},{16,8},{24,0},{1,25},{9,17},{17,9},{25,1},{2,26},{10... | collective-permute-start | bytes 196616 | tf_op jit(solution)/shard_map/ppermute | solution.py:341
  3.9 0.5 %collective-permute-start.1 = (bf16[8,4,2,512]{3,0,2,1:T(8,128)(2,1)S(1)}, bf16[8,4,2,512]{3,0,2,1:T(8,128)(2,1)S(1)}, u32[]{:S(2)}, u32[]{:S(2)}) collective-permute-start(bf16[8,4,2,512]{3,0,2,1:T(8,128)(2,1)S(1)} %copy.13), channel_id=1, source_target_pairs={{0,16},{8,24},{16,0},{24,8},{1,17},{9,25},{17,1},{25,9},{2,18},{10... | collective-permute-start | bytes 196616 | tf_op jit(solution)/shard_map/ppermute | solution.py:341
  4.4 1.2 %shard_map.67 = bf16[3,3,3,8,256]{4,3,2,1,0:T(8,128)(2,1)S(1)} custom-call(bf16[3,3,3,32,256]{4,3,2,1,0:T(8,128)(2,1)} %bitcast.26), custom_call_target="tpu_custom_call" | custom-call | flops 6000000000 | bytes 1000000 | tf_op jit(solution)/shard_map/pallas_call | solution.py:21
  5.7 1.6 %collective-permute-start.10 = (bf16[3,3,3,8,256]{4,3,2,1,0:T(8,128)(2,1)S(1)}, bf16[3,3,3,8,256]{4,3,2,1,0:T(8,128)(2,1)S(1)}, u32[]{:S(2)}, u32[]{:S(2)}) collective-permute-start(bf16[3,3,3,8,256]{4,3,2,1,0:T(8,128)(2,1)S(1)} %shard_map.67), channel_id=1, source_target_pairs={{0,6},{1,7},{2,4},{3,5},{4,2},{5,3},{6,0},{7,1},{8,14},{9,15},{10,... | collective-permute-start | bytes 331784 | tf_op jit(solution)/shard_map/ppermute | solution.py:341
  7.3 2.5 %collective-permute-start.8 = (bf16[3,3,3,8,256]{4,3,2,1,0:T(8,128)(2,1)S(1)}, bf16[3,3,3,8,256]{4,3,2,1,0:T(8,128)(2,1)S(1)}, u32[]{:S(2)}, u32[]{:S(2)}) collective-permute-start(bf16[3,3,3,8,256]{4,3,2,1,0:T(8,128)(2,1)S(1)} %shard_map.67), channel_id=1, source_target_pairs={{0,2},{1,3},{2,0},{3,1},{4,6},{5,7},{6,4},{7,5},{8,10},{9,11},{10,... | collective-permute-start | bytes 331784 | tf_op jit(solution)/shard_map/ppermute | solution.py:341
  9.9 1.7 %shard_map.64.refs_0_ = bf16[4,128,128]{2,1,0:T(8,128)(2,1)S(1)} custom-call(bf16[4,2,8,512]{3,2,1,0:T(8,128)(2,1)S(1)} %bitcast.14, bf16[4,2,8,512]{3,2,1,0:T(8,128)(2,1)S(1)} %bitcast.17, bf16[4,2,8,512]{3,2,1,0:T(8,128)(2,1)S(1)} %bitcast.21, bf16[4,2,8,512]{3,2,1,0:T(8,128)(2,1)S(1)} %bitcast.19, bf16[3,3,3,512,128]{4,3,2,1,0:T(8,128)(2,1)S(1)} %copy-done), custom_call_target="tpu_custom_call" | custom-call | flops 905969664 | bytes 5000000 | tf_op jit(solution)/shard_map/pallas_call | solution.py:21
  11.6 2.5 %collective-permute-start.5 = (bf16[4,128,128]{2,1,0:T(8,128)(2,1)S(1)}, bf16[4,128,128]{2,1,0:T(8,128)(2,1)S(1)}, u32[]{:S(2)}, u32[]{:S(2)}) collective-permute-start(bf16[4,128,128]{2,1,0:T(8,128)(2,1)S(1)} %shard_map.64.refs_0_), channel_id=1, source_target_pairs={{0,24},{8,16},{16,8},{24,0},{1,25},{9,17},{17,9},{25,1},{2,26},{10... | collective-permute-start | bytes 393224 | tf_op jit(solution)/shard_map/ppermute | solution.py:341
  14.2 0.5 %collective-permute-start.4 = (bf16[4,128,128]{2,1,0:T(8,128)(2,1)S(1)}, bf16[4,128,128]{2,1,0:T(8,128)(2,1)S(1)}, u32[]{:S(2)}, u32[]{:S(2)}) collective-permute-start(bf16[4,128,128]{2,1,0:T(8,128)(2,1)S(1)} %shard_map.64.refs_0_), channel_id=1, source_target_pairs={{0,16},{8,24},{16,0},{24,8},{1,17},{9,25},{17,1},{25,9},{2,18},{10... | collective-permute-start | bytes 393224 | tf_op jit(solution)/shard_map/ppermute | solution.py:341
  15.3 1.5 %collective-permute-start.3 = (bf16[4,128,128]{2,1,0:T(8,128)(2,1)S(1)}, bf16[4,128,128]{2,1,0:T(8,128)(2,1)S(1)}, u32[]{:S(2)}, u32[]{:S(2)}) collective-permute-start(bf16[4,128,128]{2,1,0:T(8,128)(2,1)S(1)} %shard_map.64.refs_0_), channel_id=1, source_target_pairs={{0,8},{8,0},{16,24},{24,16},{1,9},{9,1},{17,25},{25,17},{2,10},{10... | collective-permute-start | bytes 393224 | tf_op jit(solution)/shard_map/ppermute | solution.py:341
  16.9 1.8 %collective-permute-done.5.refs_3_ = bf16[4,128,128]{2,1,0:T(8,128)(2,1)S(1)} collective-permute-done((bf16[4,128,128]{2,1,0:T(8,128)(2,1)S(1)}, bf16[4,128,128]{2,1,0:T(8,128)(2,1)S(1)}, u32[]{:S(2)}, u32[]{:S(2)}) %collective-permute-start.5) | collective-permute-done | bytes 131104 | tf_op jit(solution)/shard_map/ppermute | solution.py:341
  18.7 0.9 %collective-permute-done.4.refs_2_ = bf16[4,128,128]{2,1,0:T(8,128)(2,1)S(1)} collective-permute-done((bf16[4,128,128]{2,1,0:T(8,128)(2,1)S(1)}, bf16[4,128,128]{2,1,0:T(8,128)(2,1)S(1)}, u32[]{:S(2)}, u32[]{:S(2)}) %collective-permute-start.4) | collective-permute-done | bytes 131104 | tf_op jit(solution)/shard_map/ppermute | solution.py:341
  19.6 0.7 %collective-permute-done.3.refs_1_ = bf16[4,128,128]{2,1,0:T(8,128)(2,1)S(1)} collective-permute-done((bf16[4,128,128]{2,1,0:T(8,128)(2,1)S(1)}, bf16[4,128,128]{2,1,0:T(8,128)(2,1)S(1)}, u32[]{:S(2)}, u32[]{:S(2)}) %collective-permute-start.3) | collective-permute-done | bytes 131104 | tf_op jit(solution)/shard_map/ppermute | solution.py:341
  20.8 0.6 %collective-permute-start.6 = (bf16[2,128,256]{2,1,0:T(8,128)(2,1)S(1)}, bf16[2,128,256]{2,1,0:T(8,128)(2,1)S(1)}, u32[]{:S(2)}, u32[]{:S(2)}) collective-permute-start(bf16[2,128,256]{2,1,0:T(8,128)(2,1)S(1)} %get-tuple-element.23), channel_id=1, source_target_pairs={{0,1},{1,0},{2,3},{3,2},{4,5},{5,4},{6,7},{7,6},{8,9},{9,8},{10,11... | collective-permute-start | bytes 393224 | tf_op jit(solution)/shard_map/ppermute | solution.py:341
  21.4 2.2 %collective-permute-start.7 = (bf16[2,128,256]{2,1,0:T(8,128)(2,1)S(1)}, bf16[2,128,256]{2,1,0:T(8,128)(2,1)S(1)}, u32[]{:S(2)}, u32[]{:S(2)}) collective-permute-start(bf16[2,128,256]{2,1,0:T(8,128)(2,1)S(1)} %get-tuple-element.24), channel_id=1, source_target_pairs={{1,2},{3,4},{5,6},{2,1},{4,3},{6,5},{9,10},{11,12},{13,14},{10,9},... | collective-permute-start | bytes 393224 | tf_op jit(solution)/shard_map/ppermute | solution.py:424
  23.6 0.7 %shard_map.68.filters = bf16[3,3,2,256,256]{4,3,2,1,0:T(8,128)(2,1)S(1)} custom-call(bf16[8,3,3,3,8,256]{5,4,3,2,1,0:T(8,128)(2,1)S(1)} %constant_dynamic-update-slice_fusion.pieces), custom_call_target="tpu_custom_call" | custom-call | flops 1000000 | bytes 4000000 | tf_op jit(solution)/shard_map/pallas_call | solution.py:21
  24.3 3.3 %collective-permute-done.7.odd_in = bf16[2,128,256]{2,1,0:T(8,128)(2,1)S(1)} collective-permute-done((bf16[2,128,256]{2,1,0:T(8,128)(2,1)S(1)}, bf16[2,128,256]{2,1,0:T(8,128)(2,1)S(1)}, u32[]{:S(2)}, u32[]{:S(2)}) %collective-permute-start.7) | collective-permute-done | bytes 131104 | tf_op jit(solution)/shard_map/ppermute | solution.py:424
  27.6 1.3 %shard_map.69 = (bf16[3,48,256]{2,1,0:T(8,128)(2,1)S(1)}, bf16[3,48,256]{2,1,0:T(8,128)(2,1)S(1)}, bf16[3,48,256]{2,1,0:T(8,128)(2,1)S(1)}, bf16[3,48,256]{2,1,0:T(8,128)(2,1)S(1)}, bf16[4,48,256]{2,1,0:T(8,128)(2,1)S(1)}) custom-call(f32[4,128,256]{2,1,0:T(8,128)S(1)} %get-tuple-element.22.own, bf16[2,128,256]{2,1,0:T(8,128)(2,1)S(1)} %collective-permute-done.6.even_in, ...), custom_call_target="tpu_custom_call" | custom-call | flops 905969664 | bytes 5000000 | tf_op jit(solution)/shard_map/pallas_call | solution.py:21
  29.0 1.6 %collective-permute-start.12 = (bf16[3,48,256]{2,1,0:T(8,128)(2,1)S(1)}, bf16[3,48,256]{2,1,0:T(8,128)(2,1)S(1)}, u32[]{:S(2)}, u32[]{:S(2)}) collective-permute-start(bf16[3,48,256]{2,1,0:T(8,128)(2,1)S(1)} %get-tuple-element.27), channel_id=1, source_target_pairs={{0,8},{8,0},{16,24},{24,16},{1,9},{9,1},{17,25},{25,17},{2,10},{10... | collective-permute-start | bytes 221192 | tf_op jit(solution)/shard_map/ppermute | solution.py:341
  30.5 1.5 %collective-permute-start.13 = (bf16[3,48,256]{2,1,0:T(8,128)(2,1)S(1)}, bf16[3,48,256]{2,1,0:T(8,128)(2,1)S(1)}, u32[]{:S(2)}, u32[]{:S(2)}) collective-permute-start(bf16[3,48,256]{2,1,0:T(8,128)(2,1)S(1)} %get-tuple-element.28), channel_id=1, source_target_pairs={{0,16},{8,24},{16,0},{24,8},{1,17},{9,25},{17,1},{25,9},{2,18},{10... | collective-permute-start | bytes 221192 | tf_op jit(solution)/shard_map/ppermute | solution.py:341
  33.4 1.5 %collective-permute-done.13.refs_2_ = bf16[3,48,256]{2,1,0:T(8,128)(2,1)S(1)} collective-permute-done((bf16[3,48,256]{2,1,0:T(8,128)(2,1)S(1)}, bf16[3,48,256]{2,1,0:T(8,128)(2,1)S(1)}, u32[]{:S(2)}, u32[]{:S(2)}) %collective-permute-start.13) | collective-permute-done | bytes 73760 | tf_op jit(solution)/shard_map/ppermute | solution.py:341
  34.9 2.4 %collective-permute-done.14.refs_3_ = bf16[3,48,256]{2,1,0:T(8,128)(2,1)S(1)} collective-permute-done((bf16[3,48,256]{2,1,0:T(8,128)(2,1)S(1)}, bf16[3,48,256]{2,1,0:T(8,128)(2,1)S(1)}, u32[]{:S(2)}, u32[]{:S(2)}) %collective-permute-start.14) | collective-permute-done | bytes 73760 | tf_op jit(solution)/shard_map/ppermute | solution.py:341
  37.3 1.9 %shard_map.71 = bf16[8,16,8,128]{3,2,1,0:T(8,128)(2,1)} custom-call(bf16[3,48,256]{2,1,0:T(8,128)(2,1)S(1)} %get-tuple-element.26.refs_0_, bf16[3,48,256]{2,1,0:T(8,128)(2,1)S(1)} %collective-permute-done.12.refs_1_, bf16[3,48,256]{2,1,0:T(8,128)(2,1)S(1)} %collective-permute-done.13.refs_2_, bf16[3,48,256]{2,1,0:T(8,128)(2,1)S(1)} %collective-permute-done.14.refs_3_, ...), custom_call_target="tpu_custom_call" | custom-call | flops 503316480 | bytes 3000000 | tf_op jit(solution)/shard_map/pallas_call | solution.py:21
  (29 shorter events, 2.7 us)
Async XLA Ops:
  0.9 8.9 %collective-permute-start = (bf16[8,4,2,512]{3,0,2,1:T(8,128)(2,1)S(1)}, bf16[8,4,2,512]{3,0,2,1:T(8,128)(2,1)S(1)}, u32[]{:S(2)}, u32[]{:S(2)}) collective-permute-start(bf16[8,4,2,512]{3,0,2,1:T(8,128)(2,1)S(1)} %copy.13), channel_id=1, source_target_pairs={{0,8},{8,0},{16,24},{24,16},{1,9},{9,1},{17,25},{25,17},{2,10},{10... | collective-permute-start | bytes 196616 | tf_op jit(solution)/shard_map/ppermute | solution.py:341
  2.4 7.5 %collective-permute-start.2 = (bf16[8,4,2,512]{3,0,2,1:T(8,128)(2,1)S(1)}, bf16[8,4,2,512]{3,0,2,1:T(8,128)(2,1)S(1)}, u32[]{:S(2)}, u32[]{:S(2)}) collective-permute-start(bf16[8,4,2,512]{3,0,2,1:T(8,128)(2,1)S(1)} %copy.13), channel_id=1, source_target_pairs={{0,24},{8,16},{16,8},{24,0},{1,25},{9,17},{17,9},{25,1},{2,26},{10... | collective-permute-start | bytes 196616 | tf_op jit(solution)/shard_map/ppermute | solution.py:341
  3.9 6.0 %collective-permute-start.1 = (bf16[8,4,2,512]{3,0,2,1:T(8,128)(2,1)S(1)}, bf16[8,4,2,512]{3,0,2,1:T(8,128)(2,1)S(1)}, u32[]{:S(2)}, u32[]{:S(2)}) collective-permute-start(bf16[8,4,2,512]{3,0,2,1:T(8,128)(2,1)S(1)} %copy.13), channel_id=1, source_target_pairs={{0,16},{8,24},{16,0},{24,8},{1,17},{9,25},{17,1},{25,9},{2,18},{10... | collective-permute-start | bytes 196616 | tf_op jit(solution)/shard_map/ppermute | solution.py:341
  4.4 5.5 %copy-start = (bf16[3,3,3,512,128]{4,3,2,1,0:T(8,128)(2,1)S(1)}, bf16[3,3,3,512,128]{4,3,2,1,0:T(8,128)(2,1)}, u32[]{:S(2)}) copy-start(bf16[3,3,3,512,128]{4,3,2,1,0:T(8,128)(2,1)} %refs_4_.3) | copy-start | bytes 10616836
  5.7 9.0 %copy-start.1 = (bf16[512,256]{1,0:T(8,128)(2,1)S(1)}, bf16[512,256]{1,0:T(8,128)(2,1)}, u32[]{:S(2)}) copy-start(bf16[512,256]{1,0:T(8,128)(2,1)} %refs_4_.5) | copy-start | bytes 786436
  5.7 11.2 %collective-permute-start.10 = (bf16[3,3,3,8,256]{4,3,2,1,0:T(8,128)(2,1)S(1)}, bf16[3,3,3,8,256]{4,3,2,1,0:T(8,128)(2,1)S(1)}, u32[]{:S(2)}, u32[]{:S(2)}) collective-permute-start(bf16[3,3,3,8,256]{4,3,2,1,0:T(8,128)(2,1)S(1)} %shard_map.67), channel_id=1, source_target_pairs={{0,6},{1,7},{2,4},{3,5},{4,2},{5,3},{6,0},{7,1},{8,14},{9,15},{10,... | collective-permute-start | bytes 331784 | tf_op jit(solution)/shard_map/ppermute | solution.py:341
  7.3 8.0 %collective-permute-start.8 = (bf16[3,3,3,8,256]{4,3,2,1,0:T(8,128)(2,1)S(1)}, bf16[3,3,3,8,256]{4,3,2,1,0:T(8,128)(2,1)S(1)}, u32[]{:S(2)}, u32[]{:S(2)}) collective-permute-start(bf16[3,3,3,8,256]{4,3,2,1,0:T(8,128)(2,1)S(1)} %shard_map.67), channel_id=1, source_target_pairs={{0,2},{1,3},{2,0},{3,1},{4,6},{5,7},{6,4},{7,5},{8,10},{9,11},{10,... | collective-permute-start | bytes 331784 | tf_op jit(solution)/shard_map/ppermute | solution.py:341
  9.8 7.0 %collective-permute-start.9 = (bf16[3,3,3,8,256]{4,3,2,1,0:T(8,128)(2,1)S(1)}, bf16[3,3,3,8,256]{4,3,2,1,0:T(8,128)(2,1)S(1)}, u32[]{:S(2)}, u32[]{:S(2)}) collective-permute-start(bf16[3,3,3,8,256]{4,3,2,1,0:T(8,128)(2,1)S(1)} %shard_map.67), channel_id=1, source_target_pairs={{0,4},{1,5},{2,6},{3,7},{4,0},{5,1},{6,2},{7,3},{8,12},{9,13},{10,... | collective-permute-start | bytes 331784 | tf_op jit(solution)/shard_map/ppermute | solution.py:341
  11.6 7.0 %collective-permute-start.5 = (bf16[4,128,128]{2,1,0:T(8,128)(2,1)S(1)}, bf16[4,128,128]{2,1,0:T(8,128)(2,1)S(1)}, u32[]{:S(2)}, u32[]{:S(2)}) collective-permute-start(bf16[4,128,128]{2,1,0:T(8,128)(2,1)S(1)} %shard_map.64.refs_0_), channel_id=1, source_target_pairs={{0,24},{8,16},{16,8},{24,0},{1,25},{9,17},{17,9},{25,1},{2,26},{10... | collective-permute-start | bytes 393224 | tf_op jit(solution)/shard_map/ppermute | solution.py:341
  14.2 5.4 %collective-permute-start.4 = (bf16[4,128,128]{2,1,0:T(8,128)(2,1)S(1)}, bf16[4,128,128]{2,1,0:T(8,128)(2,1)S(1)}, u32[]{:S(2)}, u32[]{:S(2)}) collective-permute-start(bf16[4,128,128]{2,1,0:T(8,128)(2,1)S(1)} %shard_map.64.refs_0_), channel_id=1, source_target_pairs={{0,16},{8,24},{16,0},{24,8},{1,17},{9,25},{17,1},{25,9},{2,18},{10... | collective-permute-start | bytes 393224 | tf_op jit(solution)/shard_map/ppermute | solution.py:341
  15.3 5.0 %collective-permute-start.3 = (bf16[4,128,128]{2,1,0:T(8,128)(2,1)S(1)}, bf16[4,128,128]{2,1,0:T(8,128)(2,1)S(1)}, u32[]{:S(2)}, u32[]{:S(2)}) collective-permute-start(bf16[4,128,128]{2,1,0:T(8,128)(2,1)S(1)} %shard_map.64.refs_0_), channel_id=1, source_target_pairs={{0,8},{8,0},{16,24},{24,16},{1,9},{9,1},{17,25},{25,17},{2,10},{10... | collective-permute-start | bytes 393224 | tf_op jit(solution)/shard_map/ppermute | solution.py:341
  20.7 2.8 %collective-permute-start.11 = (bf16[4,3,3,3,8,256]{5,4,3,2,1,0:T(8,128)(2,1)S(1)}, bf16[4,3,3,3,8,256]{5,4,3,2,1,0:T(8,128)(2,1)S(1)}, u32[]{:S(2)}, u32[]{:S(2)}) collective-permute-start(bf16[4,3,3,3,8,256]{5,4,3,2,1,0:T(8,128)(2,1)S(1)} %pad_maximum_fusion), channel_id=1, source_target_pairs={{0,1},{1,0},{2,3},{3,2},{4,5},{5,4},{6,7},{7,6},{8,9},{9,8},{10,11... | collective-permute-start | bytes 1327112 | tf_op jit(solution)/shard_map/ppermute | solution.py:341
  20.8 3.5 %collective-permute-start.6 = (bf16[2,128,256]{2,1,0:T(8,128)(2,1)S(1)}, bf16[2,128,256]{2,1,0:T(8,128)(2,1)S(1)}, u32[]{:S(2)}, u32[]{:S(2)}) collective-permute-start(bf16[2,128,256]{2,1,0:T(8,128)(2,1)S(1)} %get-tuple-element.23), channel_id=1, source_target_pairs={{0,1},{1,0},{2,3},{3,2},{4,5},{5,4},{6,7},{7,6},{8,9},{9,8},{10,11... | collective-permute-start | bytes 393224 | tf_op jit(solution)/shard_map/ppermute | solution.py:341
  21.4 6.3 %collective-permute-start.7 = (bf16[2,128,256]{2,1,0:T(8,128)(2,1)S(1)}, bf16[2,128,256]{2,1,0:T(8,128)(2,1)S(1)}, u32[]{:S(2)}, u32[]{:S(2)}) collective-permute-start(bf16[2,128,256]{2,1,0:T(8,128)(2,1)S(1)} %get-tuple-element.24), channel_id=1, source_target_pairs={{1,2},{3,4},{5,6},{2,1},{4,3},{6,5},{9,10},{11,12},{13,14},{10,9},... | collective-permute-start | bytes 393224 | tf_op jit(solution)/shard_map/ppermute | solution.py:424
  24.3 8.2 %copy-start.2 = (bf16[3,3,3,128,128]{4,3,2,1,0:T(8,128)(2,1)S(1)}, bf16[3,3,3,128,128]{4,3,2,1,0:T(8,128)(2,1)}, u32[]{:S(2)}) copy-start(bf16[3,3,3,128,128]{4,3,2,1,0:T(8,128)(2,1)} %filters.1) | copy-start | bytes 2654212
  24.3 8.2 %copy-start.3 = (bf16[256,128]{1,0:T(8,128)(2,1)S(1)}, bf16[256,128]{1,0:T(8,128)(2,1)}, u32[]{:S(2)}) copy-start(bf16[256,128]{1,0:T(8,128)(2,1)} %refs_6_.1) | copy-start | bytes 196612
  29.0 4.4 %collective-permute-start.12 = (bf16[3,48,256]{2,1,0:T(8,128)(2,1)S(1)}, bf16[3,48,256]{2,1,0:T(8,128)(2,1)S(1)}, u32[]{:S(2)}, u32[]{:S(2)}) collective-permute-start(bf16[3,48,256]{2,1,0:T(8,128)(2,1)S(1)} %get-tuple-element.27), channel_id=1, source_target_pairs={{0,8},{8,0},{16,24},{24,16},{1,9},{9,1},{17,25},{25,17},{2,10},{10... | collective-permute-start | bytes 221192 | tf_op jit(solution)/shard_map/ppermute | solution.py:341
  30.5 4.4 %collective-permute-start.13 = (bf16[3,48,256]{2,1,0:T(8,128)(2,1)S(1)}, bf16[3,48,256]{2,1,0:T(8,128)(2,1)S(1)}, u32[]{:S(2)}, u32[]{:S(2)}) collective-permute-start(bf16[3,48,256]{2,1,0:T(8,128)(2,1)S(1)} %get-tuple-element.28), channel_id=1, source_target_pairs={{0,16},{8,24},{16,0},{24,8},{1,17},{9,25},{17,1},{25,9},{2,18},{10... | collective-permute-start | bytes 221192 | tf_op jit(solution)/shard_map/ppermute | solution.py:341
  32.0 5.3 %collective-permute-start.14 = (bf16[3,48,256]{2,1,0:T(8,128)(2,1)S(1)}, bf16[3,48,256]{2,1,0:T(8,128)(2,1)S(1)}, u32[]{:S(2)}, u32[]{:S(2)}) collective-permute-start(bf16[3,48,256]{2,1,0:T(8,128)(2,1)S(1)} %get-tuple-element.29), channel_id=1, source_target_pairs={{0,24},{8,16},{16,8},{24,0},{1,25},{9,17},{17,9},{25,1},{2,26},{10... | collective-permute-start | bytes 221192 | tf_op jit(solution)/shard_map/ppermute | solution.py:341

commit v3 on v2

--- a/solution.py
+++ b/solution.py
@@ -176,26 +176,28 @@
     sums[:, 0:1] = empty
     sums[:, 1 : height + 1] = total
     sums[:, height + 1 : height + 2] = empty
+    half = lanes // 2
     for k in range(groups):
         chunk = sums[:, pl.ds((me ^ k) * rows, rows + 2)]
-        outs[k][...] = chunk.reshape(pairs, (rows + 2) * frames, lanes).astype(BF16)
+        ends = jnp.concatenate([chunk[:, rows + 1 :, :, :half], chunk[:, :1, :, half:]], axis=3)
+        chunk = jnp.concatenate([ends, chunk[:, 1 : rows + 1]], axis=1)
+        outs[k][...] = chunk.reshape(pairs * (rows + 1) * frames, lanes).astype(BF16)
 
 
 def fine_kernel(groups, frames, *refs):
     chunks = refs[:groups]
     block, spread, proj, filters, out, acts, acts_odd, lows = refs[groups:]
-    pairs, cells, lanes = chunks[0].shape
-    extent = block.shape[0]
-    rows = cells // frames - 2
+    extent, cells = block.shape[:2]
+    pairs, rows = extent - 1, cells // frames - 2
     width = proj.shape[1]
     tall, broad = 2 * rows, 2 * (extent - 2)
     me, last_me = lax.axis_index("grp"), lax.axis_size("grp") - 1
     tile, last_tile = lax.axis_index("tile"), lax.axis_size("tile") - 1
     total = None
     for k in range(groups):
-        term = dot(chunks[k][...].reshape(pairs * cells, lanes), spread[k])
+        term = dot(chunks[k][...], spread[k])
         total = term if total is None else total + term
-    total = total.reshape(pairs, rows + 2, frames, 4 * width)
+    total = total.reshape(pairs, rows + 1, frames, 4 * width)
     base = dot(block[...].reshape(extent * cells, block.shape[2]), proj[...])
     base = base.reshape(extent, rows + 2, frames, width)
     nothing = jnp.zeros((1, frames, width), F32)
@@ -203,10 +205,11 @@
         pair, side = divmod(col, 2)
         upper, lower = [
             total[pair, :, :, (2 * p + side) * width : (2 * p + side + 1) * width]
-            + base[pair + side]
             for p in range(2)
         ]
-        woven = jnp.stack([lower[: rows + 1], upper[1:]], axis=1)
+        lower = lower + base[pair + side, : rows + 1]
+        upper = jnp.concatenate([upper[1:], upper[:1]], axis=0) + base[pair + side, 1:]
+        woven = jnp.stack([lower, upper], axis=1)
         value = woven.reshape(tall + 2, frames, width).astype(BF16).astype(F32)
         if col == 0:
             value = jnp.where(tile == 0, 0.0, value)
@@ -369,8 +372,11 @@
             mid_rows,
             stay=(0,),
         )
-        mine = [mine] + [exchange(mine, "tile", k) for k in range(2, tiles, 2)]
-        mine = jnp.stack(mine)
+        mine, bit = mine[None], 2
+        while 2 * bit < tiles:
+            mine = jnp.concatenate([mine, exchange(mine, "tile", bit)])
+            bit *= 2
+        beyond = exchange(mine, "tile", bit)
     else:
         every = lax.all_gather(mid_rows, "tile", axis=3, tiled=True)
         mine = lax.dynamic_slice_in_dim(every, me * share, share, axis=3)[None]
@@ -379,8 +385,8 @@
         functools.partial(coarse_kernel, groups),
         jax.ShapeDtypeStruct((cols + 2, cells, width0), BF16),
         [pltpu.VMEM((3, height + 2, cols * frames, depth0), BF16)],
-        2 * 27 * cells * cols * depth0 * width0,
-        5 * 10**6,
+        5 * 10**8,
+        10**5,
         *pieces,
         coarse_filters,
     )
@@ -409,8 +415,9 @@
         straight,
     )
     if divided:
-        later, _ = lax.optimization_barrier((mine, own))
-        mine = jnp.concatenate([mine, exchange(later, "tile", 1)])
+        beyond, _ = lax.optimization_barrier((beyond, own))
+        mine = jnp.concatenate([mine, beyond])
+        mine = jnp.concatenate([mine, exchange(mine, "tile", 1)])
     mid_folded = call(
         fold_middle_kernel,
         jax.ShapeDtypeStruct((3, 3, 2, depth1, lanes), BF16),
@@ -425,7 +432,10 @@
     local = (rows + 2) * frames
     *chunks, block = call(
         functools.partial(middle_kernel, groups, rows, frames),
-        tuple(jax.ShapeDtypeStruct((cols + 1, local, lanes), BF16) for _ in range(groups))
+        tuple(
+            jax.ShapeDtypeStruct(((cols + 1) * (rows + 1) * frames, lanes), BF16)
+            for _ in range(groups)
+        )
         + (jax.ShapeDtypeStruct((cols + 2, local, depth1), BF16),),
         [
             pltpu.VMEM((3, cols + 2, cells + 2 * frames, depth1), BF16),

time: 39.4 us -> 37.6 us (0.954)
  the two profiles are of different devices: /device:TPU:8 before, /device:TPU:16 now
where the time goes in v3:
time: 37.6 us; the launch traced here: 37.5 us
  starting transfers between devices  15.2 us (40%)
  waiting for transfers between devices  14 us (37%)
  Pallas kernels  7.94 us (21%)
    ppermute x13, starting transfers between devices, exchange(): return lax.ppermute(values, axis, [(i, i ^ k) for i in range(size)])  13.3 us
    ppermute x13, waiting for transfers between devices, exchange(): return lax.ppermute(values, axis, [(i, i ^ k) for i in range(size)])  10.4 us
    pallas_call x8, Pallas kernels, call(): pl.pallas_call(kernel, out_shape=outs, in_specs=[FAR if n in stay else VM...  7.94 us
    ppermute x1, waiting for transfers between devices, body(): lax.ppermute(odd_out, 'tile', odd_pairs + [(j, i) for i, j in odd_pairs])  3.54 us
    ppermute x1, starting transfers between devices, body(): lax.ppermute(odd_out, 'tile', odd_pairs + [(j, i) for i, j in odd_pairs])  1.91 us
  transfers between devices with their start and end apart: 14, of which 10 were waited for; matrix products, arithmetic and copies ran while one was open for 0% of the time, Pallas kernels for 9%

profile of v3, /device:TPU:16, one launch (start us, length us, event | category | flops | bytes accessed | tf_op | source)
XLA Modules:
  0.0 37.5 jit_solution(1669410428771937730)
XLA Ops:
  0.0 1.2 %shard_map.67 = bf16[3,3,3,8,256]{4,3,2,1,0:T(8,128)(2,1)S(1)} custom-call(bf16[3,3,3,32,256]{4,3,2,1,0:T(8,128)(2,1)} %bitcast.19), custom_call_target="tpu_custom_call" | custom-call | flops 6000000000 | bytes 1000000 | tf_op jit(solution)/shard_map/pallas_call | solution.py:21
  1.3 1.6 %collective-permute-start.8 = (bf16[1,3,3,3,8,256]{5,4,3,2,1,0:T(8,128)(2,1)S(1)}, bf16[1,3,3,3,8,256]{5,4,3,2,1,0:T(8,128)(2,1)S(1)}, u32[]{:S(2)}, u32[]{:S(2)}) collective-permute-start(bf16[1,3,3,3,8,256]{5,4,3,2,1,0:T(8,128)(2,1)S(1)} %bitcast.7), channel_id=1, source_target_pairs={{0,2},{1,3},{2,0},{3,1},{4,6},{5,7},{6,4},{7,5},{8,10},{9,11},{10,... | collective-permute-start | bytes 331784 | tf_op jit(solution)/shard_map/ppermute | solution.py:344
  2.9 1.6 %collective-permute-start = (bf16[8,4,2,512]{3,0,2,1:T(8,128)(2,1)S(1)}, bf16[8,4,2,512]{3,0,2,1:T(8,128)(2,1)S(1)}, u32[]{:S(2)}, u32[]{:S(2)}) collective-permute-start(bf16[8,4,2,512]{3,0,2,1:T(8,128)(2,1)S(1)} %copy.13), channel_id=1, source_target_pairs={{0,8},{8,0},{16,24},{24,16},{1,9},{9,1},{17,25},{25,17},{2,10},{10... | collective-permute-start | bytes 196616 | tf_op jit(solution)/shard_map/ppermute | solution.py:344
  4.5 1.5 %collective-permute-start.2 = (bf16[8,4,2,512]{3,0,2,1:T(8,128)(2,1)S(1)}, bf16[8,4,2,512]{3,0,2,1:T(8,128)(2,1)S(1)}, u32[]{:S(2)}, u32[]{:S(2)}) collective-permute-start(bf16[8,4,2,512]{3,0,2,1:T(8,128)(2,1)S(1)} %copy.13), channel_id=1, source_target_pairs={{0,24},{8,16},{16,8},{24,0},{1,25},{9,17},{17,9},{25,1},{2,26},{10... | collective-permute-start | bytes 196616 | tf_op jit(solution)/shard_map/ppermute | solution.py:344
  6.0 0.5 %collective-permute-start.1 = (bf16[8,4,2,512]{3,0,2,1:T(8,128)(2,1)S(1)}, bf16[8,4,2,512]{3,0,2,1:T(8,128)(2,1)S(1)}, u32[]{:S(2)}, u32[]{:S(2)}) collective-permute-start(bf16[8,4,2,512]{3,0,2,1:T(8,128)(2,1)S(1)} %copy.13), channel_id=1, source_target_pairs={{0,16},{8,24},{16,0},{24,8},{1,17},{9,25},{17,1},{25,9},{2,18},{10... | collective-permute-start | bytes 196616 | tf_op jit(solution)/shard_map/ppermute | solution.py:344
  7.3 2.4 %collective-permute-done.2 = bf16[8,4,2,512]{3,0,2,1:T(8,128)(2,1)S(1)} collective-permute-done((bf16[8,4,2,512]{3,0,2,1:T(8,128)(2,1)S(1)}, bf16[8,4,2,512]{3,0,2,1:T(8,128)(2,1)S(1)}, u32[]{:S(2)}, u32[]{:S(2)}) %collective-permute-start.2) | collective-permute-done | bytes 65568 | tf_op jit(solution)/shard_map/ppermute | solution.py:344
  9.7 0.7 %collective-permute-done.1 = bf16[8,4,2,512]{3,0,2,1:T(8,128)(2,1)S(1)} collective-permute-done((bf16[8,4,2,512]{3,0,2,1:T(8,128)(2,1)S(1)}, bf16[8,4,2,512]{3,0,2,1:T(8,128)(2,1)S(1)}, u32[]{:S(2)}, u32[]{:S(2)}) %collective-permute-start.1) | collective-permute-done | bytes 65568 | tf_op jit(solution)/shard_map/ppermute | solution.py:344
  10.4 1.7 %shard_map.64.refs_0_ = bf16[4,128,128]{2,1,0:T(8,128)(2,1)S(1)} custom-call(bf16[4,2,8,512]{3,2,1,0:T(8,128)(2,1)S(1)} %bitcast.11, bf16[4,2,8,512]{3,2,1,0:T(8,128)(2,1)S(1)} %bitcast.13, bf16[4,2,8,512]{3,2,1,0:T(8,128)(2,1)S(1)} %bitcast.17, bf16[4,2,8,512]{3,2,1,0:T(8,128)(2,1)S(1)} %bitcast.15, bf16[3,3,3,512,128]{4,3,2,1,0:T(8,128)(2,1)S(1)} %copy-done), custom_call_target="tpu_custom_call" | custom-call | flops 500000000 | bytes 100000 | tf_op jit(solution)/shard_map/pallas_call | solution.py:21
  12.1 1.6 %collective-permute-start.5 = (bf16[4,128,128]{2,1,0:T(8,128)(2,1)S(1)}, bf16[4,128,128]{2,1,0:T(8,128)(2,1)S(1)}, u32[]{:S(2)}, u32[]{:S(2)}) collective-permute-start(bf16[4,128,128]{2,1,0:T(8,128)(2,1)S(1)} %shard_map.64.refs_0_), channel_id=1, source_target_pairs={{0,24},{8,16},{16,8},{24,0},{1,25},{9,17},{17,9},{25,1},{2,26},{10... | collective-permute-start | bytes 393224 | tf_op jit(solution)/shard_map/ppermute | solution.py:344
  13.6 1.4 %collective-permute-start.4 = (bf16[4,128,128]{2,1,0:T(8,128)(2,1)S(1)}, bf16[4,128,128]{2,1,0:T(8,128)(2,1)S(1)}, u32[]{:S(2)}, u32[]{:S(2)}) collective-permute-start(bf16[4,128,128]{2,1,0:T(8,128)(2,1)S(1)} %shard_map.64.refs_0_), channel_id=1, source_target_pairs={{0,16},{8,24},{16,0},{24,8},{1,17},{9,25},{17,1},{25,9},{2,18},{10... | collective-permute-start | bytes 393224 | tf_op jit(solution)/shard_map/ppermute | solution.py:344
  15.0 0.6 %collective-permute-start.3 = (bf16[4,128,128]{2,1,0:T(8,128)(2,1)S(1)}, bf16[4,128,128]{2,1,0:T(8,128)(2,1)S(1)}, u32[]{:S(2)}, u32[]{:S(2)}) collective-permute-start(bf16[4,128,128]{2,1,0:T(8,128)(2,1)S(1)} %shard_map.64.refs_0_), channel_id=1, source_target_pairs={{0,8},{8,0},{16,24},{24,16},{1,9},{9,1},{17,25},{25,17},{2,10},{10... | collective-permute-start | bytes 393224 | tf_op jit(solution)/shard_map/ppermute | solution.py:344
  15.9 2.2 %collective-permute-done.5.refs_3_ = bf16[4,128,128]{2,1,0:T(8,128)(2,1)S(1)} collective-permute-done((bf16[4,128,128]{2,1,0:T(8,128)(2,1)S(1)}, bf16[4,128,128]{2,1,0:T(8,128)(2,1)S(1)}, u32[]{:S(2)}, u32[]{:S(2)}) %collective-permute-start.5) | collective-permute-done | bytes 131104 | tf_op jit(solution)/shard_map/ppermute | solution.py:344
  18.2 1.3 %collective-permute-done.4.refs_2_ = bf16[4,128,128]{2,1,0:T(8,128)(2,1)S(1)} collective-permute-done((bf16[4,128,128]{2,1,0:T(8,128)(2,1)S(1)}, bf16[4,128,128]{2,1,0:T(8,128)(2,1)S(1)}, u32[]{:S(2)}, u32[]{:S(2)}) %collective-permute-start.4) | collective-permute-done | bytes 131104 | tf_op jit(solution)/shard_map/ppermute | solution.py:344
  20.5 0.5 %collective-permute-start.6 = (bf16[2,128,256]{2,1,0:T(8,128)(2,1)S(1)}, bf16[2,128,256]{2,1,0:T(8,128)(2,1)S(1)}, u32[]{:S(2)}, u32[]{:S(2)}) collective-permute-start(bf16[2,128,256]{2,1,0:T(8,128)(2,1)S(1)} %get-tuple-element.23), channel_id=1, source_target_pairs={{0,1},{1,0},{2,3},{3,2},{4,5},{5,4},{6,7},{7,6},{8,9},{9,8},{10,11... | collective-permute-start | bytes 393224 | tf_op jit(solution)/shard_map/ppermute | solution.py:344
  21.0 1.9 %collective-permute-start.7 = (bf16[2,128,256]{2,1,0:T(8,128)(2,1)S(1)}, bf16[2,128,256]{2,1,0:T(8,128)(2,1)S(1)}, u32[]{:S(2)}, u32[]{:S(2)}) collective-permute-start(bf16[2,128,256]{2,1,0:T(8,128)(2,1)S(1)} %get-tuple-element.24), channel_id=1, source_target_pairs={{1,2},{3,4},{5,6},{2,1},{4,3},{6,5},{9,10},{11,12},{13,14},{10,9},... | collective-permute-start | bytes 393224 | tf_op jit(solution)/shard_map/ppermute | solution.py:431
  23.0 0.7 %shard_map.68.filters = bf16[3,3,2,256,256]{4,3,2,1,0:T(8,128)(2,1)S(1)} custom-call(bf16[8,3,3,3,8,256]{5,4,3,2,1,0:T(8,128)(2,1)S(1)} %pad_maximum_fusion.pieces), custom_call_target="tpu_custom_call" | custom-call | flops 1000000 | bytes 4000000 | tf_op jit(solution)/shard_map/pallas_call | solution.py:21
  23.8 3.5 %collective-permute-done.7.odd_in = bf16[2,128,256]{2,1,0:T(8,128)(2,1)S(1)} collective-permute-done((bf16[2,128,256]{2,1,0:T(8,128)(2,1)S(1)}, bf16[2,128,256]{2,1,0:T(8,128)(2,1)S(1)}, u32[]{:S(2)}, u32[]{:S(2)}) %collective-permute-start.7) | collective-permute-done | bytes 131104 | tf_op jit(solution)/shard_map/ppermute | solution.py:431
  27.3 1.3 %shard_map.69 = (bf16[120,256]{1,0:T(8,128)(2,1)S(1)}, bf16[120,256]{1,0:T(8,128)(2,1)S(1)}, bf16[120,256]{1,0:T(8,128)(2,1)S(1)}, bf16[120,256]{1,0:T(8,128)(2,1)S(1)}, bf16[4,48,256]{2,1,0:T(8,128)(2,1)S(1)}) custom-call(f32[4,128,256]{2,1,0:T(8,128)S(1)} %get-tuple-element.22.own, bf16[2,128,256]{2,1,0:T(8,128)(2,1)S(1)} %collective-permute-done.6.even_in, ...), custom_call_target="tpu_custom_call" | custom-call | flops 905969664 | bytes 5000000 | tf_op jit(solution)/shard_map/pallas_call | solution.py:21
  28.6 0.9 %collective-permute-start.11 = (bf16[120,256]{1,0:T(8,128)(2,1)S(1)}, bf16[120,256]{1,0:T(8,128)(2,1)S(1)}, u32[]{:S(2)}, u32[]{:S(2)}) collective-permute-start(bf16[120,256]{1,0:T(8,128)(2,1)S(1)} %get-tuple-element.27), channel_id=1, source_target_pairs={{0,8},{8,0},{16,24},{24,16},{1,9},{9,1},{17,25},{25,17},{2,10},{10... | collective-permute-start | bytes 184328 | tf_op jit(solution)/shard_map/ppermute | solution.py:344
  29.5 0.9 %collective-permute-start.12 = (bf16[120,256]{1,0:T(8,128)(2,1)S(1)}, bf16[120,256]{1,0:T(8,128)(2,1)S(1)}, u32[]{:S(2)}, u32[]{:S(2)}) collective-permute-start(bf16[120,256]{1,0:T(8,128)(2,1)S(1)} %get-tuple-element.28), channel_id=1, source_target_pairs={{0,16},{8,24},{16,0},{24,8},{1,17},{9,25},{17,1},{25,9},{2,18},{10... | collective-permute-start | bytes 184328 | tf_op jit(solution)/shard_map/ppermute | solution.py:344
  30.4 1.7 %collective-permute-start.13 = (bf16[120,256]{1,0:T(8,128)(2,1)S(1)}, bf16[120,256]{1,0:T(8,128)(2,1)S(1)}, u32[]{:S(2)}, u32[]{:S(2)}) collective-permute-start(bf16[120,256]{1,0:T(8,128)(2,1)S(1)} %get-tuple-element.29), channel_id=1, source_target_pairs={{0,24},{8,16},{16,8},{24,0},{1,25},{9,17},{17,9},{25,1},{2,26},{10... | collective-permute-start | bytes 184328 | tf_op jit(solution)/shard_map/ppermute | solution.py:344
  32.9 1.5 %collective-permute-done.12.refs_2_ = bf16[120,256]{1,0:T(8,128)(2,1)S(1)} collective-permute-done((bf16[120,256]{1,0:T(8,128)(2,1)S(1)}, bf16[120,256]{1,0:T(8,128)(2,1)S(1)}, u32[]{:S(2)}, u32[]{:S(2)}) %collective-permute-start.12) | collective-permute-done | bytes 61472 | tf_op jit(solution)/shard_map/ppermute | solution.py:344
  34.4 1.1 %collective-permute-done.13.refs_3_ = bf16[120,256]{1,0:T(8,128)(2,1)S(1)} collective-permute-done((bf16[120,256]{1,0:T(8,128)(2,1)S(1)}, bf16[120,256]{1,0:T(8,128)(2,1)S(1)}, u32[]{:S(2)}, u32[]{:S(2)}) %collective-permute-start.13) | collective-permute-done | bytes 61472 | tf_op jit(solution)/shard_map/ppermute | solution.py:344
  35.5 1.9 %shard_map.71 = bf16[8,16,8,128]{3,2,1,0:T(8,128)(2,1)} custom-call(bf16[120,256]{1,0:T(8,128)(2,1)S(1)} %get-tuple-element.26.refs_0_, bf16[120,256]{1,0:T(8,128)(2,1)S(1)} %collective-permute-done.11.refs_1_, bf16[120,256]{1,0:T(8,128)(2,1)S(1)} %collective-permute-done.12.refs_2_, bf16[120,256]{1,0:T(8,128)(2,1)S(1)} %collective-permute-done.13.refs_3_, ...), custom_call_target="tpu_custom_call" | custom-call | flops 503316480 | bytes 3000000 | tf_op jit(solution)/shard_map/pallas_call | solution.py:21
  (26 shorter events, 2.9 us)
Async XLA Ops:
  0.0 2.9 %copy-start.4 = (bf16[8,4,2,512]{3,2,1,0:T(2,128)(2,1)S(1)}, bf16[8,4,2,512]{3,2,1,0:T(2,128)(2,1)}, u32[]{:S(2)}) copy-start(bf16[8,4,2,512]{3,2,1,0:T(2,128)(2,1)} %param.6) | copy-start | bytes 196612
  0.0 10.3 %copy-start = (bf16[3,3,3,512,128]{4,3,2,1,0:T(8,128)(2,1)S(1)}, bf16[3,3,3,512,128]{4,3,2,1,0:T(8,128)(2,1)}, u32[]{:S(2)}) copy-start(bf16[3,3,3,512,128]{4,3,2,1,0:T(8,128)(2,1)} %refs_4_.3) | copy-start | bytes 10616836
  1.2 14.4 %copy-start.1 = (bf16[512,256]{1,0:T(8,128)(2,1)S(1)}, bf16[512,256]{1,0:T(8,128)(2,1)}, u32[]{:S(2)}) copy-start(bf16[512,256]{1,0:T(8,128)(2,1)} %refs_4_.5) | copy-start | bytes 786436
  1.3 5.2 %collective-permute-start.8 = (bf16[1,3,3,3,8,256]{5,4,3,2,1,0:T(8,128)(2,1)S(1)}, bf16[1,3,3,3,8,256]{5,4,3,2,1,0:T(8,128)(2,1)S(1)}, u32[]{:S(2)}, u32[]{:S(2)}) collective-permute-start(bf16[1,3,3,3,8,256]{5,4,3,2,1,0:T(8,128)(2,1)S(1)} %bitcast.7), channel_id=1, source_target_pairs={{0,2},{1,3},{2,0},{3,1},{4,6},{5,7},{6,4},{7,5},{8,10},{9,11},{10,... | collective-permute-start | bytes 331784 | tf_op jit(solution)/shard_map/ppermute | solution.py:344
  2.9 4.3 %collective-permute-start = (bf16[8,4,2,512]{3,0,2,1:T(8,128)(2,1)S(1)}, bf16[8,4,2,512]{3,0,2,1:T(8,128)(2,1)S(1)}, u32[]{:S(2)}, u32[]{:S(2)}) collective-permute-start(bf16[8,4,2,512]{3,0,2,1:T(8,128)(2,1)S(1)} %copy.13), channel_id=1, source_target_pairs={{0,8},{8,0},{16,24},{24,16},{1,9},{9,1},{17,25},{25,17},{2,10},{10... | collective-permute-start | bytes 196616 | tf_op jit(solution)/shard_map/ppermute | solution.py:344
  4.5 5.2 %collective-permute-start.2 = (bf16[8,4,2,512]{3,0,2,1:T(8,128)(2,1)S(1)}, bf16[8,4,2,512]{3,0,2,1:T(8,128)(2,1)S(1)}, u32[]{:S(2)}, u32[]{:S(2)}) collective-permute-start(bf16[8,4,2,512]{3,0,2,1:T(8,128)(2,1)S(1)} %copy.13), channel_id=1, source_target_pairs={{0,24},{8,16},{16,8},{24,0},{1,25},{9,17},{17,9},{25,1},{2,26},{10... | collective-permute-start | bytes 196616 | tf_op jit(solution)/shard_map/ppermute | solution.py:344
  6.0 4.4 %collective-permute-start.1 = (bf16[8,4,2,512]{3,0,2,1:T(8,128)(2,1)S(1)}, bf16[8,4,2,512]{3,0,2,1:T(8,128)(2,1)S(1)}, u32[]{:S(2)}, u32[]{:S(2)}) collective-permute-start(bf16[8,4,2,512]{3,0,2,1:T(8,128)(2,1)S(1)} %copy.13), channel_id=1, source_target_pairs={{0,16},{8,24},{16,0},{24,8},{1,17},{9,25},{17,1},{25,9},{2,18},{10... | collective-permute-start | bytes 196616 | tf_op jit(solution)/shard_map/ppermute | solution.py:344
  6.5 13.9 %collective-permute-start.9 = (bf16[2,3,3,3,8,256]{5,4,3,2,1,0:T(8,128)(2,1)S(1)}, bf16[2,3,3,3,8,256]{5,4,3,2,1,0:T(8,128)(2,1)S(1)}, u32[]{:S(2)}, u32[]{:S(2)}) collective-permute-start(bf16[2,3,3,3,8,256]{5,4,3,2,1,0:T(8,128)(2,1)S(1)} %pad_maximum_fusion.2), channel_id=1, source_target_pairs={{0,4},{1,5},{2,6},{3,7},{4,0},{5,1},{6,2},{7,3},{8,12},{9,13},{10,... | collective-permute-start | bytes 663560 | tf_op jit(solution)/shard_map/ppermute | solution.py:344
  12.1 6.1 %collective-permute-start.5 = (bf16[4,128,128]{2,1,0:T(8,128)(2,1)S(1)}, bf16[4,128,128]{2,1,0:T(8,128)(2,1)S(1)}, u32[]{:S(2)}, u32[]{:S(2)}) collective-permute-start(bf16[4,128,128]{2,1,0:T(8,128)(2,1)S(1)} %shard_map.64.refs_0_), channel_id=1, source_target_pairs={{0,24},{8,16},{16,8},{24,0},{1,25},{9,17},{17,9},{25,1},{2,26},{10... | collective-permute-start | bytes 393224 | tf_op jit(solution)/shard_map/ppermute | solution.py:344
  13.6 5.9 %collective-permute-start.4 = (bf16[4,128,128]{2,1,0:T(8,128)(2,1)S(1)}, bf16[4,128,128]{2,1,0:T(8,128)(2,1)S(1)}, u32[]{:S(2)}, u32[]{:S(2)}) collective-permute-start(bf16[4,128,128]{2,1,0:T(8,128)(2,1)S(1)} %shard_map.64.refs_0_), channel_id=1, source_target_pairs={{0,16},{8,24},{16,0},{24,8},{1,17},{9,25},{17,1},{25,9},{2,18},{10... | collective-permute-start | bytes 393224 | tf_op jit(solution)/shard_map/ppermute | solution.py:344
  15.0 5.0 %collective-permute-start.3 = (bf16[4,128,128]{2,1,0:T(8,128)(2,1)S(1)}, bf16[4,128,128]{2,1,0:T(8,128)(2,1)S(1)}, u32[]{:S(2)}, u32[]{:S(2)}) collective-permute-start(bf16[4,128,128]{2,1,0:T(8,128)(2,1)S(1)} %shard_map.64.refs_0_), channel_id=1, source_target_pairs={{0,8},{8,0},{16,24},{24,16},{1,9},{9,1},{17,25},{25,17},{2,10},{10... | collective-permute-start | bytes 393224 | tf_op jit(solution)/shard_map/ppermute | solution.py:344
  20.4 2.5 %collective-permute-start.10 = (bf16[4,3,3,3,8,256]{5,4,3,2,1,0:T(8,128)(2,1)S(1)}, bf16[4,3,3,3,8,256]{5,4,3,2,1,0:T(8,128)(2,1)S(1)}, u32[]{:S(2)}, u32[]{:S(2)}) collective-permute-start(bf16[4,3,3,3,8,256]{5,4,3,2,1,0:T(8,128)(2,1)S(1)} %pad_maximum_fusion.1), channel_id=1, source_target_pairs={{0,1},{1,0},{2,3},{3,2},{4,5},{5,4},{6,7},{7,6},{8,9},{9,8},{10,11... | collective-permute-start | bytes 1327112 | tf_op jit(solution)/shard_map/ppermute | solution.py:344
  20.5 3.2 %collective-permute-start.6 = (bf16[2,128,256]{2,1,0:T(8,128)(2,1)S(1)}, bf16[2,128,256]{2,1,0:T(8,128)(2,1)S(1)}, u32[]{:S(2)}, u32[]{:S(2)}) collective-permute-start(bf16[2,128,256]{2,1,0:T(8,128)(2,1)S(1)} %get-tuple-element.23), channel_id=1, source_target_pairs={{0,1},{1,0},{2,3},{3,2},{4,5},{5,4},{6,7},{7,6},{8,9},{9,8},{10,11... | collective-permute-start | bytes 393224 | tf_op jit(solution)/shard_map/ppermute | solution.py:344
  21.0 6.3 %collective-permute-start.7 = (bf16[2,128,256]{2,1,0:T(8,128)(2,1)S(1)}, bf16[2,128,256]{2,1,0:T(8,128)(2,1)S(1)}, u32[]{:S(2)}, u32[]{:S(2)}) collective-permute-start(bf16[2,128,256]{2,1,0:T(8,128)(2,1)S(1)} %get-tuple-element.24), channel_id=1, source_target_pairs={{1,2},{3,4},{5,6},{2,1},{4,3},{6,5},{9,10},{11,12},{13,14},{10,9},... | collective-permute-start | bytes 393224 | tf_op jit(solution)/shard_map/ppermute | solution.py:431
  23.7 8.4 %copy-start.2 = (bf16[3,3,3,128,128]{4,3,2,1,0:T(8,128)(2,1)S(1)}, bf16[3,3,3,128,128]{4,3,2,1,0:T(8,128)(2,1)}, u32[]{:S(2)}) copy-start(bf16[3,3,3,128,128]{4,3,2,1,0:T(8,128)(2,1)} %filters.1) | copy-start | bytes 2654212
  23.7 8.4 %copy-start.3 = (bf16[256,128]{1,0:T(8,128)(2,1)S(1)}, bf16[256,128]{1,0:T(8,128)(2,1)}, u32[]{:S(2)}) copy-start(bf16[256,128]{1,0:T(8,128)(2,1)} %refs_6_.1) | copy-start | bytes 196612
  28.6 4.3 %collective-permute-start.11 = (bf16[120,256]{1,0:T(8,128)(2,1)S(1)}, bf16[120,256]{1,0:T(8,128)(2,1)S(1)}, u32[]{:S(2)}, u32[]{:S(2)}) collective-permute-start(bf16[120,256]{1,0:T(8,128)(2,1)S(1)} %get-tuple-element.27), channel_id=1, source_target_pairs={{0,8},{8,0},{16,24},{24,16},{1,9},{9,1},{17,25},{25,17},{2,10},{10... | collective-permute-start | bytes 184328 | tf_op jit(solution)/shard_map/ppermute | solution.py:344
  29.5 4.9 %collective-permute-start.12 = (bf16[120,256]{1,0:T(8,128)(2,1)S(1)}, bf16[120,256]{1,0:T(8,128)(2,1)S(1)}, u32[]{:S(2)}, u32[]{:S(2)}) collective-permute-start(bf16[120,256]{1,0:T(8,128)(2,1)S(1)} %get-tuple-element.28), channel_id=1, source_target_pairs={{0,16},{8,24},{16,0},{24,8},{1,17},{9,25},{17,1},{25,9},{2,18},{10... | collective-permute-start | bytes 184328 | tf_op jit(solution)/shard_map/ppermute | solution.py:344
  30.4 5.1 %collective-permute-start.13 = (bf16[120,256]{1,0:T(8,128)(2,1)S(1)}, bf16[120,256]{1,0:T(8,128)(2,1)S(1)}, u32[]{:S(2)}, u32[]{:S(2)}) collective-permute-start(bf16[120,256]{1,0:T(8,128)(2,1)S(1)} %get-tuple-element.29), channel_id=1, source_target_pairs={{0,24},{8,16},{16,8},{24,0},{1,25},{9,17},{17,9},{25,1},{2,26},{10... | collective-permute-start | bytes 184328 | tf_op jit(solution)/shard_map/ppermute | solution.py:344

commit v4 on v3

--- a/solution.py
+++ b/solution.py
@@ -4,6 +4,7 @@
 import jax.numpy as jnp
 from jax import lax
 from jax.experimental import pallas as pl
+from jax.experimental.layout import Layout, with_layout_constraint
 from jax.experimental.pallas import tpu as pltpu
 from jax.sharding import PartitionSpec as P
 
@@ -96,7 +97,7 @@
 
 
 def project_kernel(groups, *refs):
-    parts, (proj, straight, own, even_out, odd_out) = refs[:groups], refs[groups:]
+    parts, (proj, straight, odd_out, even_out, own) = refs[:groups], refs[groups:]
     extent, cells, width = parts[0].shape
     outputs = proj.shape[1]
     me = lax.axis_index("grp")
@@ -118,7 +119,7 @@
     odd_out[...] = jnp.where(odd, right, left).astype(BF16)
 
 
-def middle_kernel(groups, rows, frames, own, even_in, odd_in, filters, *refs):
+def middle_kernel(groups, rows, frames, odd_in, even_in, own, filters, *refs):
     outs, (block, acts, acts_odd, kept, sums) = refs[:groups], refs[groups:]
     extent, cells, depth = own.shape
     cols = extent - 2
@@ -358,7 +359,7 @@
     share, shares = (own_mid // groups, tiles) if divided else (depth1 // groups, 1)
     lanes = 4 * shares * share
     arrived = [exchange(latent, "grp", k) for k in range(1, groups)]
-    arrived = lax.optimization_barrier(arrived)
+    arrived = [with_layout_constraint(piece, Layout((0, 1, 2, 3))) for piece in arrived]
     pieces = [jnp.transpose(piece, (1, 2, 0, 3)) for piece in [latent] + arrived]
 
     mid_rows = jnp.transpose(mid_filters, (0, 1, 2, 4, 3))
@@ -400,12 +401,12 @@
         coarse_proj,
     )
     parts = [part] + [exchange(part, "grp", k) for k in range(1, groups)]
-    own, even_out, odd_out = call(
+    odd_out, even_out, own = call(
         functools.partial(project_kernel, groups),
         (
-            jax.ShapeDtypeStruct((cols + 2, cells, depth1), F32),
             jax.ShapeDtypeStruct((2, cells, depth1), BF16),
             jax.ShapeDtypeStruct((2, cells, depth1), BF16),
+            jax.ShapeDtypeStruct((cols + 2, cells, depth1), F32),
         ),
         [],
         2 * cells * (cols + 2) * depth0 * depth1,
@@ -414,6 +415,9 @@
         coarse_proj,
         straight,
     )
+    odd_pairs = [(i, i + 1) for i in range(1, tiles - 1, 2)]
+    odd_in = lax.ppermute(odd_out, "tile", odd_pairs + [(j, i) for i, j in odd_pairs])
+    even_in = exchange(even_out, "tile", 1)
     if divided:
         beyond, _ = lax.optimization_barrier((beyond, own))
         mine = jnp.concatenate([mine, beyond])
@@ -426,9 +430,6 @@
         4 * 10**6,
         mine,
     )
-    odd_pairs = [(i, i + 1) for i in range(1, tiles - 1, 2)]
-    even_in = exchange(even_out, "tile", 1)
-    odd_in = lax.ppermute(odd_out, "tile", odd_pairs + [(j, i) for i, j in odd_pairs])
     local = (rows + 2) * frames
     *chunks, block = call(
         functools.partial(middle_kernel, groups, rows, frames),
@@ -445,9 +446,9 @@
         ],
         2 * 18 * (cols + 1) * cells * depth1 * lanes,
         5 * 10**6,
+        odd_in,
+        even_in,
         own,
-        even_in,
-        odd_in,
         mid_folded,
     )
     chunks = [chunks[0]] + [exchange(chunks[k], "grp", k) for k in range(1, groups)]

time: 37.6 us -> 37.1 us (0.987)
  the two profiles are of different devices: /device:TPU:16 before, /device:TPU:1 now
where the time goes in v4:
time: 37.1 us; the launch traced here: 36.7 us
  starting transfers between devices  18.2 us (49%)
  waiting for transfers between devices  10.1 us (27%)
  Pallas kernels  7.93 us (21%)
    ppermute x13, starting transfers between devices, exchange(): return lax.ppermute(values, axis, [(i, i ^ k) for i in range(size)])  16.1 us
    pallas_call x8, Pallas kernels, call(): pl.pallas_call(kernel, out_shape=outs, in_specs=[FAR if n in stay else VM...  7.93 us
    ppermute x13, waiting for transfers between devices, exchange(): return lax.ppermute(values, axis, [(i, i ^ k) for i in range(size)])  6.83 us
    ppermute x1, waiting for transfers between devices, body(): lax.ppermute(odd_out, 'tile', odd_pairs + [(j, i) for i, j in odd_pairs])  3.27 us
    ppermute x1, starting transfers between devices, body(): lax.ppermute(odd_out, 'tile', odd_pairs + [(j, i) for i, j in odd_pairs])  2.11 us
  transfers between devices with their start and end apart: 14, of which 10 were waited for; matrix products, arithmetic and copies ran while one was open for 1% of the time, Pallas kernels for 10%

profile of v4, /device:TPU:1, one launch (start us, length us, event | category | flops | bytes accessed | tf_op | source)
XLA Modules:
  0.0 36.7 jit_solution(13677405906640391602)
XLA Ops:
  0.0 1.2 %shard_map.67 = bf16[3,3,3,8,256]{4,3,2,1,0:T(8,128)(2,1)S(1)} custom-call(bf16[3,3,3,32,256]{4,3,2,1,0:T(8,128)(2,1)} %bitcast.26), custom_call_target="tpu_custom_call" | custom-call | flops 6000000000 | bytes 1000000 | tf_op jit(solution)/shard_map/pallas_call | solution.py:22
  1.3 2.2 %collective-permute-start.8 = (bf16[1,3,3,3,8,256]{5,4,3,2,1,0:T(8,128)(2,1)S(1)}, bf16[1,3,3,3,8,256]{5,4,3,2,1,0:T(8,128)(2,1)S(1)}, u32[]{:S(2)}, u32[]{:S(2)}) collective-permute-start(bf16[1,3,3,3,8,256]{5,4,3,2,1,0:T(8,128)(2,1)S(1)} %bitcast.14), channel_id=1, source_target_pairs={{0,2},{1,3},{2,0},{3,1},{4,6},{5,7},{6,4},{7,5},{8,10},{9,11},{10,... | collective-permute-start | bytes 331784 | tf_op jit(solution)/shard_map/ppermute | solution.py:345
  3.4 1.2 %collective-permute-start = (bf16[8,4,2,512]{3,2,1,0:T(2,128)(2,1)S(1)}, bf16[8,4,2,512]{3,2,1,0:T(2,128)(2,1)S(1)}, u32[]{:S(2)}, u32[]{:S(2)}) collective-permute-start(bf16[8,4,2,512]{3,2,1,0:T(2,128)(2,1)S(1)} %copy-done.4), channel_id=1, source_target_pairs={{0,8},{8,0},{16,24},{24,16},{1,9},{9,1},{17,25},{25,17},{2,10},{10... | collective-permute-start | bytes 196616 | tf_op jit(solution)/shard_map/ppermute | solution.py:345
  4.7 1.2 %collective-permute-start.2 = (bf16[8,4,2,512]{3,2,1,0:T(2,128)(2,1)S(1)}, bf16[8,4,2,512]{3,2,1,0:T(2,128)(2,1)S(1)}, u32[]{:S(2)}, u32[]{:S(2)}) collective-permute-start(bf16[8,4,2,512]{3,2,1,0:T(2,128)(2,1)S(1)} %copy-done.4), channel_id=1, source_target_pairs={{0,24},{8,16},{16,8},{24,0},{1,25},{9,17},{17,9},{25,1},{2,26},{10... | collective-permute-start | bytes 196616 | tf_op jit(solution)/shard_map/ppermute | solution.py:345
  6.3 2.2 %collective-permute-start.9 = (bf16[2,3,3,3,8,256]{5,4,3,2,1,0:T(8,128)(2,1)S(1)}, bf16[2,3,3,3,8,256]{5,4,3,2,1,0:T(8,128)(2,1)S(1)}, u32[]{:S(2)}, u32[]{:S(2)}) collective-permute-start(bf16[2,3,3,3,8,256]{5,4,3,2,1,0:T(8,128)(2,1)S(1)} %pad_maximum_fusion.2), channel_id=1, source_target_pairs={{0,4},{1,5},{2,6},{3,7},{4,0},{5,1},{6,2},{7,3},{8,12},{9,13},{10,... | collective-permute-start | bytes 663560 | tf_op jit(solution)/shard_map/ppermute | solution.py:345
  8.6 0.5 %collective-permute-done.2 = bf16[8,4,2,512]{3,2,1,0:T(2,128)(2,1)S(1)} collective-permute-done((bf16[8,4,2,512]{3,2,1,0:T(2,128)(2,1)S(1)}, bf16[8,4,2,512]{3,2,1,0:T(2,128)(2,1)S(1)}, u32[]{:S(2)}, u32[]{:S(2)}) %collective-permute-start.2) | collective-permute-done | bytes 65568 | tf_op jit(solution)/shard_map/ppermute | solution.py:345
  9.4 1.7 %shard_map.64.refs_0_ = bf16[4,128,128]{2,1,0:T(8,128)(2,1)S(1)} custom-call(bf16[4,2,8,512]{3,2,1,0:T(8,128)(2,1)S(1)} %bitcast.18, bf16[4,2,8,512]{3,2,1,0:T(8,128)(2,1)S(1)} %bitcast.20, bf16[4,2,8,512]{3,2,1,0:T(8,128)(2,1)S(1)} %bitcast.24, bf16[4,2,8,512]{3,2,1,0:T(8,128)(2,1)S(1)} %bitcast.22, bf16[3,3,3,512,128]{4,3,2,1,0:T(8,128)(2,1)S(1)} %copy-done), custom_call_target="tpu_custom_call" | custom-call | flops 500000000 | bytes 100000 | tf_op jit(solution)/shard_map/pallas_call | solution.py:22
  11.2 1.5 %collective-permute-start.5 = (bf16[4,128,128]{2,1,0:T(8,128)(2,1)S(1)}, bf16[4,128,128]{2,1,0:T(8,128)(2,1)S(1)}, u32[]{:S(2)}, u32[]{:S(2)}) collective-permute-start(bf16[4,128,128]{2,1,0:T(8,128)(2,1)S(1)} %shard_map.64.refs_0_), channel_id=1, source_target_pairs={{0,24},{8,16},{16,8},{24,0},{1,25},{9,17},{17,9},{25,1},{2,26},{10... | collective-permute-start | bytes 393224 | tf_op jit(solution)/shard_map/ppermute | solution.py:345
  12.6 0.9 %collective-permute-start.4 = (bf16[4,128,128]{2,1,0:T(8,128)(2,1)S(1)}, bf16[4,128,128]{2,1,0:T(8,128)(2,1)S(1)}, u32[]{:S(2)}, u32[]{:S(2)}) collective-permute-start(bf16[4,128,128]{2,1,0:T(8,128)(2,1)S(1)} %shard_map.64.refs_0_), channel_id=1, source_target_pairs={{0,16},{8,24},{16,0},{24,8},{1,17},{9,25},{17,1},{25,9},{2,18},{10... | collective-permute-start | bytes 393224 | tf_op jit(solution)/shard_map/ppermute | solution.py:345
  14.2 2.1 %collective-permute-done.5.refs_3_ = bf16[4,128,128]{2,1,0:T(8,128)(2,1)S(1)} collective-permute-done((bf16[4,128,128]{2,1,0:T(8,128)(2,1)S(1)}, bf16[4,128,128]{2,1,0:T(8,128)(2,1)S(1)}, u32[]{:S(2)}, u32[]{:S(2)}) %collective-permute-start.5) | collective-permute-done | bytes 131104 | tf_op jit(solution)/shard_map/ppermute | solution.py:345
  16.2 1.4 %collective-permute-done.4.refs_2_ = bf16[4,128,128]{2,1,0:T(8,128)(2,1)S(1)} collective-permute-done((bf16[4,128,128]{2,1,0:T(8,128)(2,1)S(1)}, bf16[4,128,128]{2,1,0:T(8,128)(2,1)S(1)}, u32[]{:S(2)}, u32[]{:S(2)}) %collective-permute-start.4) | collective-permute-done | bytes 131104 | tf_op jit(solution)/shard_map/ppermute | solution.py:345
  18.0 0.4 %shard_map.66 = (bf16[2,128,256]{2,1,0:T(8,128)(2,1)S(1)}, bf16[2,128,256]{2,1,0:T(8,128)(2,1)S(1)}, f32[4,128,256]{2,1,0:T(8,128)S(1)}) custom-call(bf16[4,128,128]{2,1,0:T(8,128)(2,1)S(1)} %shard_map.64.refs_0_, bf16[4,128,128]{2,1,0:T(8,128)(2,1)S(1)} %collective-permute-done.3.refs_1_, bf16[4,128,128]{2,1,0:T(8,128)(2,1)S(1)} %collective-permute-done.4.refs_2_, ...), custom_call_target="tpu_custom_call" | custom-call | flops 134217728 | bytes 2000000 | tf_op jit(solution)/shard_map/pallas_call | solution.py:22
  18.4 3.5 %collective-permute-start.10 = (bf16[4,3,3,3,8,256]{5,4,3,2,1,0:T(8,128)(2,1)S(1)}, bf16[4,3,3,3,8,256]{5,4,3,2,1,0:T(8,128)(2,1)S(1)}, u32[]{:S(2)}, u32[]{:S(2)}) collective-permute-start(bf16[4,3,3,3,8,256]{5,4,3,2,1,0:T(8,128)(2,1)S(1)} %pad_maximum_fusion.1), channel_id=1, source_target_pairs={{0,1},{1,0},{2,3},{3,2},{4,5},{5,4},{6,7},{7,6},{8,9},{9,8},{10,11... | collective-permute-start | bytes 1327112 | tf_op jit(solution)/shard_map/ppermute | solution.py:345
  22.0 2.1 %collective-permute-start.6 = (bf16[2,128,256]{2,1,0:T(8,128)(2,1)S(1)}, bf16[2,128,256]{2,1,0:T(8,128)(2,1)S(1)}, u32[]{:S(2)}, u32[]{:S(2)}) collective-permute-start(bf16[2,128,256]{2,1,0:T(8,128)(2,1)S(1)} %get-tuple-element.16), channel_id=1, source_target_pairs={{1,2},{3,4},{5,6},{2,1},{4,3},{6,5},{9,10},{11,12},{13,14},{10,9},... | collective-permute-start | bytes 393224 | tf_op jit(solution)/shard_map/ppermute | solution.py:419
  24.3 0.7 %shard_map.68.filters = bf16[3,3,2,256,256]{4,3,2,1,0:T(8,128)(2,1)S(1)} custom-call(bf16[8,3,3,3,8,256]{5,4,3,2,1,0:T(8,128)(2,1)S(1)} %pad_maximum_fusion.pieces), custom_call_target="tpu_custom_call" | custom-call | flops 1000000 | bytes 4000000 | tf_op jit(solution)/shard_map/pallas_call | solution.py:22
  25.0 3.3 %collective-permute-done.6.odd_in = bf16[2,128,256]{2,1,0:T(8,128)(2,1)S(1)} collective-permute-done((bf16[2,128,256]{2,1,0:T(8,128)(2,1)S(1)}, bf16[2,128,256]{2,1,0:T(8,128)(2,1)S(1)}, u32[]{:S(2)}, u32[]{:S(2)}) %collective-permute-start.6) | collective-permute-done | bytes 131104 | tf_op jit(solution)/shard_map/ppermute | solution.py:419
  28.2 1.3 %shard_map.69 = (bf16[120,256]{1,0:T(8,128)(2,1)S(1)}, bf16[120,256]{1,0:T(8,128)(2,1)S(1)}, bf16[120,256]{1,0:T(8,128)(2,1)S(1)}, bf16[120,256]{1,0:T(8,128)(2,1)S(1)}, bf16[4,48,256]{2,1,0:T(8,128)(2,1)S(1)}) custom-call(bf16[2,128,256]{2,1,0:T(8,128)(2,1)S(1)} %collective-permute-done.6.odd_in, bf16[2,128,256]{2,1,0:T(8,128)(2,1)S(1)} %collective-permute-done.7.even_in, ...), custom_call_target="tpu_custom_call" | custom-call | flops 905969664 | bytes 5000000 | tf_op jit(solution)/shard_map/pallas_call | solution.py:22
  29.5 0.7 %collective-permute-start.11 = (bf16[120,256]{1,0:T(8,128)(2,1)S(1)}, bf16[120,256]{1,0:T(8,128)(2,1)S(1)}, u32[]{:S(2)}, u32[]{:S(2)}) collective-permute-start(bf16[120,256]{1,0:T(8,128)(2,1)S(1)} %get-tuple-element.21), channel_id=1, source_target_pairs={{0,8},{8,0},{16,24},{24,16},{1,9},{9,1},{17,25},{25,17},{2,10},{10... | collective-permute-start | bytes 184328 | tf_op jit(solution)/shard_map/ppermute | solution.py:345
  30.2 0.6 %collective-permute-start.12 = (bf16[120,256]{1,0:T(8,128)(2,1)S(1)}, bf16[120,256]{1,0:T(8,128)(2,1)S(1)}, u32[]{:S(2)}, u32[]{:S(2)}) collective-permute-start(bf16[120,256]{1,0:T(8,128)(2,1)S(1)} %get-tuple-element.22), channel_id=1, source_target_pairs={{0,16},{8,24},{16,0},{24,8},{1,17},{9,25},{17,1},{25,9},{2,18},{10... | collective-permute-start | bytes 184328 | tf_op jit(solution)/shard_map/ppermute | solution.py:345
  30.8 1.5 %collective-permute-start.13 = (bf16[120,256]{1,0:T(8,128)(2,1)S(1)}, bf16[120,256]{1,0:T(8,128)(2,1)S(1)}, u32[]{:S(2)}, u32[]{:S(2)}) collective-permute-start(bf16[120,256]{1,0:T(8,128)(2,1)S(1)} %get-tuple-element.23), channel_id=1, source_target_pairs={{0,24},{8,16},{16,8},{24,0},{1,25},{9,17},{17,9},{25,1},{2,26},{10... | collective-permute-start | bytes 184328 | tf_op jit(solution)/shard_map/ppermute | solution.py:345
  32.6 0.5 %collective-permute-done.11.refs_1_ = bf16[120,256]{1,0:T(8,128)(2,1)S(1)} collective-permute-done((bf16[120,256]{1,0:T(8,128)(2,1)S(1)}, bf16[120,256]{1,0:T(8,128)(2,1)S(1)}, u32[]{:S(2)}, u32[]{:S(2)}) %collective-permute-start.11) | collective-permute-done | bytes 61472 | tf_op jit(solution)/shard_map/ppermute | solution.py:345
  33.1 0.8 %collective-permute-done.12.refs_2_ = bf16[120,256]{1,0:T(8,128)(2,1)S(1)} collective-permute-done((bf16[120,256]{1,0:T(8,128)(2,1)S(1)}, bf16[120,256]{1,0:T(8,128)(2,1)S(1)}, u32[]{:S(2)}, u32[]{:S(2)}) %collective-permute-start.12) | collective-permute-done | bytes 61472 | tf_op jit(solution)/shard_map/ppermute | solution.py:345
  34.0 0.8 %collective-permute-done.13.refs_3_ = bf16[120,256]{1,0:T(8,128)(2,1)S(1)} collective-permute-done((bf16[120,256]{1,0:T(8,128)(2,1)S(1)}, bf16[120,256]{1,0:T(8,128)(2,1)S(1)}, u32[]{:S(2)}, u32[]{:S(2)}) %collective-permute-start.13) | collective-permute-done | bytes 61472 | tf_op jit(solution)/shard_map/ppermute | solution.py:345
  34.8 1.9 %shard_map.71 = bf16[8,16,8,128]{3,2,1,0:T(8,128)(2,1)} custom-call(bf16[120,256]{1,0:T(8,128)(2,1)S(1)} %get-tuple-element.20.refs_0_, bf16[120,256]{1,0:T(8,128)(2,1)S(1)} %collective-permute-done.11.refs_1_, bf16[120,256]{1,0:T(8,128)(2,1)S(1)} %collective-permute-done.12.refs_2_, bf16[120,256]{1,0:T(8,128)(2,1)S(1)} %collective-permute-done.13.refs_3_, ...), custom_call_target="tpu_custom_call" | custom-call | flops 503316480 | bytes 3000000 | tf_op jit(solution)/shard_map/pallas_call | solution.py:22
  (29 shorter events, 2.3 us)
Async XLA Ops:
  0.0 3.4 %copy-start.4 = (bf16[8,4,2,512]{3,2,1,0:T(2,128)(2,1)S(1)}, bf16[8,4,2,512]{3,2,1,0:T(2,128)(2,1)}, u32[]{:S(2)}) copy-start(bf16[8,4,2,512]{3,2,1,0:T(2,128)(2,1)} %param.6) | copy-start | bytes 196612
  0.0 9.4 %copy-start = (bf16[3,3,3,512,128]{4,3,2,1,0:T(8,128)(2,1)S(1)}, bf16[3,3,3,512,128]{4,3,2,1,0:T(8,128)(2,1)}, u32[]{:S(2)}) copy-start(bf16[3,3,3,512,128]{4,3,2,1,0:T(8,128)(2,1)} %refs_4_.3) | copy-start | bytes 10616836
  1.2 12.6 %copy-start.1 = (bf16[512,256]{1,0:T(8,128)(2,1)S(1)}, bf16[512,256]{1,0:T(8,128)(2,1)}, u32[]{:S(2)}) copy-start(bf16[512,256]{1,0:T(8,128)(2,1)} %refs_4_.5) | copy-start | bytes 786436
  1.3 5.0 %collective-permute-start.8 = (bf16[1,3,3,3,8,256]{5,4,3,2,1,0:T(8,128)(2,1)S(1)}, bf16[1,3,3,3,8,256]{5,4,3,2,1,0:T(8,128)(2,1)S(1)}, u32[]{:S(2)}, u32[]{:S(2)}) collective-permute-start(bf16[1,3,3,3,8,256]{5,4,3,2,1,0:T(8,128)(2,1)S(1)} %bitcast.14), channel_id=1, source_target_pairs={{0,2},{1,3},{2,0},{3,1},{4,6},{5,7},{6,4},{7,5},{8,10},{9,11},{10,... | collective-permute-start | bytes 331784 | tf_op jit(solution)/shard_map/ppermute | solution.py:345
  3.4 5.1 %collective-permute-start = (bf16[8,4,2,512]{3,2,1,0:T(2,128)(2,1)S(1)}, bf16[8,4,2,512]{3,2,1,0:T(2,128)(2,1)S(1)}, u32[]{:S(2)}, u32[]{:S(2)}) collective-permute-start(bf16[8,4,2,512]{3,2,1,0:T(2,128)(2,1)S(1)} %copy-done.4), channel_id=1, source_target_pairs={{0,8},{8,0},{16,24},{24,16},{1,9},{9,1},{17,25},{25,17},{2,10},{10... | collective-permute-start | bytes 196616 | tf_op jit(solution)/shard_map/ppermute | solution.py:345
  4.7 4.5 %collective-permute-start.2 = (bf16[8,4,2,512]{3,2,1,0:T(2,128)(2,1)S(1)}, bf16[8,4,2,512]{3,2,1,0:T(2,128)(2,1)S(1)}, u32[]{:S(2)}, u32[]{:S(2)}) collective-permute-start(bf16[8,4,2,512]{3,2,1,0:T(2,128)(2,1)S(1)} %copy-done.4), channel_id=1, source_target_pairs={{0,24},{8,16},{16,8},{24,0},{1,25},{9,17},{17,9},{25,1},{2,26},{10... | collective-permute-start | bytes 196616 | tf_op jit(solution)/shard_map/ppermute | solution.py:345
  5.9 3.5 %collective-permute-start.1 = (bf16[8,4,2,512]{3,2,1,0:T(2,128)(2,1)S(1)}, bf16[8,4,2,512]{3,2,1,0:T(2,128)(2,1)S(1)}, u32[]{:S(2)}, u32[]{:S(2)}) collective-permute-start(bf16[8,4,2,512]{3,2,1,0:T(2,128)(2,1)S(1)} %copy-done.4), channel_id=1, source_target_pairs={{0,16},{8,24},{16,0},{24,8},{1,17},{9,25},{17,1},{25,9},{2,18},{10... | collective-permute-start | bytes 196616 | tf_op jit(solution)/shard_map/ppermute | solution.py:345
  6.3 12.1 %collective-permute-start.9 = (bf16[2,3,3,3,8,256]{5,4,3,2,1,0:T(8,128)(2,1)S(1)}, bf16[2,3,3,3,8,256]{5,4,3,2,1,0:T(8,128)(2,1)S(1)}, u32[]{:S(2)}, u32[]{:S(2)}) collective-permute-start(bf16[2,3,3,3,8,256]{5,4,3,2,1,0:T(8,128)(2,1)S(1)} %pad_maximum_fusion.2), channel_id=1, source_target_pairs={{0,4},{1,5},{2,6},{3,7},{4,0},{5,1},{6,2},{7,3},{8,12},{9,13},{10,... | collective-permute-start | bytes 663560 | tf_op jit(solution)/shard_map/ppermute | solution.py:345
  11.2 5.1 %collective-permute-start.5 = (bf16[4,128,128]{2,1,0:T(8,128)(2,1)S(1)}, bf16[4,128,128]{2,1,0:T(8,128)(2,1)S(1)}, u32[]{:S(2)}, u32[]{:S(2)}) collective-permute-start(bf16[4,128,128]{2,1,0:T(8,128)(2,1)S(1)} %shard_map.64.refs_0_), channel_id=1, source_target_pairs={{0,24},{8,16},{16,8},{24,0},{1,25},{9,17},{17,9},{25,1},{2,26},{10... | collective-permute-start | bytes 393224 | tf_op jit(solution)/shard_map/ppermute | solution.py:345
  12.6 5.0 %collective-permute-start.4 = (bf16[4,128,128]{2,1,0:T(8,128)(2,1)S(1)}, bf16[4,128,128]{2,1,0:T(8,128)(2,1)S(1)}, u32[]{:S(2)}, u32[]{:S(2)}) collective-permute-start(bf16[4,128,128]{2,1,0:T(8,128)(2,1)S(1)} %shard_map.64.refs_0_), channel_id=1, source_target_pairs={{0,16},{8,24},{16,0},{24,8},{1,17},{9,25},{17,1},{25,9},{2,18},{10... | collective-permute-start | bytes 393224 | tf_op jit(solution)/shard_map/ppermute | solution.py:345
  13.5 4.4 %collective-permute-start.3 = (bf16[4,128,128]{2,1,0:T(8,128)(2,1)S(1)}, bf16[4,128,128]{2,1,0:T(8,128)(2,1)S(1)}, u32[]{:S(2)}, u32[]{:S(2)}) collective-permute-start(bf16[4,128,128]{2,1,0:T(8,128)(2,1)S(1)} %shard_map.64.refs_0_), channel_id=1, source_target_pairs={{0,8},{8,0},{16,24},{24,16},{1,9},{9,1},{17,25},{25,17},{2,10},{10... | collective-permute-start | bytes 393224 | tf_op jit(solution)/shard_map/ppermute | solution.py:345
  18.4 5.7 %collective-permute-start.10 = (bf16[4,3,3,3,8,256]{5,4,3,2,1,0:T(8,128)(2,1)S(1)}, bf16[4,3,3,3,8,256]{5,4,3,2,1,0:T(8,128)(2,1)S(1)}, u32[]{:S(2)}, u32[]{:S(2)}) collective-permute-start(bf16[4,3,3,3,8,256]{5,4,3,2,1,0:T(8,128)(2,1)S(1)} %pad_maximum_fusion.1), channel_id=1, source_target_pairs={{0,1},{1,0},{2,3},{3,2},{4,5},{5,4},{6,7},{7,6},{8,9},{9,8},{10,11... | collective-permute-start | bytes 1327112 | tf_op jit(solution)/shard_map/ppermute | solution.py:345
  22.0 6.3 %collective-permute-start.6 = (bf16[2,128,256]{2,1,0:T(8,128)(2,1)S(1)}, bf16[2,128,256]{2,1,0:T(8,128)(2,1)S(1)}, u32[]{:S(2)}, u32[]{:S(2)}) collective-permute-start(bf16[2,128,256]{2,1,0:T(8,128)(2,1)S(1)} %get-tuple-element.16), channel_id=1, source_target_pairs={{1,2},{3,4},{5,6},{2,1},{4,3},{6,5},{9,10},{11,12},{13,14},{10,9},... | collective-permute-start | bytes 393224 | tf_op jit(solution)/shard_map/ppermute | solution.py:419
  24.1 4.2 %collective-permute-start.7 = (bf16[2,128,256]{2,1,0:T(8,128)(2,1)S(1)}, bf16[2,128,256]{2,1,0:T(8,128)(2,1)S(1)}, u32[]{:S(2)}, u32[]{:S(2)}) collective-permute-start(bf16[2,128,256]{2,1,0:T(8,128)(2,1)S(1)} %get-tuple-element.17), channel_id=1, source_target_pairs={{0,1},{1,0},{2,3},{3,2},{4,5},{5,4},{6,7},{7,6},{8,9},{9,8},{10,11... | collective-permute-start | bytes 393224 | tf_op jit(solution)/shard_map/ppermute | solution.py:345
  24.9 7.3 %copy-start.2 = (bf16[3,3,3,128,128]{4,3,2,1,0:T(8,128)(2,1)S(1)}, bf16[3,3,3,128,128]{4,3,2,1,0:T(8,128)(2,1)}, u32[]{:S(2)}) copy-start(bf16[3,3,3,128,128]{4,3,2,1,0:T(8,128)(2,1)} %filters.1) | copy-start | bytes 2654212
  25.0 7.3 %copy-start.3 = (bf16[256,128]{1,0:T(8,128)(2,1)S(1)}, bf16[256,128]{1,0:T(8,128)(2,1)}, u32[]{:S(2)}) copy-start(bf16[256,128]{1,0:T(8,128)(2,1)} %refs_6_.1) | copy-start | bytes 196612
  29.5 3.6 %collective-permute-start.11 = (bf16[120,256]{1,0:T(8,128)(2,1)S(1)}, bf16[120,256]{1,0:T(8,128)(2,1)S(1)}, u32[]{:S(2)}, u32[]{:S(2)}) collective-permute-start(bf16[120,256]{1,0:T(8,128)(2,1)S(1)} %get-tuple-element.21), channel_id=1, source_target_pairs={{0,8},{8,0},{16,24},{24,16},{1,9},{9,1},{17,25},{25,17},{2,10},{10... | collective-permute-start | bytes 184328 | tf_op jit(solution)/shard_map/ppermute | solution.py:345
  30.2 3.8 %collective-permute-start.12 = (bf16[120,256]{1,0:T(8,128)(2,1)S(1)}, bf16[120,256]{1,0:T(8,128)(2,1)S(1)}, u32[]{:S(2)}, u32[]{:S(2)}) collective-permute-start(bf16[120,256]{1,0:T(8,128)(2,1)S(1)} %get-tuple-element.22), channel_id=1, source_target_pairs={{0,16},{8,24},{16,0},{24,8},{1,17},{9,25},{17,1},{25,9},{2,18},{10... | collective-permute-start | bytes 184328 | tf_op jit(solution)/shard_map/ppermute | solution.py:345
  30.8 4.0 %collective-permute-start.13 = (bf16[120,256]{1,0:T(8,128)(2,1)S(1)}, bf16[120,256]{1,0:T(8,128)(2,1)S(1)}, u32[]{:S(2)}, u32[]{:S(2)}) collective-permute-start(bf16[120,256]{1,0:T(8,128)(2,1)S(1)} %get-tuple-element.23), channel_id=1, source_target_pairs={{0,24},{8,16},{16,8},{24,0},{1,25},{9,17},{17,9},{25,1},{2,26},{10... | collective-permute-start | bytes 184328 | tf_op jit(solution)/shard_map/ppermute | solution.py:345

commit v5 on v4

--- a/solution.py
+++ b/solution.py
@@ -185,8 +185,12 @@
         outs[k][...] = chunk.reshape(pairs * (rows + 1) * frames, lanes).astype(BF16)
 
 
+def chunk_order(groups):
+    return [0, *range(2, groups), 1]
+
+
 def fine_kernel(groups, frames, *refs):
-    chunks = refs[:groups]
+    chunks = dict(zip(chunk_order(groups), refs[:groups]))
     block, spread, proj, filters, out, acts, acts_odd, lows = refs[groups:]
     extent, cells = block.shape[:2]
     pairs, rows = extent - 1, cells // frames - 2
@@ -373,11 +377,8 @@
             mid_rows,
             stay=(0,),
         )
-        mine, bit = mine[None], 2
-        while 2 * bit < tiles:
-            mine = jnp.concatenate([mine, exchange(mine, "tile", bit)])
-            bit *= 2
-        beyond = exchange(mine, "tile", bit)
+        near = [exchange(mine, "tile", k) for k in range(4, tiles, 2)]
+        gathered = jnp.stack([mine, *near])
     else:
         every = lax.all_gather(mid_rows, "tile", axis=3, tiled=True)
         mine = lax.dynamic_slice_in_dim(every, me * share, share, axis=3)[None]
@@ -401,6 +402,9 @@
         coarse_proj,
     )
     parts = [part] + [exchange(part, "grp", k) for k in range(1, groups)]
+    if divided:
+        later, _ = lax.optimization_barrier((mine, part))
+        beyond = exchange(later, "tile", 2)
     odd_out, even_out, own = call(
         functools.partial(project_kernel, groups),
         (
@@ -419,8 +423,8 @@
     odd_in = lax.ppermute(odd_out, "tile", odd_pairs + [(j, i) for i, j in odd_pairs])
     even_in = exchange(even_out, "tile", 1)
     if divided:
-        beyond, _ = lax.optimization_barrier((beyond, own))
-        mine = jnp.concatenate([mine, beyond])
+        gathered, beyond, _ = lax.optimization_barrier((gathered, beyond, own))
+        mine = jnp.concatenate([gathered[:1], beyond[None], gathered[1:]])
         mine = jnp.concatenate([mine, exchange(mine, "tile", 1)])
     mid_folded = call(
         fold_middle_kernel,
@@ -475,7 +479,7 @@
         ],
         2 * 24 * (broad + 1) * tall * frames * depth2 * 2 * depth2,
         3 * 10**6,
-        *chunks,
+        *[chunks[k] for k in chunk_order(groups)],
         block,
         spread,
         mid_proj,

time: 37.1 us -> 36.5 us (0.984)
  waiting for transfers between devices: 10.1 us -> 8.34 us
  starting transfers between devices: 18.2 us -> 19.2 us
    ppermute x1, starting transfers between devices: 2.11 us -> 3.36 us  [body(): lax.ppermute(odd_out, 'tile', odd_pairs + [(j, i) for i, j in odd_pairs])]
    ppermute x1, waiting for transfers between devices: 3.27 us -> 2.03 us  [body(): lax.ppermute(odd_out, 'tile', odd_pairs + [(j, i) for i, j in odd_pairs])]
    ppermute x13 -> x14, waiting for transfers between devices: 6.83 us -> 6.31 us  [exchange(): return lax.ppermute(values, axis, [(i, i ^ k) for i in range(size)])]
    ppermute x13 -> x14, starting transfers between devices: 16.1 us -> 15.9 us  [exchange(): return lax.ppermute(values, axis, [(i, i ^ k) for i in range(size)])]
  transfers between devices with their start and end apart: 14 -> 15, of which waited for: 10 -> 6; matrix products, arithmetic and copies ran while one was open for 1% -> 1% of each run, Pallas kernels for 10% -> 13%
where the time goes in v5:
time: 36.5 us; the launch traced here: 36 us
  starting transfers between devices  19.2 us (53%)
  waiting for transfers between devices  8.34 us (23%)
  Pallas kernels  7.93 us (22%)
    ppermute x14, starting transfers between devices, exchange(): return lax.ppermute(values, axis, [(i, i ^ k) for i in range(size)])  15.9 us
    pallas_call x8, Pallas kernels, call(): pl.pallas_call(kernel, out_shape=outs, in_specs=[FAR if n in stay else VM...  7.93 us
    ppermute x14, waiting for transfers between devices, exchange(): return lax.ppermute(values, axis, [(i, i ^ k) for i in range(size)])  6.31 us
    ppermute x1, starting transfers between devices, body(): lax.ppermute(odd_out, 'tile', odd_pairs + [(j, i) for i, j in odd_pairs])  3.36 us
    ppermute x1, waiting for transfers between devices, body(): lax.ppermute(odd_out, 'tile', odd_pairs + [(j, i) for i, j in odd_pairs])  2.03 us
  transfers between devices with their start and end apart: 15, of which 6 were waited for; matrix products, arithmetic and copies ran while one was open for 1% of the time, Pallas kernels for 13%

profile of v5, /device:TPU:1, one launch (start us, length us, event | category | flops | bytes accessed | tf_op | source)
XLA Modules:
  0.0 36.0 jit_solution(14156723351565111683)
XLA Ops:
  0.0 2.0 %collective-permute-start = (bf16[8,4,2,512]{3,2,1,0:T(2,128)(2,1)}, bf16[8,4,2,512]{3,2,1,0:T(2,128)(2,1)S(1)}, u32[]{:S(2)}, u32[]{:S(2)}) collective-permute-start(bf16[8,4,2,512]{3,2,1,0:T(2,128)(2,1)} %param.6), channel_id=1, source_target_pairs={{0,8},{8,0},{16,24},{24,16},{1,9},{9,1},{17,25},{25,17},{2,10},{10... | collective-permute-start | bytes 196616 | tf_op jit(solution)/shard_map/ppermute | solution.py:349
  2.0 1.2 %collective-permute-start.2 = (bf16[8,4,2,512]{3,2,1,0:T(2,128)(2,1)}, bf16[8,4,2,512]{3,2,1,0:T(2,128)(2,1)S(1)}, u32[]{:S(2)}, u32[]{:S(2)}) collective-permute-start(bf16[8,4,2,512]{3,2,1,0:T(2,128)(2,1)} %param.6), channel_id=1, source_target_pairs={{0,24},{8,16},{16,8},{24,0},{1,25},{9,17},{17,9},{25,1},{2,26},{10... | collective-permute-start | bytes 196616 | tf_op jit(solution)/shard_map/ppermute | solution.py:349
  3.3 1.2 %shard_map.67 = bf16[3,3,3,8,256]{4,3,2,1,0:T(8,128)(2,1)S(1)} custom-call(bf16[3,3,3,32,256]{4,3,2,1,0:T(8,128)(2,1)} %bitcast.30), custom_call_target="tpu_custom_call" | custom-call | flops 6000000000 | bytes 1000000 | tf_op jit(solution)/shard_map/pallas_call | solution.py:22
  4.5 3.6 %collective-permute-start.9 = (bf16[3,3,3,8,256]{4,3,2,1,0:T(8,128)(2,1)S(1)}, bf16[3,3,3,8,256]{4,3,2,1,0:T(8,128)(2,1)S(1)}, u32[]{:S(2)}, u32[]{:S(2)}) collective-permute-start(bf16[3,3,3,8,256]{4,3,2,1,0:T(8,128)(2,1)S(1)} %shard_map.67), channel_id=1, source_target_pairs={{0,6},{1,7},{2,4},{3,5},{4,2},{5,3},{6,0},{7,1},{8,14},{9,15},{10,... | collective-permute-start | bytes 331784 | tf_op jit(solution)/shard_map/ppermute | solution.py:349
  8.3 1.7 %shard_map.64.refs_0_ = bf16[4,128,128]{2,1,0:T(8,128)(2,1)S(1)} custom-call(bf16[4,2,8,512]{3,2,1,0:T(8,128)(2,1)S(1)} %bitcast.17, bf16[4,2,8,512]{3,2,1,0:T(8,128)(2,1)S(1)} %bitcast.19, bf16[4,2,8,512]{3,2,1,0:T(8,128)(2,1)S(1)} %bitcast.23, bf16[4,2,8,512]{3,2,1,0:T(8,128)(2,1)S(1)} %bitcast.21, bf16[3,3,3,512,128]{4,3,2,1,0:T(8,128)(2,1)S(1)} %copy-done), custom_call_target="tpu_custom_call" | custom-call | flops 500000000 | bytes 100000 | tf_op jit(solution)/shard_map/pallas_call | solution.py:22
  10.0 2.2 %collective-permute-start.5 = (bf16[4,128,128]{2,1,0:T(8,128)(2,1)S(1)}, bf16[4,128,128]{2,1,0:T(8,128)(2,1)S(1)}, u32[]{:S(2)}, u32[]{:S(2)}) collective-permute-start(bf16[4,128,128]{2,1,0:T(8,128)(2,1)S(1)} %shard_map.64.refs_0_), channel_id=1, source_target_pairs={{0,24},{8,16},{16,8},{24,0},{1,25},{9,17},{17,9},{25,1},{2,26},{10... | collective-permute-start | bytes 393224 | tf_op jit(solution)/shard_map/ppermute | solution.py:349
  12.5 0.3 collective-permute-start.3
  12.7 0.3 shard_map.65.refs_5_
  13.0 1.9 %collective-permute-start.10 = (bf16[3,3,3,8,256]{4,3,2,1,0:T(8,128)(2,1)S(1)}, bf16[3,3,3,8,256]{4,3,2,1,0:T(8,128)(2,1)S(1)}, u32[]{:S(2)}, u32[]{:S(2)}) collective-permute-start(bf16[3,3,3,8,256]{4,3,2,1,0:T(8,128)(2,1)S(1)} %shard_map.67), channel_id=1, source_target_pairs={{0,2},{1,3},{2,0},{3,1},{4,6},{5,7},{6,4},{7,5},{8,10},{9,11},{10,... | collective-permute-start | bytes 331784 | tf_op jit(solution)/shard_map/ppermute | solution.py:349
  14.9 2.1 %collective-permute-done.8 = bf16[3,3,3,8,256]{4,3,2,1,0:T(8,128)(2,1)S(1)} collective-permute-done((bf16[3,3,3,8,256]{4,3,2,1,0:T(8,128)(2,1)S(1)}, bf16[3,3,3,8,256]{4,3,2,1,0:T(8,128)(2,1)S(1)}, u32[]{:S(2)}, u32[]{:S(2)}) %collective-permute-start.8) | collective-permute-done | bytes 110624 | tf_op jit(solution)/shard_map/ppermute | solution.py:349
  17.2 0.4 %shard_map.66 = (bf16[2,128,256]{2,1,0:T(8,128)(2,1)S(1)}, bf16[2,128,256]{2,1,0:T(8,128)(2,1)S(1)}, f32[4,128,256]{2,1,0:T(8,128)S(1)}) custom-call(bf16[4,128,128]{2,1,0:T(8,128)(2,1)S(1)} %shard_map.64.refs_0_, bf16[4,128,128]{2,1,0:T(8,128)(2,1)S(1)} %collective-permute-done.3.refs_1_, bf16[4,128,128]{2,1,0:T(8,128)(2,1)S(1)} %collective-permute-done.4.refs_2_, ...), custom_call_target="tpu_custom_call" | custom-call | flops 134217728 | bytes 2000000 | tf_op jit(solution)/shard_map/pallas_call | solution.py:22
  17.7 1.3 %collective-permute-done.10 = bf16[3,3,3,8,256]{4,3,2,1,0:T(8,128)(2,1)S(1)} collective-permute-done((bf16[3,3,3,8,256]{4,3,2,1,0:T(8,128)(2,1)S(1)}, bf16[3,3,3,8,256]{4,3,2,1,0:T(8,128)(2,1)S(1)}, u32[]{:S(2)}, u32[]{:S(2)}) %collective-permute-start.10) | collective-permute-done | bytes 110624 | tf_op jit(solution)/shard_map/ppermute | solution.py:349
  19.0 1.6 %collective-permute-start.11 = (bf16[4,3,3,3,8,256]{5,4,3,2,1,0:T(8,128)(2,1)S(1)}, bf16[4,3,3,3,8,256]{5,4,3,2,1,0:T(8,128)(2,1)S(1)}, u32[]{:S(2)}, u32[]{:S(2)}) collective-permute-start(bf16[4,3,3,3,8,256]{5,4,3,2,1,0:T(8,128)(2,1)S(1)} %pad_maximum_fusion.1), channel_id=1, source_target_pairs={{0,1},{1,0},{2,3},{3,2},{4,5},{5,4},{6,7},{7,6},{8,9},{9,8},{10,11... | collective-permute-start | bytes 1327112 | tf_op jit(solution)/shard_map/ppermute | solution.py:349
  20.7 3.4 %collective-permute-start.6 = (bf16[2,128,256]{2,1,0:T(8,128)(2,1)S(1)}, bf16[2,128,256]{2,1,0:T(8,128)(2,1)S(1)}, u32[]{:S(2)}, u32[]{:S(2)}) collective-permute-start(bf16[2,128,256]{2,1,0:T(8,128)(2,1)S(1)} %get-tuple-element.18), channel_id=1, source_target_pairs={{1,2},{3,4},{5,6},{2,1},{4,3},{6,5},{9,10},{11,12},{13,14},{10,9},... | collective-permute-start | bytes 393224 | tf_op jit(solution)/shard_map/ppermute | solution.py:423
  24.2 0.7 %shard_map.68.filters = bf16[3,3,2,256,256]{4,3,2,1,0:T(8,128)(2,1)S(1)} custom-call(bf16[8,3,3,3,8,256]{5,4,3,2,1,0:T(8,128)(2,1)S(1)} %pad_maximum_fusion.pieces), custom_call_target="tpu_custom_call" | custom-call | flops 1000000 | bytes 4000000 | tf_op jit(solution)/shard_map/pallas_call | solution.py:22
  24.9 2.0 %collective-permute-done.6.odd_in = bf16[2,128,256]{2,1,0:T(8,128)(2,1)S(1)} collective-permute-done((bf16[2,128,256]{2,1,0:T(8,128)(2,1)S(1)}, bf16[2,128,256]{2,1,0:T(8,128)(2,1)S(1)}, u32[]{:S(2)}, u32[]{:S(2)}) %collective-permute-start.6) | collective-permute-done | bytes 131104 | tf_op jit(solution)/shard_map/ppermute | solution.py:423
  27.0 1.3 %shard_map.69 = (bf16[120,256]{1,0:T(8,128)(2,1)S(1)}, bf16[120,256]{1,0:T(8,128)(2,1)S(1)}, bf16[120,256]{1,0:T(8,128)(2,1)S(1)}, bf16[120,256]{1,0:T(8,128)(2,1)S(1)}, bf16[4,48,256]{2,1,0:T(8,128)(2,1)S(1)}) custom-call(bf16[2,128,256]{2,1,0:T(8,128)(2,1)S(1)} %collective-permute-done.6.odd_in, bf16[2,128,256]{2,1,0:T(8,128)(2,1)S(1)} %collective-permute-done.7.even_in, ...), custom_call_target="tpu_custom_call" | custom-call | flops 905969664 | bytes 5000000 | tf_op jit(solution)/shard_map/pallas_call | solution.py:22
  28.2 1.3 %collective-permute-start.12 = (bf16[120,256]{1,0:T(8,128)(2,1)S(1)}, bf16[120,256]{1,0:T(8,128)(2,1)S(1)}, u32[]{:S(2)}, u32[]{:S(2)}) collective-permute-start(bf16[120,256]{1,0:T(8,128)(2,1)S(1)} %get-tuple-element.25), channel_id=1, source_target_pairs={{0,16},{8,24},{16,0},{24,8},{1,17},{9,25},{17,1},{25,9},{2,18},{10... | collective-permute-start | bytes 184328 | tf_op jit(solution)/shard_map/ppermute | solution.py:349
  29.5 1.2 %collective-permute-start.13 = (bf16[120,256]{1,0:T(8,128)(2,1)S(1)}, bf16[120,256]{1,0:T(8,128)(2,1)S(1)}, u32[]{:S(2)}, u32[]{:S(2)}) collective-permute-start(bf16[120,256]{1,0:T(8,128)(2,1)S(1)} %get-tuple-element.26), channel_id=1, source_target_pairs={{0,24},{8,16},{16,8},{24,0},{1,25},{9,17},{17,9},{25,1},{2,26},{10... | collective-permute-start | bytes 184328 | tf_op jit(solution)/shard_map/ppermute | solution.py:349
  30.7 0.3 collective-permute-start.14
  31.0 0.4 %shard_map.70 = (bf16[3,2,2,256,256]{4,3,2,1,0:T(8,128)(2,1)S(1)}, bf16[4,256,512]{2,1,0:T(8,128)(2,1)S(1)}) custom-call(bf16[3,3,3,128,128]{4,3,2,1,0:T(8,128)(2,1)S(1)} %copy-done.2, bf16[256,128]{1,0:T(8,128)(2,1)S(1)} %copy-done.3), custom_call_target="tpu_custom_call" | custom-call | flops 1000000 | bytes 4000000 | tf_op jit(solution)/shard_map/pallas_call | solution.py:22
  31.4 2.2 %collective-permute-done.13.refs_2_ = bf16[120,256]{1,0:T(8,128)(2,1)S(1)} collective-permute-done((bf16[120,256]{1,0:T(8,128)(2,1)S(1)}, bf16[120,256]{1,0:T(8,128)(2,1)S(1)}, u32[]{:S(2)}, u32[]{:S(2)}) %collective-permute-start.13) | collective-permute-done | bytes 61472 | tf_op jit(solution)/shard_map/ppermute | solution.py:349
  33.6 0.5 %collective-permute-done.14.refs_3_ = bf16[120,256]{1,0:T(8,128)(2,1)S(1)} collective-permute-done((bf16[120,256]{1,0:T(8,128)(2,1)S(1)}, bf16[120,256]{1,0:T(8,128)(2,1)S(1)}, u32[]{:S(2)}, u32[]{:S(2)}) %collective-permute-start.14) | collective-permute-done | bytes 61472 | tf_op jit(solution)/shard_map/ppermute | solution.py:349
  34.1 1.9 %shard_map.71 = bf16[8,16,8,128]{3,2,1,0:T(8,128)(2,1)} custom-call(bf16[120,256]{1,0:T(8,128)(2,1)S(1)} %get-tuple-element.24.refs_0_, bf16[120,256]{1,0:T(8,128)(2,1)S(1)} %collective-permute-done.12.refs_1_, bf16[120,256]{1,0:T(8,128)(2,1)S(1)} %collective-permute-done.13.refs_2_, bf16[120,256]{1,0:T(8,128)(2,1)S(1)} %collective-permute-done.14.refs_3_, ...), custom_call_target="tpu_custom_call" | custom-call | flops 503316480 | bytes 3000000 | tf_op jit(solution)/shard_map/pallas_call | solution.py:22
  (33 shorter events, 0.9 us)
Async XLA Ops:
  0.0 8.2 %collective-permute-start = (bf16[8,4,2,512]{3,2,1,0:T(2,128)(2,1)}, bf16[8,4,2,512]{3,2,1,0:T(2,128)(2,1)S(1)}, u32[]{:S(2)}, u32[]{:S(2)}) collective-permute-start(bf16[8,4,2,512]{3,2,1,0:T(2,128)(2,1)} %param.6), channel_id=1, source_target_pairs={{0,8},{8,0},{16,24},{24,16},{1,9},{9,1},{17,25},{25,17},{2,10},{10... | collective-permute-start | bytes 196616 | tf_op jit(solution)/shard_map/ppermute | solution.py:349
  2.0 6.2 %collective-permute-start.2 = (bf16[8,4,2,512]{3,2,1,0:T(2,128)(2,1)}, bf16[8,4,2,512]{3,2,1,0:T(2,128)(2,1)S(1)}, u32[]{:S(2)}, u32[]{:S(2)}) collective-permute-start(bf16[8,4,2,512]{3,2,1,0:T(2,128)(2,1)} %param.6), channel_id=1, source_target_pairs={{0,24},{8,16},{16,8},{24,0},{1,25},{9,17},{17,9},{25,1},{2,26},{10... | collective-permute-start | bytes 196616 | tf_op jit(solution)/shard_map/ppermute | solution.py:349
  3.3 5.0 %collective-permute-start.1 = (bf16[8,4,2,512]{3,2,1,0:T(2,128)(2,1)}, bf16[8,4,2,512]{3,2,1,0:T(2,128)(2,1)S(1)}, u32[]{:S(2)}, u32[]{:S(2)}) collective-permute-start(bf16[8,4,2,512]{3,2,1,0:T(2,128)(2,1)} %param.6), channel_id=1, source_target_pairs={{0,16},{8,24},{16,0},{24,8},{1,17},{9,25},{17,1},{25,9},{2,18},{10... | collective-permute-start | bytes 196616 | tf_op jit(solution)/shard_map/ppermute | solution.py:349
  3.3 4.8 %copy-start.4 = (bf16[8,4,2,512]{3,2,1,0:T(2,128)(2,1)S(1)}, bf16[8,4,2,512]{3,2,1,0:T(2,128)(2,1)}, u32[]{:S(2)}) copy-start(bf16[8,4,2,512]{3,2,1,0:T(2,128)(2,1)} %param.6) | copy-start | bytes 196612
  3.3 5.0 %copy-start = (bf16[3,3,3,512,128]{4,3,2,1,0:T(8,128)(2,1)S(1)}, bf16[3,3,3,512,128]{4,3,2,1,0:T(8,128)(2,1)}, u32[]{:S(2)}) copy-start(bf16[3,3,3,512,128]{4,3,2,1,0:T(8,128)(2,1)} %refs_4_.3) | copy-start | bytes 10616836
  4.5 8.2 %copy-start.1 = (bf16[512,256]{1,0:T(8,128)(2,1)S(1)}, bf16[512,256]{1,0:T(8,128)(2,1)}, u32[]{:S(2)}) copy-start(bf16[512,256]{1,0:T(8,128)(2,1)} %refs_4_.5) | copy-start | bytes 786436
  4.5 8.5 %collective-permute-start.9 = (bf16[3,3,3,8,256]{4,3,2,1,0:T(8,128)(2,1)S(1)}, bf16[3,3,3,8,256]{4,3,2,1,0:T(8,128)(2,1)S(1)}, u32[]{:S(2)}, u32[]{:S(2)}) collective-permute-start(bf16[3,3,3,8,256]{4,3,2,1,0:T(8,128)(2,1)S(1)} %shard_map.67), channel_id=1, source_target_pairs={{0,6},{1,7},{2,4},{3,5},{4,2},{5,3},{6,0},{7,1},{8,14},{9,15},{10,... | collective-permute-start | bytes 331784 | tf_op jit(solution)/shard_map/ppermute | solution.py:349
  8.1 8.9 %collective-permute-start.8 = (bf16[3,3,3,8,256]{4,3,2,1,0:T(8,128)(2,1)S(1)}, bf16[3,3,3,8,256]{4,3,2,1,0:T(8,128)(2,1)S(1)}, u32[]{:S(2)}, u32[]{:S(2)}) collective-permute-start(bf16[3,3,3,8,256]{4,3,2,1,0:T(8,128)(2,1)S(1)} %shard_map.67), channel_id=1, source_target_pairs={{0,4},{1,5},{2,6},{3,7},{4,0},{5,1},{6,2},{7,3},{8,12},{9,13},{10,... | collective-permute-start | bytes 331784 | tf_op jit(solution)/shard_map/ppermute | solution.py:349
  10.0 7.0 %collective-permute-start.5 = (bf16[4,128,128]{2,1,0:T(8,128)(2,1)S(1)}, bf16[4,128,128]{2,1,0:T(8,128)(2,1)S(1)}, u32[]{:S(2)}, u32[]{:S(2)}) collective-permute-start(bf16[4,128,128]{2,1,0:T(8,128)(2,1)S(1)} %shard_map.64.refs_0_), channel_id=1, source_target_pairs={{0,24},{8,16},{16,8},{24,0},{1,25},{9,17},{17,9},{25,1},{2,26},{10... | collective-permute-start | bytes 393224 | tf_op jit(solution)/shard_map/ppermute | solution.py:349
  12.2 5.0 %collective-permute-start.4 = (bf16[4,128,128]{2,1,0:T(8,128)(2,1)S(1)}, bf16[4,128,128]{2,1,0:T(8,128)(2,1)S(1)}, u32[]{:S(2)}, u32[]{:S(2)}) collective-permute-start(bf16[4,128,128]{2,1,0:T(8,128)(2,1)S(1)} %shard_map.64.refs_0_), channel_id=1, source_target_pairs={{0,16},{8,24},{16,0},{24,8},{1,17},{9,25},{17,1},{25,9},{2,18},{10... | collective-permute-start | bytes 393224 | tf_op jit(solution)/shard_map/ppermute | solution.py:349
  12.5 4.8 %collective-permute-start.3 = (bf16[4,128,128]{2,1,0:T(8,128)(2,1)S(1)}, bf16[4,128,128]{2,1,0:T(8,128)(2,1)S(1)}, u32[]{:S(2)}, u32[]{:S(2)}) collective-permute-start(bf16[4,128,128]{2,1,0:T(8,128)(2,1)S(1)} %shard_map.64.refs_0_), channel_id=1, source_target_pairs={{0,8},{8,0},{16,24},{24,16},{1,9},{9,1},{17,25},{25,17},{2,10},{10... | collective-permute-start | bytes 393224 | tf_op jit(solution)/shard_map/ppermute | solution.py:349
  13.0 5.9 %collective-permute-start.10 = (bf16[3,3,3,8,256]{4,3,2,1,0:T(8,128)(2,1)S(1)}, bf16[3,3,3,8,256]{4,3,2,1,0:T(8,128)(2,1)S(1)}, u32[]{:S(2)}, u32[]{:S(2)}) collective-permute-start(bf16[3,3,3,8,256]{4,3,2,1,0:T(8,128)(2,1)S(1)} %shard_map.67), channel_id=1, source_target_pairs={{0,2},{1,3},{2,0},{3,1},{4,6},{5,7},{6,4},{7,5},{8,10},{9,11},{10,... | collective-permute-start | bytes 331784 | tf_op jit(solution)/shard_map/ppermute | solution.py:349
  19.0 5.1 %collective-permute-start.11 = (bf16[4,3,3,3,8,256]{5,4,3,2,1,0:T(8,128)(2,1)S(1)}, bf16[4,3,3,3,8,256]{5,4,3,2,1,0:T(8,128)(2,1)S(1)}, u32[]{:S(2)}, u32[]{:S(2)}) collective-permute-start(bf16[4,3,3,3,8,256]{5,4,3,2,1,0:T(8,128)(2,1)S(1)} %pad_maximum_fusion.1), channel_id=1, source_target_pairs={{0,1},{1,0},{2,3},{3,2},{4,5},{5,4},{6,7},{7,6},{8,9},{9,8},{10,11... | collective-permute-start | bytes 1327112 | tf_op jit(solution)/shard_map/ppermute | solution.py:349
  20.7 6.3 %collective-permute-start.6 = (bf16[2,128,256]{2,1,0:T(8,128)(2,1)S(1)}, bf16[2,128,256]{2,1,0:T(8,128)(2,1)S(1)}, u32[]{:S(2)}, u32[]{:S(2)}) collective-permute-start(bf16[2,128,256]{2,1,0:T(8,128)(2,1)S(1)} %get-tuple-element.18), channel_id=1, source_target_pairs={{1,2},{3,4},{5,6},{2,1},{4,3},{6,5},{9,10},{11,12},{13,14},{10,9},... | collective-permute-start | bytes 393224 | tf_op jit(solution)/shard_map/ppermute | solution.py:423
  24.0 2.9 %collective-permute-start.7 = (bf16[2,128,256]{2,1,0:T(8,128)(2,1)S(1)}, bf16[2,128,256]{2,1,0:T(8,128)(2,1)S(1)}, u32[]{:S(2)}, u32[]{:S(2)}) collective-permute-start(bf16[2,128,256]{2,1,0:T(8,128)(2,1)S(1)} %get-tuple-element.19), channel_id=1, source_target_pairs={{0,1},{1,0},{2,3},{3,2},{4,5},{5,4},{6,7},{7,6},{8,9},{9,8},{10,11... | collective-permute-start | bytes 393224 | tf_op jit(solution)/shard_map/ppermute | solution.py:349
  24.9 6.1 %copy-start.2 = (bf16[3,3,3,128,128]{4,3,2,1,0:T(8,128)(2,1)S(1)}, bf16[3,3,3,128,128]{4,3,2,1,0:T(8,128)(2,1)}, u32[]{:S(2)}) copy-start(bf16[3,3,3,128,128]{4,3,2,1,0:T(8,128)(2,1)} %filters.1) | copy-start | bytes 2654212
  24.9 6.1 %copy-start.3 = (bf16[256,128]{1,0:T(8,128)(2,1)S(1)}, bf16[256,128]{1,0:T(8,128)(2,1)}, u32[]{:S(2)}) copy-start(bf16[256,128]{1,0:T(8,128)(2,1)} %refs_6_.1) | copy-start | bytes 196612
  28.2 3.1 %collective-permute-start.12 = (bf16[120,256]{1,0:T(8,128)(2,1)S(1)}, bf16[120,256]{1,0:T(8,128)(2,1)S(1)}, u32[]{:S(2)}, u32[]{:S(2)}) collective-permute-start(bf16[120,256]{1,0:T(8,128)(2,1)S(1)} %get-tuple-element.25), channel_id=1, source_target_pairs={{0,16},{8,24},{16,0},{24,8},{1,17},{9,25},{17,1},{25,9},{2,18},{10... | collective-permute-start | bytes 184328 | tf_op jit(solution)/shard_map/ppermute | solution.py:349
  29.5 4.0 %collective-permute-start.13 = (bf16[120,256]{1,0:T(8,128)(2,1)S(1)}, bf16[120,256]{1,0:T(8,128)(2,1)S(1)}, u32[]{:S(2)}, u32[]{:S(2)}) collective-permute-start(bf16[120,256]{1,0:T(8,128)(2,1)S(1)} %get-tuple-element.26), channel_id=1, source_target_pairs={{0,24},{8,16},{16,8},{24,0},{1,25},{9,17},{17,9},{25,1},{2,26},{10... | collective-permute-start | bytes 184328 | tf_op jit(solution)/shard_map/ppermute | solution.py:349
  30.7 3.4 %collective-permute-start.14 = (bf16[120,256]{1,0:T(8,128)(2,1)S(1)}, bf16[120,256]{1,0:T(8,128)(2,1)S(1)}, u32[]{:S(2)}, u32[]{:S(2)}) collective-permute-start(bf16[120,256]{1,0:T(8,128)(2,1)S(1)} %get-tuple-element.27), channel_id=1, source_target_pairs={{0,8},{8,0},{16,24},{24,16},{1,9},{9,1},{17,25},{25,17},{2,10},{10... | collective-permute-start | bytes 184328 | tf_op jit(solution)/shard_map/ppermute | solution.py:349

commit v6 on v5

--- a/solution.py
+++ b/solution.py
@@ -97,7 +97,9 @@
 
 
 def project_kernel(groups, *refs):
-    parts, (proj, straight, odd_out, even_out, own) = refs[:groups], refs[groups:]
+    parts, (proj, straight), (odd_out, even_out, own) = (
+        refs[:groups], refs[groups : groups + 2], refs[-3:],
+    )
     extent, cells, width = parts[0].shape
     outputs = proj.shape[1]
     me = lax.axis_index("grp")
@@ -359,6 +361,7 @@
     cells = height * frames
     own_mid = mid_filters.shape[4]
 
+    early = []
     divided = own_mid % groups == 0 and (own_mid // groups) % 8 == 0
     share, shares = (own_mid // groups, tiles) if divided else (depth1 // groups, 1)
     lanes = 4 * shares * share
@@ -379,6 +382,7 @@
         )
         near = [exchange(mine, "tile", k) for k in range(4, tiles, 2)]
         gathered = jnp.stack([mine, *near])
+        early = [exchange(gathered, "tile", 1)]
     else:
         every = lax.all_gather(mid_rows, "tile", axis=3, tiled=True)
         mine = lax.dynamic_slice_in_dim(every, me * share, share, axis=3)[None]
@@ -387,7 +391,7 @@
         functools.partial(coarse_kernel, groups),
         jax.ShapeDtypeStruct((cols + 2, cells, width0), BF16),
         [pltpu.VMEM((3, height + 2, cols * frames, depth0), BF16)],
-        5 * 10**8,
+        2 * 10**9,
         10**5,
         *pieces,
         coarse_filters,
@@ -396,7 +400,7 @@
         functools.partial(straight_kernel, groups),
         jax.ShapeDtypeStruct((cols, height, frames, depth1), F32),
         [],
-        2 * cells * cols * depth0 * depth1,
+        5 * 10**9,
         10**6,
         *pieces,
         coarse_proj,
@@ -418,14 +422,18 @@
         *parts,
         coarse_proj,
         straight,
+        *early,
     )
     odd_pairs = [(i, i + 1) for i in range(1, tiles - 1, 2)]
     odd_in = lax.ppermute(odd_out, "tile", odd_pairs + [(j, i) for i, j in odd_pairs])
     even_in = exchange(even_out, "tile", 1)
     if divided:
         gathered, beyond, _ = lax.optimization_barrier((gathered, beyond, own))
-        mine = jnp.concatenate([gathered[:1], beyond[None], gathered[1:]])
-        mine = jnp.concatenate([mine, exchange(mine, "tile", 1)])
+        beyond = beyond[None]
+        got = early[0]
+        mine = jnp.concatenate(
+            [gathered[:1], beyond, gathered[1:], got[:1], exchange(beyond, "tile", 1), got[1:]]
+        )
     mid_folded = call(
         fold_middle_kernel,
         jax.ShapeDtypeStruct((3, 3, 2, depth1, lanes), BF16),

time: 36.5 us -> 36.4 us (level)
  waiting for transfers between devices: 8.34 us -> 7.82 us
  starting transfers between devices: 19.2 us -> 19.6 us
    ppermute x14 -> x15, waiting for transfers between devices: 6.31 us -> 5.55 us  [exchange(): return lax.ppermute(values, axis, [(i, i ^ k) for i in range(size)])]
    ppermute x14 -> x15, starting transfers between devices: 15.9 us -> 16.5 us  [exchange(): return lax.ppermute(values, axis, [(i, i ^ k) for i in range(size)])]
  transfers between devices with their start and end apart: 15 -> 16, of which waited for: 6 -> 5; matrix products, arithmetic and copies ran while one was open for 1% -> 1% of each run, Pallas kernels for 13% -> 13%
where the time goes in v6:
time: 36.4 us; the launch traced here: 35.9 us
  starting transfers between devices  19.6 us (54%)
  Pallas kernels  7.92 us (22%)
  waiting for transfers between devices  7.82 us (21%)
    ppermute x15, starting transfers between devices, exchange(): return lax.ppermute(values, axis, [(i, i ^ k) for i in range(size)])  16.5 us
    pallas_call x8, Pallas kernels, call(): pl.pallas_call(kernel, out_shape=outs, in_specs=[FAR if n in stay else VM...  7.92 us
    ppermute x15, waiting for transfers between devices, exchange(): return lax.ppermute(values, axis, [(i, i ^ k) for i in range(size)])  5.55 us
    ppermute x1, starting transfers between devices, body(): lax.ppermute(odd_out, 'tile', odd_pairs + [(j, i) for i, j in odd_pairs])  3.1 us
    ppermute x1, waiting for transfers between devices, body(): lax.ppermute(odd_out, 'tile', odd_pairs + [(j, i) for i, j in odd_pairs])  2.26 us
  transfers between devices with their start and end apart: 16, of which 5 were waited for; matrix products, arithmetic and copies ran while one was open for 1% of the time, Pallas kernels for 13%

profile of v6, /device:TPU:1, one launch (start us, length us, event | category | flops | bytes accessed | tf_op | source)
XLA Modules:
  0.0 35.9 jit_solution(17029917011761781551)
XLA Ops:
  0.0 2.0 %collective-permute-start = (bf16[8,4,2,512]{3,2,1,0:T(2,128)(2,1)}, bf16[8,4,2,512]{3,2,1,0:T(2,128)(2,1)S(1)}, u32[]{:S(2)}, u32[]{:S(2)}) collective-permute-start(bf16[8,4,2,512]{3,2,1,0:T(2,128)(2,1)} %param.6), channel_id=1, source_target_pairs={{0,8},{8,0},{16,24},{24,16},{1,9},{9,1},{17,25},{25,17},{2,10},{10... | collective-permute-start | bytes 196616 | tf_op jit(solution)/shard_map/ppermute | solution.py:351
  2.0 1.2 %collective-permute-start.2 = (bf16[8,4,2,512]{3,2,1,0:T(2,128)(2,1)}, bf16[8,4,2,512]{3,2,1,0:T(2,128)(2,1)S(1)}, u32[]{:S(2)}, u32[]{:S(2)}) collective-permute-start(bf16[8,4,2,512]{3,2,1,0:T(2,128)(2,1)} %param.6), channel_id=1, source_target_pairs={{0,24},{8,16},{16,8},{24,0},{1,25},{9,17},{17,9},{25,1},{2,26},{10... | collective-permute-start | bytes 196616 | tf_op jit(solution)/shard_map/ppermute | solution.py:351
  3.3 1.2 %shard_map.66 = bf16[3,3,3,8,256]{4,3,2,1,0:T(8,128)(2,1)S(1)} custom-call(bf16[3,3,3,32,256]{4,3,2,1,0:T(8,128)(2,1)} %bitcast.30), custom_call_target="tpu_custom_call" | custom-call | flops 6000000000 | bytes 1000000 | tf_op jit(solution)/shard_map/pallas_call | solution.py:22
  4.5 3.6 %collective-permute-start.7 = (bf16[3,3,3,8,256]{4,3,2,1,0:T(8,128)(2,1)S(1)}, bf16[3,3,3,8,256]{4,3,2,1,0:T(8,128)(2,1)S(1)}, u32[]{:S(2)}, u32[]{:S(2)}) collective-permute-start(bf16[3,3,3,8,256]{4,3,2,1,0:T(8,128)(2,1)S(1)} %shard_map.66), channel_id=1, source_target_pairs={{0,6},{1,7},{2,4},{3,5},{4,2},{5,3},{6,0},{7,1},{8,14},{9,15},{10,... | collective-permute-start | bytes 331784 | tf_op jit(solution)/shard_map/ppermute | solution.py:351
  8.3 1.7 %shard_map.64.refs_0_ = bf16[4,128,128]{2,1,0:T(8,128)(2,1)S(1)} custom-call(bf16[4,2,8,512]{3,2,1,0:T(8,128)(2,1)S(1)} %bitcast.19, bf16[4,2,8,512]{3,2,1,0:T(8,128)(2,1)S(1)} %bitcast.21, bf16[4,2,8,512]{3,2,1,0:T(8,128)(2,1)S(1)} %bitcast.25, bf16[4,2,8,512]{3,2,1,0:T(8,128)(2,1)S(1)} %bitcast.23, bf16[3,3,3,512,128]{4,3,2,1,0:T(8,128)(2,1)S(1)} %copy-done.3), custom_call_target="tpu_custom_call" | custom-call | flops 2000000000 | bytes 100000 | tf_op jit(solution)/shard_map/pallas_call | solution.py:22
  10.0 2.2 %collective-permute-start.5 = (bf16[4,128,128]{2,1,0:T(8,128)(2,1)S(1)}, bf16[4,128,128]{2,1,0:T(8,128)(2,1)S(1)}, u32[]{:S(2)}, u32[]{:S(2)}) collective-permute-start(bf16[4,128,128]{2,1,0:T(8,128)(2,1)S(1)} %shard_map.64.refs_0_), channel_id=1, source_target_pairs={{0,24},{8,16},{16,8},{24,0},{1,25},{9,17},{17,9},{25,1},{2,26},{10... | collective-permute-start | bytes 393224 | tf_op jit(solution)/shard_map/ppermute | solution.py:351
  12.5 0.3 collective-permute-start.3
  12.7 2.2 %collective-permute-start.11 = (bf16[3,3,3,8,256]{4,3,2,1,0:T(8,128)(2,1)S(1)}, bf16[3,3,3,8,256]{4,3,2,1,0:T(8,128)(2,1)S(1)}, u32[]{:S(2)}, u32[]{:S(2)}) collective-permute-start(bf16[3,3,3,8,256]{4,3,2,1,0:T(8,128)(2,1)S(1)} %shard_map.66), channel_id=1, source_target_pairs={{0,2},{1,3},{2,0},{3,1},{4,6},{5,7},{6,4},{7,5},{8,10},{9,11},{10,... | collective-permute-start | bytes 331784 | tf_op jit(solution)/shard_map/ppermute | solution.py:351
  14.9 2.1 %collective-permute-done.6 = bf16[3,3,3,8,256]{4,3,2,1,0:T(8,128)(2,1)S(1)} collective-permute-done((bf16[3,3,3,8,256]{4,3,2,1,0:T(8,128)(2,1)S(1)}, bf16[3,3,3,8,256]{4,3,2,1,0:T(8,128)(2,1)S(1)}, u32[]{:S(2)}, u32[]{:S(2)}) %collective-permute-start.6) | collective-permute-done | bytes 110624 | tf_op jit(solution)/shard_map/ppermute | solution.py:351
  17.0 1.6 %collective-permute-start.8 = (bf16[3,3,3,3,8,256]{5,4,3,2,1,0:T(8,128)(2,1)S(1)}, bf16[3,3,3,3,8,256]{5,4,3,2,1,0:T(8,128)(2,1)S(1)}, u32[]{:S(2)}, u32[]{:S(2)}) collective-permute-start(bf16[3,3,3,3,8,256]{5,4,3,2,1,0:T(8,128)(2,1)S(1)} %pad_maximum_fusion), channel_id=1, source_target_pairs={{0,1},{1,0},{2,3},{3,2},{4,5},{5,4},{6,7},{7,6},{8,9},{9,8},{10,11... | collective-permute-start | bytes 995336 | tf_op jit(solution)/shard_map/ppermute | solution.py:351
  18.6 0.3 shard_map.65.refs_5_
  18.9 0.9 %collective-permute-done.8.refs_6_ = bf16[3,3,3,3,8,256]{5,4,3,2,1,0:T(8,128)(2,1)S(1)} collective-permute-done((bf16[3,3,3,3,8,256]{5,4,3,2,1,0:T(8,128)(2,1)S(1)}, bf16[3,3,3,3,8,256]{5,4,3,2,1,0:T(8,128)(2,1)S(1)}, u32[]{:S(2)}, u32[]{:S(2)}) %collective-permute-start.8) | collective-permute-done | bytes 331808 | tf_op jit(solution)/shard_map/ppermute | solution.py:351
  19.9 0.4 %shard_map.67 = (bf16[2,128,256]{2,1,0:T(8,128)(2,1)S(1)}, bf16[2,128,256]{2,1,0:T(8,128)(2,1)S(1)}, f32[4,128,256]{2,1,0:T(8,128)S(1)}) custom-call(bf16[4,128,128]{2,1,0:T(8,128)(2,1)S(1)} %shard_map.64.refs_0_, bf16[4,128,128]{2,1,0:T(8,128)(2,1)S(1)} %collective-permute-done.3.refs_1_, bf16[4,128,128]{2,1,0:T(8,128)(2,1)S(1)} %collective-permute-done.4.refs_2_, ...), custom_call_target="tpu_custom_call" | custom-call | flops 134217728 | bytes 2000000 | tf_op jit(solution)/shard_map/pallas_call | solution.py:22
  20.3 0.4 %collective-permute-start.12 = (bf16[1,3,3,3,8,256]{5,4,3,2,1,0:T(8,128)(2,1)S(1)}, bf16[1,3,3,3,8,256]{5,4,3,2,1,0:T(8,128)(2,1)S(1)}, u32[]{:S(2)}, u32[]{:S(2)}) collective-permute-start(bf16[1,3,3,3,8,256]{5,4,3,2,1,0:T(8,128)(2,1)S(1)} %bitcast.27), channel_id=1, source_target_pairs={{0,1},{1,0},{2,3},{3,2},{4,5},{5,4},{6,7},{7,6},{8,9},{9,8},{10,11... | collective-permute-start | bytes 331784 | tf_op jit(solution)/shard_map/ppermute | solution.py:351
  20.7 3.1 %collective-permute-start.9 = (bf16[2,128,256]{2,1,0:T(8,128)(2,1)S(1)}, bf16[2,128,256]{2,1,0:T(8,128)(2,1)S(1)}, u32[]{:S(2)}, u32[]{:S(2)}) collective-permute-start(bf16[2,128,256]{2,1,0:T(8,128)(2,1)S(1)} %get-tuple-element.18), channel_id=1, source_target_pairs={{1,2},{3,4},{5,6},{2,1},{4,3},{6,5},{9,10},{11,12},{13,14},{10,9},... | collective-permute-start | bytes 393224 | tf_op jit(solution)/shard_map/ppermute | solution.py:428
  24.1 0.7 %shard_map.68.filters = bf16[3,3,2,256,256]{4,3,2,1,0:T(8,128)(2,1)S(1)} custom-call(bf16[8,3,3,3,8,256]{5,4,3,2,1,0:T(8,128)(2,1)S(1)} %slice_dynamic-update-slice_fusion.pieces), custom_call_target="tpu_custom_call" | custom-call | flops 1000000 | bytes 4000000 | tf_op jit(solution)/shard_map/pallas_call | solution.py:22
  24.7 2.3 %collective-permute-done.9.odd_in = bf16[2,128,256]{2,1,0:T(8,128)(2,1)S(1)} collective-permute-done((bf16[2,128,256]{2,1,0:T(8,128)(2,1)S(1)}, bf16[2,128,256]{2,1,0:T(8,128)(2,1)S(1)}, u32[]{:S(2)}, u32[]{:S(2)}) %collective-permute-start.9) | collective-permute-done | bytes 131104 | tf_op jit(solution)/shard_map/ppermute | solution.py:428
  27.0 1.3 %shard_map.69 = (bf16[120,256]{1,0:T(8,128)(2,1)S(1)}, bf16[120,256]{1,0:T(8,128)(2,1)S(1)}, bf16[120,256]{1,0:T(8,128)(2,1)S(1)}, bf16[120,256]{1,0:T(8,128)(2,1)S(1)}, bf16[4,48,256]{2,1,0:T(8,128)(2,1)S(1)}) custom-call(bf16[2,128,256]{2,1,0:T(8,128)(2,1)S(1)} %collective-permute-done.9.odd_in, bf16[2,128,256]{2,1,0:T(8,128)(2,1)S(1)} %collective-permute-done.10.even_in, ...), custom_call_target="tpu_custom_call" | custom-call | flops 905969664 | bytes 5000000 | tf_op jit(solution)/shard_map/pallas_call | solution.py:22
  28.3 1.3 %collective-permute-start.13 = (bf16[120,256]{1,0:T(8,128)(2,1)S(1)}, bf16[120,256]{1,0:T(8,128)(2,1)S(1)}, u32[]{:S(2)}, u32[]{:S(2)}) collective-permute-start(bf16[120,256]{1,0:T(8,128)(2,1)S(1)} %get-tuple-element.25), channel_id=1, source_target_pairs={{0,16},{8,24},{16,0},{24,8},{1,17},{9,25},{17,1},{25,9},{2,18},{10... | collective-permute-start | bytes 184328 | tf_op jit(solution)/shard_map/ppermute | solution.py:351
  29.6 1.2 %collective-permute-start.14 = (bf16[120,256]{1,0:T(8,128)(2,1)S(1)}, bf16[120,256]{1,0:T(8,128)(2,1)S(1)}, u32[]{:S(2)}, u32[]{:S(2)}) collective-permute-start(bf16[120,256]{1,0:T(8,128)(2,1)S(1)} %get-tuple-element.26), channel_id=1, source_target_pairs={{0,24},{8,16},{16,8},{24,0},{1,25},{9,17},{17,9},{25,1},{2,26},{10... | collective-permute-start | bytes 184328 | tf_op jit(solution)/shard_map/ppermute | solution.py:351
  31.0 0.4 %shard_map.70 = (bf16[3,2,2,256,256]{4,3,2,1,0:T(8,128)(2,1)S(1)}, bf16[4,256,512]{2,1,0:T(8,128)(2,1)S(1)}) custom-call(bf16[3,3,3,128,128]{4,3,2,1,0:T(8,128)(2,1)S(1)} %copy-done, bf16[256,128]{1,0:T(8,128)(2,1)S(1)} %copy-done.2), custom_call_target="tpu_custom_call" | custom-call | flops 1000000 | bytes 4000000 | tf_op jit(solution)/shard_map/pallas_call | solution.py:22
  31.4 2.2 %collective-permute-done.14.refs_2_ = bf16[120,256]{1,0:T(8,128)(2,1)S(1)} collective-permute-done((bf16[120,256]{1,0:T(8,128)(2,1)S(1)}, bf16[120,256]{1,0:T(8,128)(2,1)S(1)}, u32[]{:S(2)}, u32[]{:S(2)}) %collective-permute-start.14) | collective-permute-done | bytes 61472 | tf_op jit(solution)/shard_map/ppermute | solution.py:351
  33.7 0.3 collective-permute-done.15.refs_3_
  33.9 1.9 %shard_map.71 = bf16[8,16,8,128]{3,2,1,0:T(8,128)(2,1)} custom-call(bf16[120,256]{1,0:T(8,128)(2,1)S(1)} %get-tuple-element.24.refs_0_, bf16[120,256]{1,0:T(8,128)(2,1)S(1)} %collective-permute-done.13.refs_1_, bf16[120,256]{1,0:T(8,128)(2,1)S(1)} %collective-permute-done.14.refs_2_, bf16[120,256]{1,0:T(8,128)(2,1)S(1)} %collective-permute-done.15.refs_3_, ...), custom_call_target="tpu_custom_call" | custom-call | flops 503316480 | bytes 3000000 | tf_op jit(solution)/shard_map/pallas_call | solution.py:22
  (37 shorter events, 0.9 us)
Async XLA Ops:
  0.0 8.1 %collective-permute-start = (bf16[8,4,2,512]{3,2,1,0:T(2,128)(2,1)}, bf16[8,4,2,512]{3,2,1,0:T(2,128)(2,1)S(1)}, u32[]{:S(2)}, u32[]{:S(2)}) collective-permute-start(bf16[8,4,2,512]{3,2,1,0:T(2,128)(2,1)} %param.6), channel_id=1, source_target_pairs={{0,8},{8,0},{16,24},{24,16},{1,9},{9,1},{17,25},{25,17},{2,10},{10... | collective-permute-start | bytes 196616 | tf_op jit(solution)/shard_map/ppermute | solution.py:351
  2.0 6.1 %collective-permute-start.2 = (bf16[8,4,2,512]{3,2,1,0:T(2,128)(2,1)}, bf16[8,4,2,512]{3,2,1,0:T(2,128)(2,1)S(1)}, u32[]{:S(2)}, u32[]{:S(2)}) collective-permute-start(bf16[8,4,2,512]{3,2,1,0:T(2,128)(2,1)} %param.6), channel_id=1, source_target_pairs={{0,24},{8,16},{16,8},{24,0},{1,25},{9,17},{17,9},{25,1},{2,26},{10... | collective-permute-start | bytes 196616 | tf_op jit(solution)/shard_map/ppermute | solution.py:351
  3.3 5.0 %collective-permute-start.1 = (bf16[8,4,2,512]{3,2,1,0:T(2,128)(2,1)}, bf16[8,4,2,512]{3,2,1,0:T(2,128)(2,1)S(1)}, u32[]{:S(2)}, u32[]{:S(2)}) collective-permute-start(bf16[8,4,2,512]{3,2,1,0:T(2,128)(2,1)} %param.6), channel_id=1, source_target_pairs={{0,16},{8,24},{16,0},{24,8},{1,17},{9,25},{17,1},{25,9},{2,18},{10... | collective-permute-start | bytes 196616 | tf_op jit(solution)/shard_map/ppermute | solution.py:351
  3.3 4.8 %copy-start.4 = (bf16[8,4,2,512]{3,2,1,0:T(2,128)(2,1)S(1)}, bf16[8,4,2,512]{3,2,1,0:T(2,128)(2,1)}, u32[]{:S(2)}) copy-start(bf16[8,4,2,512]{3,2,1,0:T(2,128)(2,1)} %param.6) | copy-start | bytes 196612
  3.3 5.0 %copy-start.3 = (bf16[3,3,3,512,128]{4,3,2,1,0:T(8,128)(2,1)S(1)}, bf16[3,3,3,512,128]{4,3,2,1,0:T(8,128)(2,1)}, u32[]{:S(2)}) copy-start(bf16[3,3,3,512,128]{4,3,2,1,0:T(8,128)(2,1)} %refs_4_.3) | copy-start | bytes 10616836
  4.5 8.2 %collective-permute-start.7 = (bf16[3,3,3,8,256]{4,3,2,1,0:T(8,128)(2,1)S(1)}, bf16[3,3,3,8,256]{4,3,2,1,0:T(8,128)(2,1)S(1)}, u32[]{:S(2)}, u32[]{:S(2)}) collective-permute-start(bf16[3,3,3,8,256]{4,3,2,1,0:T(8,128)(2,1)S(1)} %shard_map.66), channel_id=1, source_target_pairs={{0,6},{1,7},{2,4},{3,5},{4,2},{5,3},{6,0},{7,1},{8,14},{9,15},{10,... | collective-permute-start | bytes 331784 | tf_op jit(solution)/shard_map/ppermute | solution.py:351
  8.1 8.9 %collective-permute-start.6 = (bf16[3,3,3,8,256]{4,3,2,1,0:T(8,128)(2,1)S(1)}, bf16[3,3,3,8,256]{4,3,2,1,0:T(8,128)(2,1)S(1)}, u32[]{:S(2)}, u32[]{:S(2)}) collective-permute-start(bf16[3,3,3,8,256]{4,3,2,1,0:T(8,128)(2,1)S(1)} %shard_map.66), channel_id=1, source_target_pairs={{0,4},{1,5},{2,6},{3,7},{4,0},{5,1},{6,2},{7,3},{8,12},{9,13},{10,... | collective-permute-start | bytes 331784 | tf_op jit(solution)/shard_map/ppermute | solution.py:351
  8.3 10.3 %copy-start.1 = (bf16[512,256]{1,0:T(8,128)(2,1)S(1)}, bf16[512,256]{1,0:T(8,128)(2,1)}, u32[]{:S(2)}) copy-start(bf16[512,256]{1,0:T(8,128)(2,1)} %refs_4_.5) | copy-start | bytes 786436
  10.0 8.9 %collective-permute-start.5 = (bf16[4,128,128]{2,1,0:T(8,128)(2,1)S(1)}, bf16[4,128,128]{2,1,0:T(8,128)(2,1)S(1)}, u32[]{:S(2)}, u32[]{:S(2)}) collective-permute-start(bf16[4,128,128]{2,1,0:T(8,128)(2,1)S(1)} %shard_map.64.refs_0_), channel_id=1, source_target_pairs={{0,24},{8,16},{16,8},{24,0},{1,25},{9,17},{17,9},{25,1},{2,26},{10... | collective-permute-start | bytes 393224 | tf_op jit(solution)/shard_map/ppermute | solution.py:351
  12.2 6.7 %collective-permute-start.4 = (bf16[4,128,128]{2,1,0:T(8,128)(2,1)S(1)}, bf16[4,128,128]{2,1,0:T(8,128)(2,1)S(1)}, u32[]{:S(2)}, u32[]{:S(2)}) collective-permute-start(bf16[4,128,128]{2,1,0:T(8,128)(2,1)S(1)} %shard_map.64.refs_0_), channel_id=1, source_target_pairs={{0,16},{8,24},{16,0},{24,8},{1,17},{9,25},{17,1},{25,9},{2,18},{10... | collective-permute-start | bytes 393224 | tf_op jit(solution)/shard_map/ppermute | solution.py:351
  12.5 6.5 %collective-permute-start.3 = (bf16[4,128,128]{2,1,0:T(8,128)(2,1)S(1)}, bf16[4,128,128]{2,1,0:T(8,128)(2,1)S(1)}, u32[]{:S(2)}, u32[]{:S(2)}) collective-permute-start(bf16[4,128,128]{2,1,0:T(8,128)(2,1)S(1)} %shard_map.64.refs_0_), channel_id=1, source_target_pairs={{0,8},{8,0},{16,24},{24,16},{1,9},{9,1},{17,25},{25,17},{2,10},{10... | collective-permute-start | bytes 393224 | tf_op jit(solution)/shard_map/ppermute | solution.py:351
  12.7 7.6 %collective-permute-start.11 = (bf16[3,3,3,8,256]{4,3,2,1,0:T(8,128)(2,1)S(1)}, bf16[3,3,3,8,256]{4,3,2,1,0:T(8,128)(2,1)S(1)}, u32[]{:S(2)}, u32[]{:S(2)}) collective-permute-start(bf16[3,3,3,8,256]{4,3,2,1,0:T(8,128)(2,1)S(1)} %shard_map.66), channel_id=1, source_target_pairs={{0,2},{1,3},{2,0},{3,1},{4,6},{5,7},{6,4},{7,5},{8,10},{9,11},{10,... | collective-permute-start | bytes 331784 | tf_op jit(solution)/shard_map/ppermute | solution.py:351
  17.0 2.8 %collective-permute-start.8 = (bf16[3,3,3,3,8,256]{5,4,3,2,1,0:T(8,128)(2,1)S(1)}, bf16[3,3,3,3,8,256]{5,4,3,2,1,0:T(8,128)(2,1)S(1)}, u32[]{:S(2)}, u32[]{:S(2)}) collective-permute-start(bf16[3,3,3,3,8,256]{5,4,3,2,1,0:T(8,128)(2,1)S(1)} %pad_maximum_fusion), channel_id=1, source_target_pairs={{0,1},{1,0},{2,3},{3,2},{4,5},{5,4},{6,7},{7,6},{8,9},{9,8},{10,11... | collective-permute-start | bytes 995336 | tf_op jit(solution)/shard_map/ppermute | solution.py:351
  20.3 3.7 %collective-permute-start.12 = (bf16[1,3,3,3,8,256]{5,4,3,2,1,0:T(8,128)(2,1)S(1)}, bf16[1,3,3,3,8,256]{5,4,3,2,1,0:T(8,128)(2,1)S(1)}, u32[]{:S(2)}, u32[]{:S(2)}) collective-permute-start(bf16[1,3,3,3,8,256]{5,4,3,2,1,0:T(8,128)(2,1)S(1)} %bitcast.27), channel_id=1, source_target_pairs={{0,1},{1,0},{2,3},{3,2},{4,5},{5,4},{6,7},{7,6},{8,9},{9,8},{10,11... | collective-permute-start | bytes 331784 | tf_op jit(solution)/shard_map/ppermute | solution.py:351
  20.7 6.3 %collective-permute-start.9 = (bf16[2,128,256]{2,1,0:T(8,128)(2,1)S(1)}, bf16[2,128,256]{2,1,0:T(8,128)(2,1)S(1)}, u32[]{:S(2)}, u32[]{:S(2)}) collective-permute-start(bf16[2,128,256]{2,1,0:T(8,128)(2,1)S(1)} %get-tuple-element.18), channel_id=1, source_target_pairs={{1,2},{3,4},{5,6},{2,1},{4,3},{6,5},{9,10},{11,12},{13,14},{10,9},... | collective-permute-start | bytes 393224 | tf_op jit(solution)/shard_map/ppermute | solution.py:428
  23.8 3.2 %collective-permute-start.10 = (bf16[2,128,256]{2,1,0:T(8,128)(2,1)S(1)}, bf16[2,128,256]{2,1,0:T(8,128)(2,1)S(1)}, u32[]{:S(2)}, u32[]{:S(2)}) collective-permute-start(bf16[2,128,256]{2,1,0:T(8,128)(2,1)S(1)} %get-tuple-element.19), channel_id=1, source_target_pairs={{0,1},{1,0},{2,3},{3,2},{4,5},{5,4},{6,7},{7,6},{8,9},{9,8},{10,11... | collective-permute-start | bytes 393224 | tf_op jit(solution)/shard_map/ppermute | solution.py:351
  24.7 6.3 %copy-start = (bf16[3,3,3,128,128]{4,3,2,1,0:T(8,128)(2,1)S(1)}, bf16[3,3,3,128,128]{4,3,2,1,0:T(8,128)(2,1)}, u32[]{:S(2)}) copy-start(bf16[3,3,3,128,128]{4,3,2,1,0:T(8,128)(2,1)} %filters.1) | copy-start | bytes 2654212
  24.7 6.3 %copy-start.2 = (bf16[256,128]{1,0:T(8,128)(2,1)S(1)}, bf16[256,128]{1,0:T(8,128)(2,1)}, u32[]{:S(2)}) copy-start(bf16[256,128]{1,0:T(8,128)(2,1)} %refs_6_.1) | copy-start | bytes 196612
  28.3 3.1 %collective-permute-start.13 = (bf16[120,256]{1,0:T(8,128)(2,1)S(1)}, bf16[120,256]{1,0:T(8,128)(2,1)S(1)}, u32[]{:S(2)}, u32[]{:S(2)}) collective-permute-start(bf16[120,256]{1,0:T(8,128)(2,1)S(1)} %get-tuple-element.25), channel_id=1, source_target_pairs={{0,16},{8,24},{16,0},{24,8},{1,17},{9,25},{17,1},{25,9},{2,18},{10... | collective-permute-start | bytes 184328 | tf_op jit(solution)/shard_map/ppermute | solution.py:351
  29.6 4.0 %collective-permute-start.14 = (bf16[120,256]{1,0:T(8,128)(2,1)S(1)}, bf16[120,256]{1,0:T(8,128)(2,1)S(1)}, u32[]{:S(2)}, u32[]{:S(2)}) collective-permute-start(bf16[120,256]{1,0:T(8,128)(2,1)S(1)} %get-tuple-element.26), channel_id=1, source_target_pairs={{0,24},{8,16},{16,8},{24,0},{1,25},{9,17},{17,9},{25,1},{2,26},{10... | collective-permute-start | bytes 184328 | tf_op jit(solution)/shard_map/ppermute | solution.py:351
  30.8 3.2 %collective-permute-start.15 = (bf16[120,256]{1,0:T(8,128)(2,1)S(1)}, bf16[120,256]{1,0:T(8,128)(2,1)S(1)}, u32[]{:S(2)}, u32[]{:S(2)}) collective-permute-start(bf16[120,256]{1,0:T(8,128)(2,1)S(1)} %get-tuple-element.27), channel_id=1, source_target_pairs={{0,8},{8,0},{16,24},{24,16},{1,9},{9,1},{17,25},{25,17},{2,10},{10... | collective-permute-start | bytes 184328 | tf_op jit(solution)/shard_map/ppermute | solution.py:351

commit v7 on v6

--- a/solution.py
+++ b/solution.py
@@ -64,19 +64,30 @@
         for step in range(3):
             moved = delayed(act, 2 - step).reshape(rows, cols * frames, depth)
             shifted[step, pl.ds(at + 1, rows)] = moved.astype(BF16)
-    joined = width % 128 == 0
-    totals = [None] * (1 if joined else 3)
-    for step in range(3):
-        for row in range(3):
-            left = shifted[step, row : row + height].reshape(height * cols * frames, depth)
-            taps = [filters[step, row, col] for col in range(3)]
-            if joined:
-                taps = [jnp.concatenate(taps, axis=1)]
-            for n, tap in enumerate(taps):
-                term = dot(left, tap)
-                totals[n] = term if totals[n] is None else totals[n] + term
-    if joined:
-        totals = [totals[0][:, n * width : (n + 1) * width] for n in range(3)]
+    if width % 128 == 0:
+        total = None
+        for step in range(3):
+            left = shifted[step, 1 : height + 1].reshape(height * cols * frames, depth)
+            taps = [filters[step, row, col] for row in range(3) for col in range(3)]
+            term = dot(left, jnp.concatenate(taps, axis=1))
+            total = term if total is None else total + term
+        total = total.reshape(height, cols * frames, 9 * width)
+        above, level, below = [total[:, :, 3 * n * width : 3 * (n + 1) * width] for n in range(3)]
+        nothing = jnp.zeros((1, cols * frames, 3 * width), F32)
+        total = (
+            level
+            + jnp.concatenate([nothing, above[:-1]], axis=0)
+            + jnp.concatenate([below[1:], nothing], axis=0)
+        )
+        totals = [total[:, :, n * width : (n + 1) * width] for n in range(3)]
+    else:
+        totals = [None] * 3
+        for step in range(3):
+            for row in range(3):
+                left = shifted[step, row : row + height].reshape(height * cols * frames, depth)
+                for col in range(3):
+                    term = dot(left, filters[step, row, col])
+                    totals[col] = term if totals[col] is None else totals[col] + term
     totals = [total.reshape(height, cols, frames, width) for total in totals]
     for out in range(cols + 2):
         value = sum(
@@ -303,9 +314,10 @@
     me = lax.axis_index("grp")
     share = out.shape[3]
     copy.wait()
-    value = filters[:, :, :, 0:share].astype(F32)
+    every = filters[...].astype(F32)
+    value = every[:, :, :, 0:share]
     for k in range(1, groups):
-        value = jnp.where(me == k, filters[:, :, :, k * share : (k + 1) * share].astype(F32), value)
+        value = jnp.where(me == k, every[:, :, :, k * share : (k + 1) * share], value)
     out[...] = value.astype(BF16)
 
 

time: 36.4 us -> 36.4 us (level)
  no operation moved by 1% of the time
where the time goes in v7:
time: 36.4 us; the launch traced here: 35.9 us
  starting transfers between devices  19.8 us (54%)
  waiting for transfers between devices  7.82 us (21%)
  Pallas kernels  7.72 us (21%)
    ppermute x15, starting transfers between devices, exchange(): return lax.ppermute(values, axis, [(i, i ^ k) for i in range(size)])  16.7 us
    pallas_call x8, Pallas kernels, call(): pl.pallas_call(kernel, out_shape=outs, in_specs=[FAR if n in stay else VM...  7.72 us
    ppermute x15, waiting for transfers between devices, exchange(): return lax.ppermute(values, axis, [(i, i ^ k) for i in range(size)])  5.55 us
    ppermute x1, starting transfers between devices, body(): lax.ppermute(odd_out, 'tile', odd_pairs + [(j, i) for i, j in odd_pairs])  3.1 us
    ppermute x1, waiting for transfers between devices, body(): lax.ppermute(odd_out, 'tile', odd_pairs + [(j, i) for i, j in odd_pairs])  2.26 us
  transfers between devices with their start and end apart: 16, of which 5 were waited for; matrix products, arithmetic and copies ran while one was open for 1% of the time, Pallas kernels for 13%

profile of v7, /device:TPU:1, one launch (start us, length us, event | category | flops | bytes accessed | tf_op | source)
XLA Modules:
  0.0 35.9 jit_solution(13173147761491601921)
XLA Ops:
  0.0 2.0 %collective-permute-start = (bf16[8,4,2,512]{3,2,1,0:T(2,128)(2,1)}, bf16[8,4,2,512]{3,2,1,0:T(2,128)(2,1)S(1)}, u32[]{:S(2)}, u32[]{:S(2)}) collective-permute-start(bf16[8,4,2,512]{3,2,1,0:T(2,128)(2,1)} %param.6), channel_id=1, source_target_pairs={{0,8},{8,0},{16,24},{24,16},{1,9},{9,1},{17,25},{25,17},{2,10},{10... | collective-permute-start | bytes 196616 | tf_op jit(solution)/shard_map/ppermute | solution.py:363
  2.0 1.2 %collective-permute-start.2 = (bf16[8,4,2,512]{3,2,1,0:T(2,128)(2,1)}, bf16[8,4,2,512]{3,2,1,0:T(2,128)(2,1)S(1)}, u32[]{:S(2)}, u32[]{:S(2)}) collective-permute-start(bf16[8,4,2,512]{3,2,1,0:T(2,128)(2,1)} %param.6), channel_id=1, source_target_pairs={{0,24},{8,16},{16,8},{24,0},{1,25},{9,17},{17,9},{25,1},{2,26},{10... | collective-permute-start | bytes 196616 | tf_op jit(solution)/shard_map/ppermute | solution.py:363
  3.3 1.2 %shard_map.66 = bf16[3,3,3,8,256]{4,3,2,1,0:T(8,128)(2,1)S(1)} custom-call(bf16[3,3,3,32,256]{4,3,2,1,0:T(8,128)(2,1)} %bitcast.30), custom_call_target="tpu_custom_call" | custom-call | flops 6000000000 | bytes 1000000 | tf_op jit(solution)/shard_map/pallas_call | solution.py:22
  4.5 3.6 %collective-permute-start.7 = (bf16[3,3,3,8,256]{4,3,2,1,0:T(8,128)(2,1)S(1)}, bf16[3,3,3,8,256]{4,3,2,1,0:T(8,128)(2,1)S(1)}, u32[]{:S(2)}, u32[]{:S(2)}) collective-permute-start(bf16[3,3,3,8,256]{4,3,2,1,0:T(8,128)(2,1)S(1)} %shard_map.66), channel_id=1, source_target_pairs={{0,6},{1,7},{2,4},{3,5},{4,2},{5,3},{6,0},{7,1},{8,14},{9,15},{10,... | collective-permute-start | bytes 331784 | tf_op jit(solution)/shard_map/ppermute | solution.py:363
  8.3 1.5 %shard_map.64.refs_0_ = bf16[4,128,128]{2,1,0:T(8,128)(2,1)S(1)} custom-call(bf16[4,2,8,512]{3,2,1,0:T(8,128)(2,1)S(1)} %bitcast.19, bf16[4,2,8,512]{3,2,1,0:T(8,128)(2,1)S(1)} %bitcast.21, bf16[4,2,8,512]{3,2,1,0:T(8,128)(2,1)S(1)} %bitcast.25, bf16[4,2,8,512]{3,2,1,0:T(8,128)(2,1)S(1)} %bitcast.23, bf16[3,3,3,512,128]{4,3,2,1,0:T(8,128)(2,1)S(1)} %copy-done.3), custom_call_target="tpu_custom_call" | custom-call | flops 2000000000 | bytes 100000 | tf_op jit(solution)/shard_map/pallas_call | solution.py:22
  9.8 2.2 %collective-permute-start.5 = (bf16[4,128,128]{2,1,0:T(8,128)(2,1)S(1)}, bf16[4,128,128]{2,1,0:T(8,128)(2,1)S(1)}, u32[]{:S(2)}, u32[]{:S(2)}) collective-permute-start(bf16[4,128,128]{2,1,0:T(8,128)(2,1)S(1)} %shard_map.64.refs_0_), channel_id=1, source_target_pairs={{0,24},{8,16},{16,8},{24,0},{1,25},{9,17},{17,9},{25,1},{2,26},{10... | collective-permute-start | bytes 393224 | tf_op jit(solution)/shard_map/ppermute | solution.py:363
  12.5 2.4 %collective-permute-start.11 = (bf16[3,3,3,8,256]{4,3,2,1,0:T(8,128)(2,1)S(1)}, bf16[3,3,3,8,256]{4,3,2,1,0:T(8,128)(2,1)S(1)}, u32[]{:S(2)}, u32[]{:S(2)}) collective-permute-start(bf16[3,3,3,8,256]{4,3,2,1,0:T(8,128)(2,1)S(1)} %shard_map.66), channel_id=1, source_target_pairs={{0,2},{1,3},{2,0},{3,1},{4,6},{5,7},{6,4},{7,5},{8,10},{9,11},{10,... | collective-permute-start | bytes 331784 | tf_op jit(solution)/shard_map/ppermute | solution.py:363
  14.9 2.1 %collective-permute-done.6 = bf16[3,3,3,8,256]{4,3,2,1,0:T(8,128)(2,1)S(1)} collective-permute-done((bf16[3,3,3,8,256]{4,3,2,1,0:T(8,128)(2,1)S(1)}, bf16[3,3,3,8,256]{4,3,2,1,0:T(8,128)(2,1)S(1)}, u32[]{:S(2)}, u32[]{:S(2)}) %collective-permute-start.6) | collective-permute-done | bytes 110624 | tf_op jit(solution)/shard_map/ppermute | solution.py:363
  17.0 1.6 %collective-permute-start.8 = (bf16[3,3,3,3,8,256]{5,4,3,2,1,0:T(8,128)(2,1)S(1)}, bf16[3,3,3,3,8,256]{5,4,3,2,1,0:T(8,128)(2,1)S(1)}, u32[]{:S(2)}, u32[]{:S(2)}) collective-permute-start(bf16[3,3,3,3,8,256]{5,4,3,2,1,0:T(8,128)(2,1)S(1)} %pad_maximum_fusion), channel_id=1, source_target_pairs={{0,1},{1,0},{2,3},{3,2},{4,5},{5,4},{6,7},{7,6},{8,9},{9,8},{10,11... | collective-permute-start | bytes 995336 | tf_op jit(solution)/shard_map/ppermute | solution.py:363
  18.6 0.3 shard_map.65.refs_5_
  18.9 0.9 %collective-permute-done.8.refs_6_ = bf16[3,3,3,3,8,256]{5,4,3,2,1,0:T(8,128)(2,1)S(1)} collective-permute-done((bf16[3,3,3,3,8,256]{5,4,3,2,1,0:T(8,128)(2,1)S(1)}, bf16[3,3,3,3,8,256]{5,4,3,2,1,0:T(8,128)(2,1)S(1)}, u32[]{:S(2)}, u32[]{:S(2)}) %collective-permute-start.8) | collective-permute-done | bytes 331808 | tf_op jit(solution)/shard_map/ppermute | solution.py:363
  19.9 0.4 %shard_map.67 = (bf16[2,128,256]{2,1,0:T(8,128)(2,1)S(1)}, bf16[2,128,256]{2,1,0:T(8,128)(2,1)S(1)}, f32[4,128,256]{2,1,0:T(8,128)S(1)}) custom-call(bf16[4,128,128]{2,1,0:T(8,128)(2,1)S(1)} %shard_map.64.refs_0_, bf16[4,128,128]{2,1,0:T(8,128)(2,1)S(1)} %collective-permute-done.3.refs_1_, bf16[4,128,128]{2,1,0:T(8,128)(2,1)S(1)} %collective-permute-done.4.refs_2_, ...), custom_call_target="tpu_custom_call" | custom-call | flops 134217728 | bytes 2000000 | tf_op jit(solution)/shard_map/pallas_call | solution.py:22
  20.3 0.4 %collective-permute-start.12 = (bf16[1,3,3,3,8,256]{5,4,3,2,1,0:T(8,128)(2,1)S(1)}, bf16[1,3,3,3,8,256]{5,4,3,2,1,0:T(8,128)(2,1)S(1)}, u32[]{:S(2)}, u32[]{:S(2)}) collective-permute-start(bf16[1,3,3,3,8,256]{5,4,3,2,1,0:T(8,128)(2,1)S(1)} %bitcast.27), channel_id=1, source_target_pairs={{0,1},{1,0},{2,3},{3,2},{4,5},{5,4},{6,7},{7,6},{8,9},{9,8},{10,11... | collective-permute-start | bytes 331784 | tf_op jit(solution)/shard_map/ppermute | solution.py:363
  20.7 3.1 %collective-permute-start.9 = (bf16[2,128,256]{2,1,0:T(8,128)(2,1)S(1)}, bf16[2,128,256]{2,1,0:T(8,128)(2,1)S(1)}, u32[]{:S(2)}, u32[]{:S(2)}) collective-permute-start(bf16[2,128,256]{2,1,0:T(8,128)(2,1)S(1)} %get-tuple-element.18), channel_id=1, source_target_pairs={{1,2},{3,4},{5,6},{2,1},{4,3},{6,5},{9,10},{11,12},{13,14},{10,9},... | collective-permute-start | bytes 393224 | tf_op jit(solution)/shard_map/ppermute | solution.py:440
  24.1 0.7 %shard_map.68.filters = bf16[3,3,2,256,256]{4,3,2,1,0:T(8,128)(2,1)S(1)} custom-call(bf16[8,3,3,3,8,256]{5,4,3,2,1,0:T(8,128)(2,1)S(1)} %slice_dynamic-update-slice_fusion.pieces), custom_call_target="tpu_custom_call" | custom-call | flops 1000000 | bytes 4000000 | tf_op jit(solution)/shard_map/pallas_call | solution.py:22
  24.7 2.3 %collective-permute-done.9.odd_in = bf16[2,128,256]{2,1,0:T(8,128)(2,1)S(1)} collective-permute-done((bf16[2,128,256]{2,1,0:T(8,128)(2,1)S(1)}, bf16[2,128,256]{2,1,0:T(8,128)(2,1)S(1)}, u32[]{:S(2)}, u32[]{:S(2)}) %collective-permute-start.9) | collective-permute-done | bytes 131104 | tf_op jit(solution)/shard_map/ppermute | solution.py:440
  27.0 1.3 %shard_map.69 = (bf16[120,256]{1,0:T(8,128)(2,1)S(1)}, bf16[120,256]{1,0:T(8,128)(2,1)S(1)}, bf16[120,256]{1,0:T(8,128)(2,1)S(1)}, bf16[120,256]{1,0:T(8,128)(2,1)S(1)}, bf16[4,48,256]{2,1,0:T(8,128)(2,1)S(1)}) custom-call(bf16[2,128,256]{2,1,0:T(8,128)(2,1)S(1)} %collective-permute-done.9.odd_in, bf16[2,128,256]{2,1,0:T(8,128)(2,1)S(1)} %collective-permute-done.10.even_in, ...), custom_call_target="tpu_custom_call" | custom-call | flops 905969664 | bytes 5000000 | tf_op jit(solution)/shard_map/pallas_call | solution.py:22
  28.3 1.3 %collective-permute-start.13 = (bf16[120,256]{1,0:T(8,128)(2,1)S(1)}, bf16[120,256]{1,0:T(8,128)(2,1)S(1)}, u32[]{:S(2)}, u32[]{:S(2)}) collective-permute-start(bf16[120,256]{1,0:T(8,128)(2,1)S(1)} %get-tuple-element.25), channel_id=1, source_target_pairs={{0,16},{8,24},{16,0},{24,8},{1,17},{9,25},{17,1},{25,9},{2,18},{10... | collective-permute-start | bytes 184328 | tf_op jit(solution)/shard_map/ppermute | solution.py:363
  29.6 1.2 %collective-permute-start.14 = (bf16[120,256]{1,0:T(8,128)(2,1)S(1)}, bf16[120,256]{1,0:T(8,128)(2,1)S(1)}, u32[]{:S(2)}, u32[]{:S(2)}) collective-permute-start(bf16[120,256]{1,0:T(8,128)(2,1)S(1)} %get-tuple-element.26), channel_id=1, source_target_pairs={{0,24},{8,16},{16,8},{24,0},{1,25},{9,17},{17,9},{25,1},{2,26},{10... | collective-permute-start | bytes 184328 | tf_op jit(solution)/shard_map/ppermute | solution.py:363
  30.8 0.3 collective-permute-start.15
  31.0 0.4 %shard_map.70 = (bf16[3,2,2,256,256]{4,3,2,1,0:T(8,128)(2,1)S(1)}, bf16[4,256,512]{2,1,0:T(8,128)(2,1)S(1)}) custom-call(bf16[3,3,3,128,128]{4,3,2,1,0:T(8,128)(2,1)S(1)} %copy-done, bf16[256,128]{1,0:T(8,128)(2,1)S(1)} %copy-done.2), custom_call_target="tpu_custom_call" | custom-call | flops 1000000 | bytes 4000000 | tf_op jit(solution)/shard_map/pallas_call | solution.py:22
  31.4 2.2 %collective-permute-done.14.refs_2_ = bf16[120,256]{1,0:T(8,128)(2,1)S(1)} collective-permute-done((bf16[120,256]{1,0:T(8,128)(2,1)S(1)}, bf16[120,256]{1,0:T(8,128)(2,1)S(1)}, u32[]{:S(2)}, u32[]{:S(2)}) %collective-permute-start.14) | collective-permute-done | bytes 61472 | tf_op jit(solution)/shard_map/ppermute | solution.py:363
  33.7 0.3 collective-permute-done.15.refs_3_
  33.9 1.9 %shard_map.71 = bf16[8,16,8,128]{3,2,1,0:T(8,128)(2,1)} custom-call(bf16[120,256]{1,0:T(8,128)(2,1)S(1)} %get-tuple-element.24.refs_0_, bf16[120,256]{1,0:T(8,128)(2,1)S(1)} %collective-permute-done.13.refs_1_, bf16[120,256]{1,0:T(8,128)(2,1)S(1)} %collective-permute-done.14.refs_2_, bf16[120,256]{1,0:T(8,128)(2,1)S(1)} %collective-permute-done.15.refs_3_, ...), custom_call_target="tpu_custom_call" | custom-call | flops 503316480 | bytes 3000000 | tf_op jit(solution)/shard_map/pallas_call | solution.py:22
  (37 shorter events, 0.9 us)
Async XLA Ops:
  0.0 8.1 %collective-permute-start = (bf16[8,4,2,512]{3,2,1,0:T(2,128)(2,1)}, bf16[8,4,2,512]{3,2,1,0:T(2,128)(2,1)S(1)}, u32[]{:S(2)}, u32[]{:S(2)}) collective-permute-start(bf16[8,4,2,512]{3,2,1,0:T(2,128)(2,1)} %param.6), channel_id=1, source_target_pairs={{0,8},{8,0},{16,24},{24,16},{1,9},{9,1},{17,25},{25,17},{2,10},{10... | collective-permute-start | bytes 196616 | tf_op jit(solution)/shard_map/ppermute | solution.py:363
  2.0 6.1 %collective-permute-start.2 = (bf16[8,4,2,512]{3,2,1,0:T(2,128)(2,1)}, bf16[8,4,2,512]{3,2,1,0:T(2,128)(2,1)S(1)}, u32[]{:S(2)}, u32[]{:S(2)}) collective-permute-start(bf16[8,4,2,512]{3,2,1,0:T(2,128)(2,1)} %param.6), channel_id=1, source_target_pairs={{0,24},{8,16},{16,8},{24,0},{1,25},{9,17},{17,9},{25,1},{2,26},{10... | collective-permute-start | bytes 196616 | tf_op jit(solution)/shard_map/ppermute | solution.py:363
  3.3 5.0 %collective-permute-start.1 = (bf16[8,4,2,512]{3,2,1,0:T(2,128)(2,1)}, bf16[8,4,2,512]{3,2,1,0:T(2,128)(2,1)S(1)}, u32[]{:S(2)}, u32[]{:S(2)}) collective-permute-start(bf16[8,4,2,512]{3,2,1,0:T(2,128)(2,1)} %param.6), channel_id=1, source_target_pairs={{0,16},{8,24},{16,0},{24,8},{1,17},{9,25},{17,1},{25,9},{2,18},{10... | collective-permute-start | bytes 196616 | tf_op jit(solution)/shard_map/ppermute | solution.py:363
  3.3 4.8 %copy-start.4 = (bf16[8,4,2,512]{3,2,1,0:T(2,128)(2,1)S(1)}, bf16[8,4,2,512]{3,2,1,0:T(2,128)(2,1)}, u32[]{:S(2)}) copy-start(bf16[8,4,2,512]{3,2,1,0:T(2,128)(2,1)} %param.6) | copy-start | bytes 196612
  3.3 5.0 %copy-start.3 = (bf16[3,3,3,512,128]{4,3,2,1,0:T(8,128)(2,1)S(1)}, bf16[3,3,3,512,128]{4,3,2,1,0:T(8,128)(2,1)}, u32[]{:S(2)}) copy-start(bf16[3,3,3,512,128]{4,3,2,1,0:T(8,128)(2,1)} %refs_4_.3) | copy-start | bytes 10616836
  4.5 8.0 %collective-permute-start.7 = (bf16[3,3,3,8,256]{4,3,2,1,0:T(8,128)(2,1)S(1)}, bf16[3,3,3,8,256]{4,3,2,1,0:T(8,128)(2,1)S(1)}, u32[]{:S(2)}, u32[]{:S(2)}) collective-permute-start(bf16[3,3,3,8,256]{4,3,2,1,0:T(8,128)(2,1)S(1)} %shard_map.66), channel_id=1, source_target_pairs={{0,6},{1,7},{2,4},{3,5},{4,2},{5,3},{6,0},{7,1},{8,14},{9,15},{10,... | collective-permute-start | bytes 331784 | tf_op jit(solution)/shard_map/ppermute | solution.py:363
  8.1 8.9 %collective-permute-start.6 = (bf16[3,3,3,8,256]{4,3,2,1,0:T(8,128)(2,1)S(1)}, bf16[3,3,3,8,256]{4,3,2,1,0:T(8,128)(2,1)S(1)}, u32[]{:S(2)}, u32[]{:S(2)}) collective-permute-start(bf16[3,3,3,8,256]{4,3,2,1,0:T(8,128)(2,1)S(1)} %shard_map.66), channel_id=1, source_target_pairs={{0,4},{1,5},{2,6},{3,7},{4,0},{5,1},{6,2},{7,3},{8,12},{9,13},{10,... | collective-permute-start | bytes 331784 | tf_op jit(solution)/shard_map/ppermute | solution.py:363
  8.3 10.3 %copy-start.1 = (bf16[512,256]{1,0:T(8,128)(2,1)S(1)}, bf16[512,256]{1,0:T(8,128)(2,1)}, u32[]{:S(2)}) copy-start(bf16[512,256]{1,0:T(8,128)(2,1)} %refs_4_.5) | copy-start | bytes 786436
  9.8 9.1 %collective-permute-start.5 = (bf16[4,128,128]{2,1,0:T(8,128)(2,1)S(1)}, bf16[4,128,128]{2,1,0:T(8,128)(2,1)S(1)}, u32[]{:S(2)}, u32[]{:S(2)}) collective-permute-start(bf16[4,128,128]{2,1,0:T(8,128)(2,1)S(1)} %shard_map.64.refs_0_), channel_id=1, source_target_pairs={{0,24},{8,16},{16,8},{24,0},{1,25},{9,17},{17,9},{25,1},{2,26},{10... | collective-permute-start | bytes 393224 | tf_op jit(solution)/shard_map/ppermute | solution.py:363
  12.0 6.9 %collective-permute-start.4 = (bf16[4,128,128]{2,1,0:T(8,128)(2,1)S(1)}, bf16[4,128,128]{2,1,0:T(8,128)(2,1)S(1)}, u32[]{:S(2)}, u32[]{:S(2)}) collective-permute-start(bf16[4,128,128]{2,1,0:T(8,128)(2,1)S(1)} %shard_map.64.refs_0_), channel_id=1, source_target_pairs={{0,16},{8,24},{16,0},{24,8},{1,17},{9,25},{17,1},{25,9},{2,18},{10... | collective-permute-start | bytes 393224 | tf_op jit(solution)/shard_map/ppermute | solution.py:363
  12.3 6.7 %collective-permute-start.3 = (bf16[4,128,128]{2,1,0:T(8,128)(2,1)S(1)}, bf16[4,128,128]{2,1,0:T(8,128)(2,1)S(1)}, u32[]{:S(2)}, u32[]{:S(2)}) collective-permute-start(bf16[4,128,128]{2,1,0:T(8,128)(2,1)S(1)} %shard_map.64.refs_0_), channel_id=1, source_target_pairs={{0,8},{8,0},{16,24},{24,16},{1,9},{9,1},{17,25},{25,17},{2,10},{10... | collective-permute-start | bytes 393224 | tf_op jit(solution)/shard_map/ppermute | solution.py:363
  12.5 7.8 %collective-permute-start.11 = (bf16[3,3,3,8,256]{4,3,2,1,0:T(8,128)(2,1)S(1)}, bf16[3,3,3,8,256]{4,3,2,1,0:T(8,128)(2,1)S(1)}, u32[]{:S(2)}, u32[]{:S(2)}) collective-permute-start(bf16[3,3,3,8,256]{4,3,2,1,0:T(8,128)(2,1)S(1)} %shard_map.66), channel_id=1, source_target_pairs={{0,2},{1,3},{2,0},{3,1},{4,6},{5,7},{6,4},{7,5},{8,10},{9,11},{10,... | collective-permute-start | bytes 331784 | tf_op jit(solution)/shard_map/ppermute | solution.py:363
  17.0 2.8 %collective-permute-start.8 = (bf16[3,3,3,3,8,256]{5,4,3,2,1,0:T(8,128)(2,1)S(1)}, bf16[3,3,3,3,8,256]{5,4,3,2,1,0:T(8,128)(2,1)S(1)}, u32[]{:S(2)}, u32[]{:S(2)}) collective-permute-start(bf16[3,3,3,3,8,256]{5,4,3,2,1,0:T(8,128)(2,1)S(1)} %pad_maximum_fusion), channel_id=1, source_target_pairs={{0,1},{1,0},{2,3},{3,2},{4,5},{5,4},{6,7},{7,6},{8,9},{9,8},{10,11... | collective-permute-start | bytes 995336 | tf_op jit(solution)/shard_map/ppermute | solution.py:363
  20.3 3.7 %collective-permute-start.12 = (bf16[1,3,3,3,8,256]{5,4,3,2,1,0:T(8,128)(2,1)S(1)}, bf16[1,3,3,3,8,256]{5,4,3,2,1,0:T(8,128)(2,1)S(1)}, u32[]{:S(2)}, u32[]{:S(2)}) collective-permute-start(bf16[1,3,3,3,8,256]{5,4,3,2,1,0:T(8,128)(2,1)S(1)} %bitcast.27), channel_id=1, source_target_pairs={{0,1},{1,0},{2,3},{3,2},{4,5},{5,4},{6,7},{7,6},{8,9},{9,8},{10,11... | collective-permute-start | bytes 331784 | tf_op jit(solution)/shard_map/ppermute | solution.py:363
  20.7 6.3 %collective-permute-start.9 = (bf16[2,128,256]{2,1,0:T(8,128)(2,1)S(1)}, bf16[2,128,256]{2,1,0:T(8,128)(2,1)S(1)}, u32[]{:S(2)}, u32[]{:S(2)}) collective-permute-start(bf16[2,128,256]{2,1,0:T(8,128)(2,1)S(1)} %get-tuple-element.18), channel_id=1, source_target_pairs={{1,2},{3,4},{5,6},{2,1},{4,3},{6,5},{9,10},{11,12},{13,14},{10,9},... | collective-permute-start | bytes 393224 | tf_op jit(solution)/shard_map/ppermute | solution.py:440
  23.8 3.2 %collective-permute-start.10 = (bf16[2,128,256]{2,1,0:T(8,128)(2,1)S(1)}, bf16[2,128,256]{2,1,0:T(8,128)(2,1)S(1)}, u32[]{:S(2)}, u32[]{:S(2)}) collective-permute-start(bf16[2,128,256]{2,1,0:T(8,128)(2,1)S(1)} %get-tuple-element.19), channel_id=1, source_target_pairs={{0,1},{1,0},{2,3},{3,2},{4,5},{5,4},{6,7},{7,6},{8,9},{9,8},{10,11... | collective-permute-start | bytes 393224 | tf_op jit(solution)/shard_map/ppermute | solution.py:363
  24.7 6.3 %copy-start = (bf16[3,3,3,128,128]{4,3,2,1,0:T(8,128)(2,1)S(1)}, bf16[3,3,3,128,128]{4,3,2,1,0:T(8,128)(2,1)}, u32[]{:S(2)}) copy-start(bf16[3,3,3,128,128]{4,3,2,1,0:T(8,128)(2,1)} %filters.1) | copy-start | bytes 2654212
  24.7 6.3 %copy-start.2 = (bf16[256,128]{1,0:T(8,128)(2,1)S(1)}, bf16[256,128]{1,0:T(8,128)(2,1)}, u32[]{:S(2)}) copy-start(bf16[256,128]{1,0:T(8,128)(2,1)} %refs_6_.1) | copy-start | bytes 196612
  28.3 3.1 %collective-permute-start.13 = (bf16[120,256]{1,0:T(8,128)(2,1)S(1)}, bf16[120,256]{1,0:T(8,128)(2,1)S(1)}, u32[]{:S(2)}, u32[]{:S(2)}) collective-permute-start(bf16[120,256]{1,0:T(8,128)(2,1)S(1)} %get-tuple-element.25), channel_id=1, source_target_pairs={{0,16},{8,24},{16,0},{24,8},{1,17},{9,25},{17,1},{25,9},{2,18},{10... | collective-permute-start | bytes 184328 | tf_op jit(solution)/shard_map/ppermute | solution.py:363
  29.6 4.0 %collective-permute-start.14 = (bf16[120,256]{1,0:T(8,128)(2,1)S(1)}, bf16[120,256]{1,0:T(8,128)(2,1)S(1)}, u32[]{:S(2)}, u32[]{:S(2)}) collective-permute-start(bf16[120,256]{1,0:T(8,128)(2,1)S(1)} %get-tuple-element.26), channel_id=1, source_target_pairs={{0,24},{8,16},{16,8},{24,0},{1,25},{9,17},{17,9},{25,1},{2,26},{10... | collective-permute-start | bytes 184328 | tf_op jit(solution)/shard_map/ppermute | solution.py:363
  30.8 3.2 %collective-permute-start.15 = (bf16[120,256]{1,0:T(8,128)(2,1)S(1)}, bf16[120,256]{1,0:T(8,128)(2,1)S(1)}, u32[]{:S(2)}, u32[]{:S(2)}) collective-permute-start(bf16[120,256]{1,0:T(8,128)(2,1)S(1)} %get-tuple-element.27), channel_id=1, source_target_pairs={{0,8},{8,0},{16,24},{24,16},{1,9},{9,1},{17,25},{25,17},{2,10},{10... | collective-permute-start | bytes 184328 | tf_op jit(solution)/shard_map/ppermute | solution.py:363

commit v8 on v7

--- a/solution.py
+++ b/solution.py
@@ -14,7 +14,7 @@
 BF16 = jnp.bfloat16
 
 
-def call(kernel, outs, scratch, flops, nbytes, *args, stay=()):
+def call(kernel, outs, scratch, flops, nbytes, *args, stay=(), far_out=False):
     args = [
         pltpu.with_memory_space_constraint(arg, pltpu.HBM) if n in stay else arg
         for n, arg in enumerate(args)
@@ -23,7 +23,7 @@
         kernel,
         out_shape=outs,
         in_specs=[FAR if n in stay else VMEM for n in range(len(args))],
-        out_specs=jax.tree.map(lambda _: VMEM, outs),
+        out_specs=jax.tree.map(lambda _: FAR if far_out else VMEM, outs),
         scratch_shapes=scratch,
         compiler_params=pltpu.CompilerParams(vmem_limit_bytes=40 << 20),
         cost_estimate=pl.CostEstimate(flops=flops, bytes_accessed=nbytes, transcendentals=0),
@@ -204,10 +204,10 @@
 
 def fine_kernel(groups, frames, *refs):
     chunks = dict(zip(chunk_order(groups), refs[:groups]))
-    block, spread, proj, filters, out, acts, acts_odd, lows = refs[groups:]
-    extent, cells = block.shape[:2]
-    pairs, rows = extent - 1, cells // frames - 2
-    width = proj.shape[1]
+    base, spread, filters, out, acts, acts_odd, lows, ready, sent = refs[groups:]
+    extent, rows = base.shape[0], base.shape[1] - 2
+    pairs = extent - 1
+    width = base.shape[3]
     tall, broad = 2 * rows, 2 * (extent - 2)
     me, last_me = lax.axis_index("grp"), lax.axis_size("grp") - 1
     tile, last_tile = lax.axis_index("tile"), lax.axis_size("tile") - 1
@@ -216,8 +216,6 @@
         term = dot(chunks[k][...], spread[k])
         total = term if total is None else total + term
     total = total.reshape(pairs, rows + 1, frames, 4 * width)
-    base = dot(block[...].reshape(extent * cells, block.shape[2]), proj[...])
-    base = base.reshape(extent, rows + 2, frames, width)
     nothing = jnp.zeros((1, frames, width), F32)
     for col in range(broad + 2):
         pair, side = divmod(col, 2)
@@ -270,7 +268,10 @@
             fields.append(sums[pair, :, :, side * width : (side + 1) * width] + low)
         field = jnp.stack(fields, axis=1)
         for row in range(tall):
-            out[:, 2 * row + p] = jnp.swapaxes(field[row], 0, 1).astype(BF16)
+            ready[p, :, row] = jnp.swapaxes(field[row], 0, 1).astype(BF16)
+        pltpu.make_async_copy(ready.at[p], out.at[:, :, p], sent.at[p]).start()
+    for p in range(2):
+        pltpu.make_async_copy(ready.at[p], out.at[:, :, p], sent.at[p]).wait()
 
 
 def fold_middle_kernel(pieces, out):
@@ -321,7 +322,10 @@
     out[...] = value.astype(BF16)
 
 
-def prepare_kernel(groups, parts, filters, proj, folded, spread, plain):
+def prepare_kernel(groups, parts, frames, block, filters, proj, folded, spread, base, plain):
+    extent, cells, wide = block.shape
+    low = dot(block[...].reshape(extent * cells, wide), proj[...])
+    base[...] = low.reshape(base.shape)
     def per_step(step, carry):
         taps = [[filters[step, r, c].astype(F32) for c in range(3)] for r in range(3)]
         for p in range(2):
@@ -476,35 +480,40 @@
         mid_folded,
     )
     chunks = [chunks[0]] + [exchange(chunks[k], "grp", k) for k in range(1, groups)]
-    fine_folded, spread = call(
-        functools.partial(prepare_kernel, groups, shares),
+    fine_folded, spread, base = call(
+        functools.partial(prepare_kernel, groups, shares, frames),
         (
             jax.ShapeDtypeStruct((3, 2, 2, 2 * depth2, 2 * depth2), BF16),
             jax.ShapeDtypeStruct((groups, lanes, 4 * depth2), BF16),
+            jax.ShapeDtypeStruct((cols + 2, rows + 2, frames, depth2), F32),
         ),
         [pltpu.VMEM((depth1, depth2), F32)],
         10**6,
         4 * 10**6,
+        block,
         fine_filters,
         mid_proj,
     )
     tall, broad = 2 * rows, 2 * cols
-    return call(
+    out = call(
         functools.partial(fine_kernel, groups, frames),
-        jax.ShapeDtypeStruct((frames, 2 * tall, 2 * broad, depth2), BF16),
+        jax.ShapeDtypeStruct((frames, tall, 2, 2 * broad, depth2), BF16),
         [
             pltpu.VMEM((3, broad + 2, (tall + 2) * frames, depth2), BF16),
             pltpu.VMEM((3, broad + 2, tall * frames, depth2), BF16),
             pltpu.VMEM((broad + 2, tall, frames, depth2), F32),
+            pltpu.VMEM((2, frames, tall, 2 * broad, depth2), BF16),
+            pltpu.SemaphoreType.DMA((2,)),
         ],
         2 * 24 * (broad + 1) * tall * frames * depth2 * 2 * depth2,
         3 * 10**6,
         *[chunks[k] for k in chunk_order(groups)],
-        block,
+        base,
         spread,
-        mid_proj,
         fine_folded,
-    )
+        far_out=True,
+    )
+    return out.reshape(frames, 2 * tall, 2 * broad, depth2)
 
 
 def solution(mesh):

time: 36.4 us -> 36.3 us (level)
  no operation moved by 1% of the time
where the time goes in v8:
time: 36.3 us; the launch traced here: 35.8 us
  starting transfers between devices  19.8 us (55%)
  Pallas kernels  7.85 us (22%)
  waiting for transfers between devices  7.65 us (21%)
    ppermute x15, starting transfers between devices, exchange(): return lax.ppermute(values, axis, [(i, i ^ k) for i in range(size)])  16.7 us
    pallas_call x8, Pallas kernels, call(): pl.pallas_call(kernel, out_shape=outs, in_specs=[FAR if n in stay else VM...  7.85 us
    ppermute x15, waiting for transfers between devices, exchange(): return lax.ppermute(values, axis, [(i, i ^ k) for i in range(size)])  5.38 us
    ppermute x1, starting transfers between devices, body(): lax.ppermute(odd_out, 'tile', odd_pairs + [(j, i) for i, j in odd_pairs])  3.1 us
    ppermute x1, waiting for transfers between devices, body(): lax.ppermute(odd_out, 'tile', odd_pairs + [(j, i) for i, j in odd_pairs])  2.26 us
  transfers between devices with their start and end apart: 16, of which 5 were waited for; matrix products, arithmetic and copies ran while one was open for 1% of the time, Pallas kernels for 13%

profile of v8, /device:TPU:1, one launch (start us, length us, event | category | flops | bytes accessed | tf_op | source)
XLA Modules:
  0.0 35.8 jit_solution(17642240239216354021)
XLA Ops:
  0.0 2.0 %collective-permute-start = (bf16[8,4,2,512]{3,2,1,0:T(2,128)(2,1)}, bf16[8,4,2,512]{3,2,1,0:T(2,128)(2,1)S(1)}, u32[]{:S(2)}, u32[]{:S(2)}) collective-permute-start(bf16[8,4,2,512]{3,2,1,0:T(2,128)(2,1)} %param.6), channel_id=1, source_target_pairs={{0,8},{8,0},{16,24},{24,16},{1,9},{9,1},{17,25},{25,17},{2,10},{10... | collective-permute-start | bytes 196616 | tf_op jit(solution)/shard_map/ppermute | solution.py:367
  2.0 1.2 %collective-permute-start.2 = (bf16[8,4,2,512]{3,2,1,0:T(2,128)(2,1)}, bf16[8,4,2,512]{3,2,1,0:T(2,128)(2,1)S(1)}, u32[]{:S(2)}, u32[]{:S(2)}) collective-permute-start(bf16[8,4,2,512]{3,2,1,0:T(2,128)(2,1)} %param.6), channel_id=1, source_target_pairs={{0,24},{8,16},{16,8},{24,0},{1,25},{9,17},{17,9},{25,1},{2,26},{10... | collective-permute-start | bytes 196616 | tf_op jit(solution)/shard_map/ppermute | solution.py:367
  3.3 1.2 %shard_map.66 = bf16[3,3,3,8,256]{4,3,2,1,0:T(8,128)(2,1)S(1)} custom-call(bf16[3,3,3,32,256]{4,3,2,1,0:T(8,128)(2,1)} %bitcast.31), custom_call_target="tpu_custom_call" | custom-call | flops 6000000000 | bytes 1000000 | tf_op jit(solution)/shard_map/pallas_call | solution.py:22
  4.5 3.6 %collective-permute-start.7 = (bf16[3,3,3,8,256]{4,3,2,1,0:T(8,128)(2,1)S(1)}, bf16[3,3,3,8,256]{4,3,2,1,0:T(8,128)(2,1)S(1)}, u32[]{:S(2)}, u32[]{:S(2)}) collective-permute-start(bf16[3,3,3,8,256]{4,3,2,1,0:T(8,128)(2,1)S(1)} %shard_map.66), channel_id=1, source_target_pairs={{0,6},{1,7},{2,4},{3,5},{4,2},{5,3},{6,0},{7,1},{8,14},{9,15},{10,... | collective-permute-start | bytes 331784 | tf_op jit(solution)/shard_map/ppermute | solution.py:367
  8.3 1.5 %shard_map.64.refs_0_ = bf16[4,128,128]{2,1,0:T(8,128)(2,1)S(1)} custom-call(bf16[4,2,8,512]{3,2,1,0:T(8,128)(2,1)S(1)} %bitcast.20, bf16[4,2,8,512]{3,2,1,0:T(8,128)(2,1)S(1)} %bitcast.22, bf16[4,2,8,512]{3,2,1,0:T(8,128)(2,1)S(1)} %bitcast.26, bf16[4,2,8,512]{3,2,1,0:T(8,128)(2,1)S(1)} %bitcast.24, bf16[3,3,3,512,128]{4,3,2,1,0:T(8,128)(2,1)S(1)} %copy-done.3), custom_call_target="tpu_custom_call" | custom-call | flops 2000000000 | bytes 100000 | tf_op jit(solution)/shard_map/pallas_call | solution.py:22
  9.8 2.2 %collective-permute-start.5 = (bf16[4,128,128]{2,1,0:T(8,128)(2,1)S(1)}, bf16[4,128,128]{2,1,0:T(8,128)(2,1)S(1)}, u32[]{:S(2)}, u32[]{:S(2)}) collective-permute-start(bf16[4,128,128]{2,1,0:T(8,128)(2,1)S(1)} %shard_map.64.refs_0_), channel_id=1, source_target_pairs={{0,24},{8,16},{16,8},{24,0},{1,25},{9,17},{17,9},{25,1},{2,26},{10... | collective-permute-start | bytes 393224 | tf_op jit(solution)/shard_map/ppermute | solution.py:367
  12.5 2.4 %collective-permute-start.11 = (bf16[3,3,3,8,256]{4,3,2,1,0:T(8,128)(2,1)S(1)}, bf16[3,3,3,8,256]{4,3,2,1,0:T(8,128)(2,1)S(1)}, u32[]{:S(2)}, u32[]{:S(2)}) collective-permute-start(bf16[3,3,3,8,256]{4,3,2,1,0:T(8,128)(2,1)S(1)} %shard_map.66), channel_id=1, source_target_pairs={{0,2},{1,3},{2,0},{3,1},{4,6},{5,7},{6,4},{7,5},{8,10},{9,11},{10,... | collective-permute-start | bytes 331784 | tf_op jit(solution)/shard_map/ppermute | solution.py:367
  14.9 2.1 %collective-permute-done.6 = bf16[3,3,3,8,256]{4,3,2,1,0:T(8,128)(2,1)S(1)} collective-permute-done((bf16[3,3,3,8,256]{4,3,2,1,0:T(8,128)(2,1)S(1)}, bf16[3,3,3,8,256]{4,3,2,1,0:T(8,128)(2,1)S(1)}, u32[]{:S(2)}, u32[]{:S(2)}) %collective-permute-start.6) | collective-permute-done | bytes 110624 | tf_op jit(solution)/shard_map/ppermute | solution.py:367
  17.0 1.6 %collective-permute-start.8 = (bf16[3,3,3,3,8,256]{5,4,3,2,1,0:T(8,128)(2,1)S(1)}, bf16[3,3,3,3,8,256]{5,4,3,2,1,0:T(8,128)(2,1)S(1)}, u32[]{:S(2)}, u32[]{:S(2)}) collective-permute-start(bf16[3,3,3,3,8,256]{5,4,3,2,1,0:T(8,128)(2,1)S(1)} %pad_maximum_fusion), channel_id=1, source_target_pairs={{0,1},{1,0},{2,3},{3,2},{4,5},{5,4},{6,7},{7,6},{8,9},{9,8},{10,11... | collective-permute-start | bytes 995336 | tf_op jit(solution)/shard_map/ppermute | solution.py:367
  18.6 0.3 shard_map.65.refs_5_
  18.9 0.9 %collective-permute-done.8.refs_6_ = bf16[3,3,3,3,8,256]{5,4,3,2,1,0:T(8,128)(2,1)S(1)} collective-permute-done((bf16[3,3,3,3,8,256]{5,4,3,2,1,0:T(8,128)(2,1)S(1)}, bf16[3,3,3,3,8,256]{5,4,3,2,1,0:T(8,128)(2,1)S(1)}, u32[]{:S(2)}, u32[]{:S(2)}) %collective-permute-start.8) | collective-permute-done | bytes 331808 | tf_op jit(solution)/shard_map/ppermute | solution.py:367
  19.9 0.4 %shard_map.67 = (bf16[2,128,256]{2,1,0:T(8,128)(2,1)S(1)}, bf16[2,128,256]{2,1,0:T(8,128)(2,1)S(1)}, f32[4,128,256]{2,1,0:T(8,128)S(1)}) custom-call(bf16[4,128,128]{2,1,0:T(8,128)(2,1)S(1)} %shard_map.64.refs_0_, bf16[4,128,128]{2,1,0:T(8,128)(2,1)S(1)} %collective-permute-done.3.refs_1_, bf16[4,128,128]{2,1,0:T(8,128)(2,1)S(1)} %collective-permute-done.4.refs_2_, ...), custom_call_target="tpu_custom_call" | custom-call | flops 134217728 | bytes 2000000 | tf_op jit(solution)/shard_map/pallas_call | solution.py:22
  20.3 0.4 %collective-permute-start.12 = (bf16[1,3,3,3,8,256]{5,4,3,2,1,0:T(8,128)(2,1)S(1)}, bf16[1,3,3,3,8,256]{5,4,3,2,1,0:T(8,128)(2,1)S(1)}, u32[]{:S(2)}, u32[]{:S(2)}) collective-permute-start(bf16[1,3,3,3,8,256]{5,4,3,2,1,0:T(8,128)(2,1)S(1)} %bitcast.28), channel_id=1, source_target_pairs={{0,1},{1,0},{2,3},{3,2},{4,5},{5,4},{6,7},{7,6},{8,9},{9,8},{10,11... | collective-permute-start | bytes 331784 | tf_op jit(solution)/shard_map/ppermute | solution.py:367
  20.7 3.1 %collective-permute-start.9 = (bf16[2,128,256]{2,1,0:T(8,128)(2,1)S(1)}, bf16[2,128,256]{2,1,0:T(8,128)(2,1)S(1)}, u32[]{:S(2)}, u32[]{:S(2)}) collective-permute-start(bf16[2,128,256]{2,1,0:T(8,128)(2,1)S(1)} %get-tuple-element.19), channel_id=1, source_target_pairs={{1,2},{3,4},{5,6},{2,1},{4,3},{6,5},{9,10},{11,12},{13,14},{10,9},... | collective-permute-start | bytes 393224 | tf_op jit(solution)/shard_map/ppermute | solution.py:444
  24.1 0.7 %shard_map.68.filters = bf16[3,3,2,256,256]{4,3,2,1,0:T(8,128)(2,1)S(1)} custom-call(bf16[8,3,3,3,8,256]{5,4,3,2,1,0:T(8,128)(2,1)S(1)} %slice_dynamic-update-slice_fusion.pieces), custom_call_target="tpu_custom_call" | custom-call | flops 1000000 | bytes 4000000 | tf_op jit(solution)/shard_map/pallas_call | solution.py:22
  24.7 2.3 %collective-permute-done.9.odd_in = bf16[2,128,256]{2,1,0:T(8,128)(2,1)S(1)} collective-permute-done((bf16[2,128,256]{2,1,0:T(8,128)(2,1)S(1)}, bf16[2,128,256]{2,1,0:T(8,128)(2,1)S(1)}, u32[]{:S(2)}, u32[]{:S(2)}) %collective-permute-start.9) | collective-permute-done | bytes 131104 | tf_op jit(solution)/shard_map/ppermute | solution.py:444
  27.0 1.3 %shard_map.69 = (bf16[120,256]{1,0:T(8,128)(2,1)S(1)}, bf16[120,256]{1,0:T(8,128)(2,1)S(1)}, bf16[120,256]{1,0:T(8,128)(2,1)S(1)}, bf16[120,256]{1,0:T(8,128)(2,1)S(1)}, bf16[4,48,256]{2,1,0:T(8,128)(2,1)S(1)}) custom-call(bf16[2,128,256]{2,1,0:T(8,128)(2,1)S(1)} %collective-permute-done.9.odd_in, bf16[2,128,256]{2,1,0:T(8,128)(2,1)S(1)} %collective-permute-done.10.even_in, ...), custom_call_target="tpu_custom_call" | custom-call | flops 905969664 | bytes 5000000 | tf_op jit(solution)/shard_map/pallas_call | solution.py:22
  28.3 1.3 %collective-permute-start.13 = (bf16[120,256]{1,0:T(8,128)(2,1)S(1)}, bf16[120,256]{1,0:T(8,128)(2,1)S(1)}, u32[]{:S(2)}, u32[]{:S(2)}) collective-permute-start(bf16[120,256]{1,0:T(8,128)(2,1)S(1)} %get-tuple-element.26), channel_id=1, source_target_pairs={{0,16},{8,24},{16,0},{24,8},{1,17},{9,25},{17,1},{25,9},{2,18},{10... | collective-permute-start | bytes 184328 | tf_op jit(solution)/shard_map/ppermute | solution.py:367
  29.6 1.2 %collective-permute-start.14 = (bf16[120,256]{1,0:T(8,128)(2,1)S(1)}, bf16[120,256]{1,0:T(8,128)(2,1)S(1)}, u32[]{:S(2)}, u32[]{:S(2)}) collective-permute-start(bf16[120,256]{1,0:T(8,128)(2,1)S(1)} %get-tuple-element.27), channel_id=1, source_target_pairs={{0,24},{8,16},{16,8},{24,0},{1,25},{9,17},{17,9},{25,1},{2,26},{10... | collective-permute-start | bytes 184328 | tf_op jit(solution)/shard_map/ppermute | solution.py:367
  30.8 0.3 collective-permute-start.15
  31.0 0.6 %shard_map.70 = (bf16[3,2,2,256,256]{4,3,2,1,0:T(8,128)(2,1)S(1)}, bf16[4,256,512]{2,1,0:T(8,128)(2,1)S(1)}, f32[4,6,8,128]{3,2,1,0:T(8,128)S(1)}) custom-call(bf16[4,48,256]{2,1,0:T(8,128)(2,1)S(1)} %get-tuple-element.29.block, bf16[3,3,3,128,128]{4,3,2,1,0:T(8,128)(2,1)S(1)} %copy-done, bf16[256,128]{1,0:T(8,128)(2,1)S(1)} %copy-done.2), custom_call_target="tpu_custom_call" | custom-call | flops 1000000 | bytes 4000000 | tf_op jit(solution)/shard_map/pallas_call | solution.py:22
  31.6 2.1 %collective-permute-done.14.refs_2_ = bf16[120,256]{1,0:T(8,128)(2,1)S(1)} collective-permute-done((bf16[120,256]{1,0:T(8,128)(2,1)S(1)}, bf16[120,256]{1,0:T(8,128)(2,1)S(1)}, u32[]{:S(2)}, u32[]{:S(2)}) %collective-permute-start.14) | collective-permute-done | bytes 61472 | tf_op jit(solution)/shard_map/ppermute | solution.py:367
  33.7 0.3 collective-permute-done.15.refs_3_
  34.0 1.9 %shard_map.71 = bf16[8,8,2,8,128]{4,3,2,1,0:T(8,128)(2,1)} custom-call(bf16[120,256]{1,0:T(8,128)(2,1)S(1)} %get-tuple-element.25.refs_0_, bf16[120,256]{1,0:T(8,128)(2,1)S(1)} %collective-permute-done.13.refs_1_, bf16[120,256]{1,0:T(8,128)(2,1)S(1)} %collective-permute-done.14.refs_2_, bf16[120,256]{1,0:T(8,128)(2,1)S(1)} %collective-permute-done.15.refs_3_, ...), custom_call_target="tpu_custom_call" | custom-call | flops 503316480 | bytes 3000000 | tf_op jit(solution)/shard_map/pallas_call | solution.py:22
  (37 shorter events, 0.9 us)
Async XLA Ops:
  0.0 8.1 %collective-permute-start = (bf16[8,4,2,512]{3,2,1,0:T(2,128)(2,1)}, bf16[8,4,2,512]{3,2,1,0:T(2,128)(2,1)S(1)}, u32[]{:S(2)}, u32[]{:S(2)}) collective-permute-start(bf16[8,4,2,512]{3,2,1,0:T(2,128)(2,1)} %param.6), channel_id=1, source_target_pairs={{0,8},{8,0},{16,24},{24,16},{1,9},{9,1},{17,25},{25,17},{2,10},{10... | collective-permute-start | bytes 196616 | tf_op jit(solution)/shard_map/ppermute | solution.py:367
  2.0 6.1 %collective-permute-start.2 = (bf16[8,4,2,512]{3,2,1,0:T(2,128)(2,1)}, bf16[8,4,2,512]{3,2,1,0:T(2,128)(2,1)S(1)}, u32[]{:S(2)}, u32[]{:S(2)}) collective-permute-start(bf16[8,4,2,512]{3,2,1,0:T(2,128)(2,1)} %param.6), channel_id=1, source_target_pairs={{0,24},{8,16},{16,8},{24,0},{1,25},{9,17},{17,9},{25,1},{2,26},{10... | collective-permute-start | bytes 196616 | tf_op jit(solution)/shard_map/ppermute | solution.py:367
  3.3 5.0 %collective-permute-start.1 = (bf16[8,4,2,512]{3,2,1,0:T(2,128)(2,1)}, bf16[8,4,2,512]{3,2,1,0:T(2,128)(2,1)S(1)}, u32[]{:S(2)}, u32[]{:S(2)}) collective-permute-start(bf16[8,4,2,512]{3,2,1,0:T(2,128)(2,1)} %param.6), channel_id=1, source_target_pairs={{0,16},{8,24},{16,0},{24,8},{1,17},{9,25},{17,1},{25,9},{2,18},{10... | collective-permute-start | bytes 196616 | tf_op jit(solution)/shard_map/ppermute | solution.py:367
  3.3 4.8 %copy-start.4 = (bf16[8,4,2,512]{3,2,1,0:T(2,128)(2,1)S(1)}, bf16[8,4,2,512]{3,2,1,0:T(2,128)(2,1)}, u32[]{:S(2)}) copy-start(bf16[8,4,2,512]{3,2,1,0:T(2,128)(2,1)} %param.6) | copy-start | bytes 196612
  3.3 5.0 %copy-start.3 = (bf16[3,3,3,512,128]{4,3,2,1,0:T(8,128)(2,1)S(1)}, bf16[3,3,3,512,128]{4,3,2,1,0:T(8,128)(2,1)}, u32[]{:S(2)}) copy-start(bf16[3,3,3,512,128]{4,3,2,1,0:T(8,128)(2,1)} %refs_4_.3) | copy-start | bytes 10616836
  4.5 8.0 %collective-permute-start.7 = (bf16[3,3,3,8,256]{4,3,2,1,0:T(8,128)(2,1)S(1)}, bf16[3,3,3,8,256]{4,3,2,1,0:T(8,128)(2,1)S(1)}, u32[]{:S(2)}, u32[]{:S(2)}) collective-permute-start(bf16[3,3,3,8,256]{4,3,2,1,0:T(8,128)(2,1)S(1)} %shard_map.66), channel_id=1, source_target_pairs={{0,6},{1,7},{2,4},{3,5},{4,2},{5,3},{6,0},{7,1},{8,14},{9,15},{10,... | collective-permute-start | bytes 331784 | tf_op jit(solution)/shard_map/ppermute | solution.py:367
  8.1 8.9 %collective-permute-start.6 = (bf16[3,3,3,8,256]{4,3,2,1,0:T(8,128)(2,1)S(1)}, bf16[3,3,3,8,256]{4,3,2,1,0:T(8,128)(2,1)S(1)}, u32[]{:S(2)}, u32[]{:S(2)}) collective-permute-start(bf16[3,3,3,8,256]{4,3,2,1,0:T(8,128)(2,1)S(1)} %shard_map.66), channel_id=1, source_target_pairs={{0,4},{1,5},{2,6},{3,7},{4,0},{5,1},{6,2},{7,3},{8,12},{9,13},{10,... | collective-permute-start | bytes 331784 | tf_op jit(solution)/shard_map/ppermute | solution.py:367
  8.3 10.3 %copy-start.1 = (bf16[512,256]{1,0:T(8,128)(2,1)S(1)}, bf16[512,256]{1,0:T(8,128)(2,1)}, u32[]{:S(2)}) copy-start(bf16[512,256]{1,0:T(8,128)(2,1)} %refs_4_.5) | copy-start | bytes 786436
  9.8 9.1 %collective-permute-start.5 = (bf16[4,128,128]{2,1,0:T(8,128)(2,1)S(1)}, bf16[4,128,128]{2,1,0:T(8,128)(2,1)S(1)}, u32[]{:S(2)}, u32[]{:S(2)}) collective-permute-start(bf16[4,128,128]{2,1,0:T(8,128)(2,1)S(1)} %shard_map.64.refs_0_), channel_id=1, source_target_pairs={{0,24},{8,16},{16,8},{24,0},{1,25},{9,17},{17,9},{25,1},{2,26},{10... | collective-permute-start | bytes 393224 | tf_op jit(solution)/shard_map/ppermute | solution.py:367
  12.0 6.9 %collective-permute-start.4 = (bf16[4,128,128]{2,1,0:T(8,128)(2,1)S(1)}, bf16[4,128,128]{2,1,0:T(8,128)(2,1)S(1)}, u32[]{:S(2)}, u32[]{:S(2)}) collective-permute-start(bf16[4,128,128]{2,1,0:T(8,128)(2,1)S(1)} %shard_map.64.refs_0_), channel_id=1, source_target_pairs={{0,16},{8,24},{16,0},{24,8},{1,17},{9,25},{17,1},{25,9},{2,18},{10... | collective-permute-start | bytes 393224 | tf_op jit(solution)/shard_map/ppermute | solution.py:367
  12.3 6.7 %collective-permute-start.3 = (bf16[4,128,128]{2,1,0:T(8,128)(2,1)S(1)}, bf16[4,128,128]{2,1,0:T(8,128)(2,1)S(1)}, u32[]{:S(2)}, u32[]{:S(2)}) collective-permute-start(bf16[4,128,128]{2,1,0:T(8,128)(2,1)S(1)} %shard_map.64.refs_0_), channel_id=1, source_target_pairs={{0,8},{8,0},{16,24},{24,16},{1,9},{9,1},{17,25},{25,17},{2,10},{10... | collective-permute-start | bytes 393224 | tf_op jit(solution)/shard_map/ppermute | solution.py:367
  12.5 7.8 %collective-permute-start.11 = (bf16[3,3,3,8,256]{4,3,2,1,0:T(8,128)(2,1)S(1)}, bf16[3,3,3,8,256]{4,3,2,1,0:T(8,128)(2,1)S(1)}, u32[]{:S(2)}, u32[]{:S(2)}) collective-permute-start(bf16[3,3,3,8,256]{4,3,2,1,0:T(8,128)(2,1)S(1)} %shard_map.66), channel_id=1, source_target_pairs={{0,2},{1,3},{2,0},{3,1},{4,6},{5,7},{6,4},{7,5},{8,10},{9,11},{10,... | collective-permute-start | bytes 331784 | tf_op jit(solution)/shard_map/ppermute | solution.py:367
  17.0 2.8 %collective-permute-start.8 = (bf16[3,3,3,3,8,256]{5,4,3,2,1,0:T(8,128)(2,1)S(1)}, bf16[3,3,3,3,8,256]{5,4,3,2,1,0:T(8,128)(2,1)S(1)}, u32[]{:S(2)}, u32[]{:S(2)}) collective-permute-start(bf16[3,3,3,3,8,256]{5,4,3,2,1,0:T(8,128)(2,1)S(1)} %pad_maximum_fusion), channel_id=1, source_target_pairs={{0,1},{1,0},{2,3},{3,2},{4,5},{5,4},{6,7},{7,6},{8,9},{9,8},{10,11... | collective-permute-start | bytes 995336 | tf_op jit(solution)/shard_map/ppermute | solution.py:367
  20.3 3.7 %collective-permute-start.12 = (bf16[1,3,3,3,8,256]{5,4,3,2,1,0:T(8,128)(2,1)S(1)}, bf16[1,3,3,3,8,256]{5,4,3,2,1,0:T(8,128)(2,1)S(1)}, u32[]{:S(2)}, u32[]{:S(2)}) collective-permute-start(bf16[1,3,3,3,8,256]{5,4,3,2,1,0:T(8,128)(2,1)S(1)} %bitcast.28), channel_id=1, source_target_pairs={{0,1},{1,0},{2,3},{3,2},{4,5},{5,4},{6,7},{7,6},{8,9},{9,8},{10,11... | collective-permute-start | bytes 331784 | tf_op jit(solution)/shard_map/ppermute | solution.py:367
  20.7 6.3 %collective-permute-start.9 = (bf16[2,128,256]{2,1,0:T(8,128)(2,1)S(1)}, bf16[2,128,256]{2,1,0:T(8,128)(2,1)S(1)}, u32[]{:S(2)}, u32[]{:S(2)}) collective-permute-start(bf16[2,128,256]{2,1,0:T(8,128)(2,1)S(1)} %get-tuple-element.19), channel_id=1, source_target_pairs={{1,2},{3,4},{5,6},{2,1},{4,3},{6,5},{9,10},{11,12},{13,14},{10,9},... | collective-permute-start | bytes 393224 | tf_op jit(solution)/shard_map/ppermute | solution.py:444
  23.8 3.2 %collective-permute-start.10 = (bf16[2,128,256]{2,1,0:T(8,128)(2,1)S(1)}, bf16[2,128,256]{2,1,0:T(8,128)(2,1)S(1)}, u32[]{:S(2)}, u32[]{:S(2)}) collective-permute-start(bf16[2,128,256]{2,1,0:T(8,128)(2,1)S(1)} %get-tuple-element.20), channel_id=1, source_target_pairs={{0,1},{1,0},{2,3},{3,2},{4,5},{5,4},{6,7},{7,6},{8,9},{9,8},{10,11... | collective-permute-start | bytes 393224 | tf_op jit(solution)/shard_map/ppermute | solution.py:367
  24.7 6.3 %copy-start = (bf16[3,3,3,128,128]{4,3,2,1,0:T(8,128)(2,1)S(1)}, bf16[3,3,3,128,128]{4,3,2,1,0:T(8,128)(2,1)}, u32[]{:S(2)}) copy-start(bf16[3,3,3,128,128]{4,3,2,1,0:T(8,128)(2,1)} %filters.1) | copy-start | bytes 2654212
  24.7 6.3 %copy-start.2 = (bf16[256,128]{1,0:T(8,128)(2,1)S(1)}, bf16[256,128]{1,0:T(8,128)(2,1)}, u32[]{:S(2)}) copy-start(bf16[256,128]{1,0:T(8,128)(2,1)} %proj.1) | copy-start | bytes 196612
  28.3 3.3 %collective-permute-start.13 = (bf16[120,256]{1,0:T(8,128)(2,1)S(1)}, bf16[120,256]{1,0:T(8,128)(2,1)S(1)}, u32[]{:S(2)}, u32[]{:S(2)}) collective-permute-start(bf16[120,256]{1,0:T(8,128)(2,1)S(1)} %get-tuple-element.26), channel_id=1, source_target_pairs={{0,16},{8,24},{16,0},{24,8},{1,17},{9,25},{17,1},{25,9},{2,18},{10... | collective-permute-start | bytes 184328 | tf_op jit(solution)/shard_map/ppermute | solution.py:367
  29.6 4.0 %collective-permute-start.14 = (bf16[120,256]{1,0:T(8,128)(2,1)S(1)}, bf16[120,256]{1,0:T(8,128)(2,1)S(1)}, u32[]{:S(2)}, u32[]{:S(2)}) collective-permute-start(bf16[120,256]{1,0:T(8,128)(2,1)S(1)} %get-tuple-element.27), channel_id=1, source_target_pairs={{0,24},{8,16},{16,8},{24,0},{1,25},{9,17},{17,9},{25,1},{2,26},{10... | collective-permute-start | bytes 184328 | tf_op jit(solution)/shard_map/ppermute | solution.py:367
  30.8 3.2 %collective-permute-start.15 = (bf16[120,256]{1,0:T(8,128)(2,1)S(1)}, bf16[120,256]{1,0:T(8,128)(2,1)S(1)}, u32[]{:S(2)}, u32[]{:S(2)}) collective-permute-start(bf16[120,256]{1,0:T(8,128)(2,1)S(1)} %get-tuple-element.28), channel_id=1, source_target_pairs={{0,8},{8,0},{16,24},{24,16},{1,9},{9,1},{17,25},{25,17},{2,10},{10... | collective-permute-start | bytes 184328 | tf_op jit(solution)/shard_map/ppermute | solution.py:367

commit v9 on v7

--- a/solution.py
+++ b/solution.py
@@ -122,9 +122,9 @@
     total = total.reshape(extent, cells, outputs)
     cols = extent - 2
     middle = total[1 : cols + 1] + straight[...].reshape(cols, cells, outputs)
-    own[0] = total[0]
-    own[1 : cols + 1] = middle
-    own[cols + 1] = total[cols + 1]
+    own[0] = total[0].astype(BF16)
+    own[1 : cols + 1] = middle.astype(BF16)
+    own[cols + 1] = total[cols + 1].astype(BF16)
     left = jnp.stack([total[0], middle[0]])
     right = jnp.stack([middle[cols - 1], total[cols + 1]])
     odd = lax.axis_index("tile") % 2 == 1
@@ -146,7 +146,7 @@
     from_right = jnp.where(odd, odd_got, even_got)
     values = []
     for col in range(extent):
-        value = own[col]
+        value = own[col].astype(F32)
         if col < 2:
             value = value + from_left[col]
         if col >= cols:
@@ -426,7 +426,7 @@
         (
             jax.ShapeDtypeStruct((2, cells, depth1), BF16),
             jax.ShapeDtypeStruct((2, cells, depth1), BF16),
-            jax.ShapeDtypeStruct((cols + 2, cells, depth1), F32),
+            jax.ShapeDtypeStruct((cols + 2, cells, depth1), BF16),
         ),
         [],
         2 * cells * (cols + 2) * depth0 * depth1,

time: 36.4 us -> 36.4 us (level)
  no operation moved by 1% of the time
where the time goes in v9:
time: 36.4 us; the launch traced here: 35.9 us
  starting transfers between devices  19.8 us (54%)
  waiting for transfers between devices  7.82 us (21%)
  Pallas kernels  7.73 us (21%)
    ppermute x15, starting transfers between devices, exchange(): return lax.ppermute(values, axis, [(i, i ^ k) for i in range(size)])  16.7 us
    pallas_call x8, Pallas kernels, call(): pl.pallas_call(kernel, out_shape=outs, in_specs=[FAR if n in stay else VM...  7.73 us
    ppermute x15, waiting for transfers between devices, exchange(): return lax.ppermute(values, axis, [(i, i ^ k) for i in range(size)])  5.55 us
    ppermute x1, starting transfers between devices, body(): lax.ppermute(odd_out, 'tile', odd_pairs + [(j, i) for i, j in odd_pairs])  3.1 us
    ppermute x1, waiting for transfers between devices, body(): lax.ppermute(odd_out, 'tile', odd_pairs + [(j, i) for i, j in odd_pairs])  2.26 us
  transfers between devices with their start and end apart: 16, of which 5 were waited for; matrix products, arithmetic and copies ran while one was open for 1% of the time, Pallas kernels for 13%

profile of v9, /device:TPU:1, one launch (start us, length us, event | category | flops | bytes accessed | tf_op | source)
XLA Modules:
  0.0 35.9 jit_solution(8670430745069409289)
XLA Ops:
  0.0 2.0 %collective-permute-start = (bf16[8,4,2,512]{3,2,1,0:T(2,128)(2,1)}, bf16[8,4,2,512]{3,2,1,0:T(2,128)(2,1)S(1)}, u32[]{:S(2)}, u32[]{:S(2)}) collective-permute-start(bf16[8,4,2,512]{3,2,1,0:T(2,128)(2,1)} %param.6), channel_id=1, source_target_pairs={{0,8},{8,0},{16,24},{24,16},{1,9},{9,1},{17,25},{25,17},{2,10},{10... | collective-permute-start | bytes 196616 | tf_op jit(solution)/shard_map/ppermute | solution.py:363
  2.0 1.2 %collective-permute-start.2 = (bf16[8,4,2,512]{3,2,1,0:T(2,128)(2,1)}, bf16[8,4,2,512]{3,2,1,0:T(2,128)(2,1)S(1)}, u32[]{:S(2)}, u32[]{:S(2)}) collective-permute-start(bf16[8,4,2,512]{3,2,1,0:T(2,128)(2,1)} %param.6), channel_id=1, source_target_pairs={{0,24},{8,16},{16,8},{24,0},{1,25},{9,17},{17,9},{25,1},{2,26},{10... | collective-permute-start | bytes 196616 | tf_op jit(solution)/shard_map/ppermute | solution.py:363
  3.3 1.2 %shard_map.66 = bf16[3,3,3,8,256]{4,3,2,1,0:T(8,128)(2,1)S(1)} custom-call(bf16[3,3,3,32,256]{4,3,2,1,0:T(8,128)(2,1)} %bitcast.30), custom_call_target="tpu_custom_call" | custom-call | flops 6000000000 | bytes 1000000 | tf_op jit(solution)/shard_map/pallas_call | solution.py:22
  4.5 3.6 %collective-permute-start.7 = (bf16[3,3,3,8,256]{4,3,2,1,0:T(8,128)(2,1)S(1)}, bf16[3,3,3,8,256]{4,3,2,1,0:T(8,128)(2,1)S(1)}, u32[]{:S(2)}, u32[]{:S(2)}) collective-permute-start(bf16[3,3,3,8,256]{4,3,2,1,0:T(8,128)(2,1)S(1)} %shard_map.66), channel_id=1, source_target_pairs={{0,6},{1,7},{2,4},{3,5},{4,2},{5,3},{6,0},{7,1},{8,14},{9,15},{10,... | collective-permute-start | bytes 331784 | tf_op jit(solution)/shard_map/ppermute | solution.py:363
  8.3 1.5 %shard_map.64.refs_0_ = bf16[4,128,128]{2,1,0:T(8,128)(2,1)S(1)} custom-call(bf16[4,2,8,512]{3,2,1,0:T(8,128)(2,1)S(1)} %bitcast.19, bf16[4,2,8,512]{3,2,1,0:T(8,128)(2,1)S(1)} %bitcast.21, bf16[4,2,8,512]{3,2,1,0:T(8,128)(2,1)S(1)} %bitcast.25, bf16[4,2,8,512]{3,2,1,0:T(8,128)(2,1)S(1)} %bitcast.23, bf16[3,3,3,512,128]{4,3,2,1,0:T(8,128)(2,1)S(1)} %copy-done.3), custom_call_target="tpu_custom_call" | custom-call | flops 2000000000 | bytes 100000 | tf_op jit(solution)/shard_map/pallas_call | solution.py:22
  9.8 2.2 %collective-permute-start.5 = (bf16[4,128,128]{2,1,0:T(8,128)(2,1)S(1)}, bf16[4,128,128]{2,1,0:T(8,128)(2,1)S(1)}, u32[]{:S(2)}, u32[]{:S(2)}) collective-permute-start(bf16[4,128,128]{2,1,0:T(8,128)(2,1)S(1)} %shard_map.64.refs_0_), channel_id=1, source_target_pairs={{0,24},{8,16},{16,8},{24,0},{1,25},{9,17},{17,9},{25,1},{2,26},{10... | collective-permute-start | bytes 393224 | tf_op jit(solution)/shard_map/ppermute | solution.py:363
  12.5 2.4 %collective-permute-start.11 = (bf16[3,3,3,8,256]{4,3,2,1,0:T(8,128)(2,1)S(1)}, bf16[3,3,3,8,256]{4,3,2,1,0:T(8,128)(2,1)S(1)}, u32[]{:S(2)}, u32[]{:S(2)}) collective-permute-start(bf16[3,3,3,8,256]{4,3,2,1,0:T(8,128)(2,1)S(1)} %shard_map.66), channel_id=1, source_target_pairs={{0,2},{1,3},{2,0},{3,1},{4,6},{5,7},{6,4},{7,5},{8,10},{9,11},{10,... | collective-permute-start | bytes 331784 | tf_op jit(solution)/shard_map/ppermute | solution.py:363
  14.9 2.1 %collective-permute-done.6 = bf16[3,3,3,8,256]{4,3,2,1,0:T(8,128)(2,1)S(1)} collective-permute-done((bf16[3,3,3,8,256]{4,3,2,1,0:T(8,128)(2,1)S(1)}, bf16[3,3,3,8,256]{4,3,2,1,0:T(8,128)(2,1)S(1)}, u32[]{:S(2)}, u32[]{:S(2)}) %collective-permute-start.6) | collective-permute-done | bytes 110624 | tf_op jit(solution)/shard_map/ppermute | solution.py:363
  17.0 1.6 %collective-permute-start.8 = (bf16[3,3,3,3,8,256]{5,4,3,2,1,0:T(8,128)(2,1)S(1)}, bf16[3,3,3,3,8,256]{5,4,3,2,1,0:T(8,128)(2,1)S(1)}, u32[]{:S(2)}, u32[]{:S(2)}) collective-permute-start(bf16[3,3,3,3,8,256]{5,4,3,2,1,0:T(8,128)(2,1)S(1)} %pad_maximum_fusion), channel_id=1, source_target_pairs={{0,1},{1,0},{2,3},{3,2},{4,5},{5,4},{6,7},{7,6},{8,9},{9,8},{10,11... | collective-permute-start | bytes 995336 | tf_op jit(solution)/shard_map/ppermute | solution.py:363
  18.6 0.3 shard_map.65.refs_5_
  18.9 0.9 %collective-permute-done.8.refs_6_ = bf16[3,3,3,3,8,256]{5,4,3,2,1,0:T(8,128)(2,1)S(1)} collective-permute-done((bf16[3,3,3,3,8,256]{5,4,3,2,1,0:T(8,128)(2,1)S(1)}, bf16[3,3,3,3,8,256]{5,4,3,2,1,0:T(8,128)(2,1)S(1)}, u32[]{:S(2)}, u32[]{:S(2)}) %collective-permute-start.8) | collective-permute-done | bytes 331808 | tf_op jit(solution)/shard_map/ppermute | solution.py:363
  19.9 0.4 %shard_map.67 = (bf16[2,128,256]{2,1,0:T(8,128)(2,1)S(1)}, bf16[2,128,256]{2,1,0:T(8,128)(2,1)S(1)}, bf16[4,128,256]{2,1,0:T(8,128)(2,1)S(1)}) custom-call(bf16[4,128,128]{2,1,0:T(8,128)(2,1)S(1)} %shard_map.64.refs_0_, bf16[4,128,128]{2,1,0:T(8,128)(2,1)S(1)} %collective-permute-done.3.refs_1_, bf16[4,128,128]{2,1,0:T(8,128)(2,1)S(1)} %collective-permute-done.4.refs_2_, ...), custom_call_target="tpu_custom_call" | custom-call | flops 134217728 | bytes 2000000 | tf_op jit(solution)/shard_map/pallas_call | solution.py:22
  20.3 0.4 %collective-permute-start.12 = (bf16[1,3,3,3,8,256]{5,4,3,2,1,0:T(8,128)(2,1)S(1)}, bf16[1,3,3,3,8,256]{5,4,3,2,1,0:T(8,128)(2,1)S(1)}, u32[]{:S(2)}, u32[]{:S(2)}) collective-permute-start(bf16[1,3,3,3,8,256]{5,4,3,2,1,0:T(8,128)(2,1)S(1)} %bitcast.27), channel_id=1, source_target_pairs={{0,1},{1,0},{2,3},{3,2},{4,5},{5,4},{6,7},{7,6},{8,9},{9,8},{10,11... | collective-permute-start | bytes 331784 | tf_op jit(solution)/shard_map/ppermute | solution.py:363
  20.7 3.1 %collective-permute-start.9 = (bf16[2,128,256]{2,1,0:T(8,128)(2,1)S(1)}, bf16[2,128,256]{2,1,0:T(8,128)(2,1)S(1)}, u32[]{:S(2)}, u32[]{:S(2)}) collective-permute-start(bf16[2,128,256]{2,1,0:T(8,128)(2,1)S(1)} %get-tuple-element.18), channel_id=1, source_target_pairs={{1,2},{3,4},{5,6},{2,1},{4,3},{6,5},{9,10},{11,12},{13,14},{10,9},... | collective-permute-start | bytes 393224 | tf_op jit(solution)/shard_map/ppermute | solution.py:440
  24.1 0.7 %shard_map.68.filters = bf16[3,3,2,256,256]{4,3,2,1,0:T(8,128)(2,1)S(1)} custom-call(bf16[8,3,3,3,8,256]{5,4,3,2,1,0:T(8,128)(2,1)S(1)} %slice_dynamic-update-slice_fusion.pieces), custom_call_target="tpu_custom_call" | custom-call | flops 1000000 | bytes 4000000 | tf_op jit(solution)/shard_map/pallas_call | solution.py:22
  24.7 2.3 %collective-permute-done.9.odd_in = bf16[2,128,256]{2,1,0:T(8,128)(2,1)S(1)} collective-permute-done((bf16[2,128,256]{2,1,0:T(8,128)(2,1)S(1)}, bf16[2,128,256]{2,1,0:T(8,128)(2,1)S(1)}, u32[]{:S(2)}, u32[]{:S(2)}) %collective-permute-start.9) | collective-permute-done | bytes 131104 | tf_op jit(solution)/shard_map/ppermute | solution.py:440
  27.0 1.3 %shard_map.69 = (bf16[120,256]{1,0:T(8,128)(2,1)S(1)}, bf16[120,256]{1,0:T(8,128)(2,1)S(1)}, bf16[120,256]{1,0:T(8,128)(2,1)S(1)}, bf16[120,256]{1,0:T(8,128)(2,1)S(1)}, bf16[4,48,256]{2,1,0:T(8,128)(2,1)S(1)}) custom-call(bf16[2,128,256]{2,1,0:T(8,128)(2,1)S(1)} %collective-permute-done.9.odd_in, bf16[2,128,256]{2,1,0:T(8,128)(2,1)S(1)} %collective-permute-done.10.even_in, ...), custom_call_target="tpu_custom_call" | custom-call | flops 905969664 | bytes 5000000 | tf_op jit(solution)/shard_map/pallas_call | solution.py:22
  28.3 1.3 %collective-permute-start.13 = (bf16[120,256]{1,0:T(8,128)(2,1)S(1)}, bf16[120,256]{1,0:T(8,128)(2,1)S(1)}, u32[]{:S(2)}, u32[]{:S(2)}) collective-permute-start(bf16[120,256]{1,0:T(8,128)(2,1)S(1)} %get-tuple-element.25), channel_id=1, source_target_pairs={{0,16},{8,24},{16,0},{24,8},{1,17},{9,25},{17,1},{25,9},{2,18},{10... | collective-permute-start | bytes 184328 | tf_op jit(solution)/shard_map/ppermute | solution.py:363
  29.6 1.2 %collective-permute-start.14 = (bf16[120,256]{1,0:T(8,128)(2,1)S(1)}, bf16[120,256]{1,0:T(8,128)(2,1)S(1)}, u32[]{:S(2)}, u32[]{:S(2)}) collective-permute-start(bf16[120,256]{1,0:T(8,128)(2,1)S(1)} %get-tuple-element.26), channel_id=1, source_target_pairs={{0,24},{8,16},{16,8},{24,0},{1,25},{9,17},{17,9},{25,1},{2,26},{10... | collective-permute-start | bytes 184328 | tf_op jit(solution)/shard_map/ppermute | solution.py:363
  30.8 0.3 collective-permute-start.15
  31.0 0.4 %shard_map.70 = (bf16[3,2,2,256,256]{4,3,2,1,0:T(8,128)(2,1)S(1)}, bf16[4,256,512]{2,1,0:T(8,128)(2,1)S(1)}) custom-call(bf16[3,3,3,128,128]{4,3,2,1,0:T(8,128)(2,1)S(1)} %copy-done, bf16[256,128]{1,0:T(8,128)(2,1)S(1)} %copy-done.2), custom_call_target="tpu_custom_call" | custom-call | flops 1000000 | bytes 4000000 | tf_op jit(solution)/shard_map/pallas_call | solution.py:22
  31.5 2.2 %collective-permute-done.14.refs_2_ = bf16[120,256]{1,0:T(8,128)(2,1)S(1)} collective-permute-done((bf16[120,256]{1,0:T(8,128)(2,1)S(1)}, bf16[120,256]{1,0:T(8,128)(2,1)S(1)}, u32[]{:S(2)}, u32[]{:S(2)}) %collective-permute-start.14) | collective-permute-done | bytes 61472 | tf_op jit(solution)/shard_map/ppermute | solution.py:363
  33.7 0.3 collective-permute-done.15.refs_3_
  34.0 1.9 %shard_map.71 = bf16[8,16,8,128]{3,2,1,0:T(8,128)(2,1)} custom-call(bf16[120,256]{1,0:T(8,128)(2,1)S(1)} %get-tuple-element.24.refs_0_, bf16[120,256]{1,0:T(8,128)(2,1)S(1)} %collective-permute-done.13.refs_1_, bf16[120,256]{1,0:T(8,128)(2,1)S(1)} %collective-permute-done.14.refs_2_, bf16[120,256]{1,0:T(8,128)(2,1)S(1)} %collective-permute-done.15.refs_3_, ...), custom_call_target="tpu_custom_call" | custom-call | flops 503316480 | bytes 3000000 | tf_op jit(solution)/shard_map/pallas_call | solution.py:22
  (37 shorter events, 0.9 us)
Async XLA Ops:
  0.0 8.1 %collective-permute-start = (bf16[8,4,2,512]{3,2,1,0:T(2,128)(2,1)}, bf16[8,4,2,512]{3,2,1,0:T(2,128)(2,1)S(1)}, u32[]{:S(2)}, u32[]{:S(2)}) collective-permute-start(bf16[8,4,2,512]{3,2,1,0:T(2,128)(2,1)} %param.6), channel_id=1, source_target_pairs={{0,8},{8,0},{16,24},{24,16},{1,9},{9,1},{17,25},{25,17},{2,10},{10... | collective-permute-start | bytes 196616 | tf_op jit(solution)/shard_map/ppermute | solution.py:363
  2.0 6.1 %collective-permute-start.2 = (bf16[8,4,2,512]{3,2,1,0:T(2,128)(2,1)}, bf16[8,4,2,512]{3,2,1,0:T(2,128)(2,1)S(1)}, u32[]{:S(2)}, u32[]{:S(2)}) collective-permute-start(bf16[8,4,2,512]{3,2,1,0:T(2,128)(2,1)} %param.6), channel_id=1, source_target_pairs={{0,24},{8,16},{16,8},{24,0},{1,25},{9,17},{17,9},{25,1},{2,26},{10... | collective-permute-start | bytes 196616 | tf_op jit(solution)/shard_map/ppermute | solution.py:363
  3.3 5.0 %collective-permute-start.1 = (bf16[8,4,2,512]{3,2,1,0:T(2,128)(2,1)}, bf16[8,4,2,512]{3,2,1,0:T(2,128)(2,1)S(1)}, u32[]{:S(2)}, u32[]{:S(2)}) collective-permute-start(bf16[8,4,2,512]{3,2,1,0:T(2,128)(2,1)} %param.6), channel_id=1, source_target_pairs={{0,16},{8,24},{16,0},{24,8},{1,17},{9,25},{17,1},{25,9},{2,18},{10... | collective-permute-start | bytes 196616 | tf_op jit(solution)/shard_map/ppermute | solution.py:363
  3.3 4.8 %copy-start.4 = (bf16[8,4,2,512]{3,2,1,0:T(2,128)(2,1)S(1)}, bf16[8,4,2,512]{3,2,1,0:T(2,128)(2,1)}, u32[]{:S(2)}) copy-start(bf16[8,4,2,512]{3,2,1,0:T(2,128)(2,1)} %param.6) | copy-start | bytes 196612
  3.3 5.0 %copy-start.3 = (bf16[3,3,3,512,128]{4,3,2,1,0:T(8,128)(2,1)S(1)}, bf16[3,3,3,512,128]{4,3,2,1,0:T(8,128)(2,1)}, u32[]{:S(2)}) copy-start(bf16[3,3,3,512,128]{4,3,2,1,0:T(8,128)(2,1)} %refs_4_.3) | copy-start | bytes 10616836
  4.5 8.0 %collective-permute-start.7 = (bf16[3,3,3,8,256]{4,3,2,1,0:T(8,128)(2,1)S(1)}, bf16[3,3,3,8,256]{4,3,2,1,0:T(8,128)(2,1)S(1)}, u32[]{:S(2)}, u32[]{:S(2)}) collective-permute-start(bf16[3,3,3,8,256]{4,3,2,1,0:T(8,128)(2,1)S(1)} %shard_map.66), channel_id=1, source_target_pairs={{0,6},{1,7},{2,4},{3,5},{4,2},{5,3},{6,0},{7,1},{8,14},{9,15},{10,... | collective-permute-start | bytes 331784 | tf_op jit(solution)/shard_map/ppermute | solution.py:363
  8.1 8.9 %collective-permute-start.6 = (bf16[3,3,3,8,256]{4,3,2,1,0:T(8,128)(2,1)S(1)}, bf16[3,3,3,8,256]{4,3,2,1,0:T(8,128)(2,1)S(1)}, u32[]{:S(2)}, u32[]{:S(2)}) collective-permute-start(bf16[3,3,3,8,256]{4,3,2,1,0:T(8,128)(2,1)S(1)} %shard_map.66), channel_id=1, source_target_pairs={{0,4},{1,5},{2,6},{3,7},{4,0},{5,1},{6,2},{7,3},{8,12},{9,13},{10,... | collective-permute-start | bytes 331784 | tf_op jit(solution)/shard_map/ppermute | solution.py:363
  8.3 10.3 %copy-start.1 = (bf16[512,256]{1,0:T(8,128)(2,1)S(1)}, bf16[512,256]{1,0:T(8,128)(2,1)}, u32[]{:S(2)}) copy-start(bf16[512,256]{1,0:T(8,128)(2,1)} %refs_4_.5) | copy-start | bytes 786436
  9.8 9.1 %collective-permute-start.5 = (bf16[4,128,128]{2,1,0:T(8,128)(2,1)S(1)}, bf16[4,128,128]{2,1,0:T(8,128)(2,1)S(1)}, u32[]{:S(2)}, u32[]{:S(2)}) collective-permute-start(bf16[4,128,128]{2,1,0:T(8,128)(2,1)S(1)} %shard_map.64.refs_0_), channel_id=1, source_target_pairs={{0,24},{8,16},{16,8},{24,0},{1,25},{9,17},{17,9},{25,1},{2,26},{10... | collective-permute-start | bytes 393224 | tf_op jit(solution)/shard_map/ppermute | solution.py:363
  12.0 6.9 %collective-permute-start.4 = (bf16[4,128,128]{2,1,0:T(8,128)(2,1)S(1)}, bf16[4,128,128]{2,1,0:T(8,128)(2,1)S(1)}, u32[]{:S(2)}, u32[]{:S(2)}) collective-permute-start(bf16[4,128,128]{2,1,0:T(8,128)(2,1)S(1)} %shard_map.64.refs_0_), channel_id=1, source_target_pairs={{0,16},{8,24},{16,0},{24,8},{1,17},{9,25},{17,1},{25,9},{2,18},{10... | collective-permute-start | bytes 393224 | tf_op jit(solution)/shard_map/ppermute | solution.py:363
  12.3 6.7 %collective-permute-start.3 = (bf16[4,128,128]{2,1,0:T(8,128)(2,1)S(1)}, bf16[4,128,128]{2,1,0:T(8,128)(2,1)S(1)}, u32[]{:S(2)}, u32[]{:S(2)}) collective-permute-start(bf16[4,128,128]{2,1,0:T(8,128)(2,1)S(1)} %shard_map.64.refs_0_), channel_id=1, source_target_pairs={{0,8},{8,0},{16,24},{24,16},{1,9},{9,1},{17,25},{25,17},{2,10},{10... | collective-permute-start | bytes 393224 | tf_op jit(solution)/shard_map/ppermute | solution.py:363
  12.5 7.8 %collective-permute-start.11 = (bf16[3,3,3,8,256]{4,3,2,1,0:T(8,128)(2,1)S(1)}, bf16[3,3,3,8,256]{4,3,2,1,0:T(8,128)(2,1)S(1)}, u32[]{:S(2)}, u32[]{:S(2)}) collective-permute-start(bf16[3,3,3,8,256]{4,3,2,1,0:T(8,128)(2,1)S(1)} %shard_map.66), channel_id=1, source_target_pairs={{0,2},{1,3},{2,0},{3,1},{4,6},{5,7},{6,4},{7,5},{8,10},{9,11},{10,... | collective-permute-start | bytes 331784 | tf_op jit(solution)/shard_map/ppermute | solution.py:363
  17.0 2.8 %collective-permute-start.8 = (bf16[3,3,3,3,8,256]{5,4,3,2,1,0:T(8,128)(2,1)S(1)}, bf16[3,3,3,3,8,256]{5,4,3,2,1,0:T(8,128)(2,1)S(1)}, u32[]{:S(2)}, u32[]{:S(2)}) collective-permute-start(bf16[3,3,3,3,8,256]{5,4,3,2,1,0:T(8,128)(2,1)S(1)} %pad_maximum_fusion), channel_id=1, source_target_pairs={{0,1},{1,0},{2,3},{3,2},{4,5},{5,4},{6,7},{7,6},{8,9},{9,8},{10,11... | collective-permute-start | bytes 995336 | tf_op jit(solution)/shard_map/ppermute | solution.py:363
  20.3 3.7 %collective-permute-start.12 = (bf16[1,3,3,3,8,256]{5,4,3,2,1,0:T(8,128)(2,1)S(1)}, bf16[1,3,3,3,8,256]{5,4,3,2,1,0:T(8,128)(2,1)S(1)}, u32[]{:S(2)}, u32[]{:S(2)}) collective-permute-start(bf16[1,3,3,3,8,256]{5,4,3,2,1,0:T(8,128)(2,1)S(1)} %bitcast.27), channel_id=1, source_target_pairs={{0,1},{1,0},{2,3},{3,2},{4,5},{5,4},{6,7},{7,6},{8,9},{9,8},{10,11... | collective-permute-start | bytes 331784 | tf_op jit(solution)/shard_map/ppermute | solution.py:363
  20.7 6.3 %collective-permute-start.9 = (bf16[2,128,256]{2,1,0:T(8,128)(2,1)S(1)}, bf16[2,128,256]{2,1,0:T(8,128)(2,1)S(1)}, u32[]{:S(2)}, u32[]{:S(2)}) collective-permute-start(bf16[2,128,256]{2,1,0:T(8,128)(2,1)S(1)} %get-tuple-element.18), channel_id=1, source_target_pairs={{1,2},{3,4},{5,6},{2,1},{4,3},{6,5},{9,10},{11,12},{13,14},{10,9},... | collective-permute-start | bytes 393224 | tf_op jit(solution)/shard_map/ppermute | solution.py:440
  23.8 3.2 %collective-permute-start.10 = (bf16[2,128,256]{2,1,0:T(8,128)(2,1)S(1)}, bf16[2,128,256]{2,1,0:T(8,128)(2,1)S(1)}, u32[]{:S(2)}, u32[]{:S(2)}) collective-permute-start(bf16[2,128,256]{2,1,0:T(8,128)(2,1)S(1)} %get-tuple-element.19), channel_id=1, source_target_pairs={{0,1},{1,0},{2,3},{3,2},{4,5},{5,4},{6,7},{7,6},{8,9},{9,8},{10,11... | collective-permute-start | bytes 393224 | tf_op jit(solution)/shard_map/ppermute | solution.py:363
  24.7 6.3 %copy-start = (bf16[3,3,3,128,128]{4,3,2,1,0:T(8,128)(2,1)S(1)}, bf16[3,3,3,128,128]{4,3,2,1,0:T(8,128)(2,1)}, u32[]{:S(2)}) copy-start(bf16[3,3,3,128,128]{4,3,2,1,0:T(8,128)(2,1)} %filters.1) | copy-start | bytes 2654212
  24.7 6.3 %copy-start.2 = (bf16[256,128]{1,0:T(8,128)(2,1)S(1)}, bf16[256,128]{1,0:T(8,128)(2,1)}, u32[]{:S(2)}) copy-start(bf16[256,128]{1,0:T(8,128)(2,1)} %refs_6_.1) | copy-start | bytes 196612
  28.3 3.1 %collective-permute-start.13 = (bf16[120,256]{1,0:T(8,128)(2,1)S(1)}, bf16[120,256]{1,0:T(8,128)(2,1)S(1)}, u32[]{:S(2)}, u32[]{:S(2)}) collective-permute-start(bf16[120,256]{1,0:T(8,128)(2,1)S(1)} %get-tuple-element.25), channel_id=1, source_target_pairs={{0,16},{8,24},{16,0},{24,8},{1,17},{9,25},{17,1},{25,9},{2,18},{10... | collective-permute-start | bytes 184328 | tf_op jit(solution)/shard_map/ppermute | solution.py:363
  29.6 4.0 %collective-permute-start.14 = (bf16[120,256]{1,0:T(8,128)(2,1)S(1)}, bf16[120,256]{1,0:T(8,128)(2,1)S(1)}, u32[]{:S(2)}, u32[]{:S(2)}) collective-permute-start(bf16[120,256]{1,0:T(8,128)(2,1)S(1)} %get-tuple-element.26), channel_id=1, source_target_pairs={{0,24},{8,16},{16,8},{24,0},{1,25},{9,17},{17,9},{25,1},{2,26},{10... | collective-permute-start | bytes 184328 | tf_op jit(solution)/shard_map/ppermute | solution.py:363
  30.8 3.2 %collective-permute-start.15 = (bf16[120,256]{1,0:T(8,128)(2,1)S(1)}, bf16[120,256]{1,0:T(8,128)(2,1)S(1)}, u32[]{:S(2)}, u32[]{:S(2)}) collective-permute-start(bf16[120,256]{1,0:T(8,128)(2,1)S(1)} %get-tuple-element.27), channel_id=1, source_target_pairs={{0,8},{8,0},{16,24},{24,16},{1,9},{9,1},{17,25},{25,17},{2,10},{10... | collective-permute-start | bytes 184328 | tf_op jit(solution)/shard_map/ppermute | solution.py:363
